TPU v7x, 128 devices: a whole 4x4x4 slice. The times are simulated.
128 devices in a mesh: dp: 16 (over z_lo, y, core), vocab: 8 (over z_hi, x).
Axes of the slice: x: 4, y: 4, z: 4 (z_hi: 2, z_lo: 2; z = z_hi * 2 + z_lo), core: 2. Of those that a mesh axis runs over, the one named last changes fastest.
Arguments:
- hidden: bfloat16 [768, 6144], P('dp')
- targets: int32 [768], replicated, may hold values from 0 to 50431
- hidden_probe: bfloat16 [768, 6144], replicated, may hold values from -1 to 1, as said below
- table: bfloat16 [50432, 6144], P(('dp', 'vocab')), as said below
- table_probe: bfloat16 [50432, 6144], P(('dp', 'vocab')), may hold values from -1 to 1, as said below
Outputs:
- hidden_tangent: bfloat16 [768, 6144], P('dp', 'vocab')
- curvature: float32 [50432], P(('dp', 'vocab'))
Inputs may be any that keep to these rules, and one draw needn't show every extreme that they name: `hidden_probe`: entries are +1 or -1. `table`: rows of the output head. `table_probe`: entries are +1 or -1.
All inputs are finite; a program needn't handle non-finite values.
Results may differ from a plain program's by a relative error of at most 0.004.
Values may be sent and summed in bfloat16 or wider, within the bound.
No kernel may reach another device: no remote copies, remote signals or barrier semaphores. Data moves between devices by JAX's collectives and lax.ppermute only.
A program may use at most 128 MiB of HBM per device.

v0:
```python
import math

import jax
import jax.numpy as jnp
from jax import lax
from jax.sharding import PartitionSpec as P

CONTRACT = (((1,), (1,)), ((), ()))


def row_products(matrix, weights):
    return lax.dot_general(matrix, weights, CONTRACT, preferred_element_type=jnp.float32)


def body(hidden, targets, hidden_probe, table, table_probe):
    width = table.shape[1]
    vocab_rows = table.shape[0]
    probe_scale = 1.0 / math.sqrt(width)
    token_count = targets.shape[0]
    vocab_total = vocab_rows * lax.axis_size("dp") * lax.axis_size("vocab")
    vocab_start = lax.axis_index(("dp", "vocab")) * vocab_rows
    block_rows = lax.all_gather(hidden, "dp", axis=0, tiled=True)
    block_logits = row_products(block_rows, table)
    block_hidden = row_products(block_rows, table_probe) * probe_scale
    block_tangent = row_products(hidden_probe, table) + block_hidden
    block_probe = row_products(hidden_probe, table_probe) * probe_scale
    stacked = jnp.stack([block_logits, block_tangent, block_hidden, block_probe], axis=1)
    logits = stacked[:, 0]
    tangent = stacked[:, 1]
    hidden_side = stacked[:, 2]
    probe_side = stacked[:, 3]
    highest = lax.pmax(jnp.max(logits, axis=1), ("dp", "vocab"))
    weights_exp = jnp.exp(logits - highest[:, None])
    normal_sum, weighted_sum = lax.psum(
        (jnp.sum(weights_exp, axis=1), jnp.sum(weights_exp * tangent, axis=1)), ("dp", "vocab")
    )
    probability = weights_exp / normal_sum[:, None]
    mean_tangent = weighted_sum / normal_sum
    curve_term = probability * (tangent - mean_tangent[:, None])
    columns = vocab_start + lax.broadcasted_iota(jnp.int32, (1, vocab_rows), 1)
    onehot = (targets[:, None] == columns).astype(jnp.float32)
    gradient = probability - onehot
    curvature = jnp.sum(curve_term * hidden_side + gradient * probe_side, axis=0) * (
        vocab_total / token_count
    )
    curve_half = curve_term.astype(jnp.bfloat16)
    gradient_half = gradient.astype(jnp.bfloat16)
    root_width = math.sqrt(width)
    first_part = jnp.dot(curve_half, table, preferred_element_type=jnp.float32)
    rows_summed = lax.psum_scatter(
        root_width * first_part
        + jnp.dot(gradient_half, table_probe, preferred_element_type=jnp.float32),
        "dp",
        scatter_dimension=0,
        tiled=True,
    )
    result = lax.psum_scatter(rows_summed, "vocab", scatter_dimension=1, tiled=True)
    return (result.astype(jnp.bfloat16), curvature)


def solution(mesh):
    placed = (P("dp", None), P(), P(), P(("dp", "vocab"), None), P(("dp", "vocab"), None))
    return jax.shard_map(
        body,
        mesh=mesh,
        in_specs=placed,
        out_specs=(P("dp", "vocab"), P(("dp", "vocab"))),
        check_vma=False,
    )
```

profile of v0, /device:TPU:0, one launch (start us, length us, event | category | flops | bytes accessed | tf_op | source)
XLA Modules:
  0.0 447.7 jit_solution(11376288733225869424)
XLA Ops:
  7.2 0.0 all-gather.2.cloned.1.call-start
  7.2 0.7 all-gather.2.cloned.1.call-update
  7.9 0.0 reduce-scatter.3.cloned.1.call-start
  8.0 61.3 %all-gather.2.cloned.1.call-done = bf16[768,6144]{1,0:T(8,128)(2,1)} async-done(((bf16[48,6144]{1,0:T(8,128)(2,1)}), bf16[768,6144]{1,0:T(8,128)(2,1)}) %all-gather.2.cloned.1.call-update) | async-done | bytes 9437200 | tf_op jit(solution)/shard_map/all_gather | solution.py:22
  69.3 10.9 %fusion.13 = (f32[768]{0:T(1024)S(1)}, f32[768,394]{0,1:T(8,128)S(1)}) fusion(bf16[768,6144]{1,0:T(8,128)(2,1)} %all-gather.2.cloned.1.call-done, bf16[394,6144]{1,0:T(8,128)(2,1)} %param.8), kind=kOutput, calls=%fused_computation.20 | convolution fusion | flops 3718552320 | bytes 15492096 | tf_op jit(solution)/shard_map/dot_general | solution.py:12
  80.2 66.2 %pmax.7 = f32[768]{0:T(1024)S(1)} all-reduce(f32[768]{0:T(1024)S(1)} %get-tuple-element.6), channel_id=1, replica_groups=mesh['dp'=16,'vocab'=8] {'dp','vocab'}, use_global_device_ids=true, to_apply=%region_1.0 | all-reduce | flops 768 | bytes 6144 | tf_op jit(solution)/shard_map/pmax | solution.py:32
  146.3 10.8 %convolution_multiply_fusion.1 = f32[768,394]{0,1:T(8,128)S(1)} fusion(bf16[768,6144]{1,0:T(8,128)(2,1)} %all-gather.2.cloned.1.call-done, bf16[394,6144]{1,0:T(8,128)(2,1)} %param.9), kind=kOutput, calls=%fused_computation.2 | convolution fusion | flops 3718553088 | bytes 15489024 | tf_op jit(solution)/shard_map/dot_general | solution.py:12
  157.2 0.0 copy-start.1
  157.2 0.0 copy-start
  157.2 11.3 %multiply_reduce_fusion = (f32[768]{0:T(1024)S(1)}, f32[768]{0:T(1024)S(1)}, f32[768,394]{0,1:T(8,128)S(1)}) fusion(f32[768,394]{0,1:T(8,128)S(1)} %get-tuple-element.7, f32[768]{0:T(1024)S(1)} %pmax.7, f32[768,394]{0,1:T(8,128)S(1)} %convolution_multiply_fusion.1, bf16[768,6144]{1,0:T(8,128)(2,1)} %param.7, bf16[394,6144]{1,0:T(8,128)(2,1)} %param.8), kind=kOutput, calls=%fused_computation.9 | convolution fusion | flops 3719761920 | bytes 17918976 | tf_op jit(solution)/shard_map/dot_general | solution.py:12
  168.6 0.0 copy-done.1
  168.6 63.0 %all-reduce = (f32[768]{0:T(1024)S(1)}, f32[768]{0:T(1024)S(1)}) all-reduce(f32[768]{0:T(1024)S(1)} %get-tuple-element.3, f32[768]{0:T(1024)S(1)} %get-tuple-element.2), channel_id=1, replica_groups=mesh['dp'=16,'vocab'=8] {'dp','vocab'}, use_global_device_ids=true, to_apply=%region_3.0 | all-reduce | flops 1536 | bytes 12288 | tf_op jit(solution)/shard_map/psum | solution.py:34
  231.6 0.0 copy-done
  231.6 11.6 %fusion.6 = f32[768,6144]{1,0:T(8,128)} fusion(bf16[394,6144]{1,0:T(8,128)(2,1)} %param.9, s32[768]{0:T(1024)S(1)} %copy-done, s32[394]{0:T(512)S(1)} %iota_add_fusion, f32[768,394]{0,1:T(8,128)S(1)} %get-tuple-element.7, f32[768]{0:T(1024)S(1)} %get-tuple-element.4, f32[768]{0:T(1024)S(1)} %pmax.7), kind=kOutput, calls=%fused_computation.14 | convolution fusion | flops 3720066048 | bytes 24937000 | tf_op jit(solution)/shard_map/dot_general | solution.py:52
  243.2 14.4 %multiply_add_fusion = f32[768,6144]{1,0:T(8,128)} fusion(f32[768,6144]{1,0:T(8,128)} %fusion.6, bf16[394,6144]{1,0:T(8,128)(2,1)} %param.8, f32[768,394]{0,1:T(8,128)S(1)} %get-tuple-element.8, f32[768]{0:T(1024)S(1)} %div.13, f32[768,394]{0,1:T(8,128)S(1)} %get-tuple-element.7, f32[768]{0:T(1024)S(1)} %get-tuple-element.4, f32[768]{0:T(1024)S(1)} %pmax.7), kind=kOutput, calls=%fused_computation | convolution fusion | flops 3729200640 | bytes 45020160 | tf_op jit(solution)/shard_map/dot_general | solution.py:49
  257.6 0.0 reduce-scatter.3.cloned.1.call-update
  257.6 0.0 reduce-scatter.5.cloned.1.call-start
  257.7 106.3 %reduce-scatter.3.cloned.1.call-done = f32[48,6144]{1,0:T(8,128)} async-done(((f32[768,6144]{1,0:T(8,128)}), f32[48,6144]{1,0:T(8,128)}) %reduce-scatter.3.cloned.1.call-update) | async-done | bytes 1179664 | tf_op jit(solution)/shard_map/reduce_scatter | solution.py:50
  364.0 0.0 reduce-scatter.5.cloned.1.call-update
  364.0 10.0 %fusion.2 = f32[394]{0:T(512)S(1)} fusion(bf16[768,6144]{1,0:T(8,128)(2,1)} %param.7, bf16[394,6144]{1,0:T(8,128)(2,1)} %param.9, f32[768,394]{0,1:T(8,128)} %copy-done.1, s32[768]{0:T(1024)S(1)} %copy-done, f32[768,394]{0,1:T(8,128)S(1)} %get-tuple-element.8, f32[768]{0:T(1024)S(1)} %div.13, s32[394]{0:T(512)S(1)} %iota_add_fusion, ...), kind=kOutput, calls=%fused_computation.6 | convolution fusion | flops 3721881088 | bytes 17925200 | tf_op jit(solution)/shard_map/dot_general | solution.py:12
  374.0 0.6 broadcast_multiply_fusion
  374.6 65.0 %reduce-scatter.5.cloned.1.call-done = f32[48,768]{1,0:T(8,128)} async-done(((f32[48,6144]{1,0:T(8,128)}), f32[48,768]{1,0:T(8,128)}) %reduce-scatter.5.cloned.1.call-update) | async-done | bytes 147472 | tf_op jit(solution)/shard_map/reduce_scatter | solution.py:57
  439.6 1.6 convert_element_type.15
  (2 shorter events, 0.0 us)
Async XLA Ops:
  7.2 62.1 %all-gather.2.cloned.1.call-start = ((), (), s32[]{:S(2)}) async-start(), calls=%async_computation.2 | async-start | bytes 10027008 | tf_op jit(solution)/shard_map/all_gather | solution.py:22
  7.9 356.1 %reduce-scatter.3.cloned.1.call-start = ((), (), s32[]{:S(2)}) async-start(), calls=%async_computation.3 | async-start | bytes 20054016 | tf_op jit(solution)/shard_map/reduce_scatter | solution.py:50
  157.2 11.4 %copy-start.1 = (f32[768,394]{0,1:T(8,128)}, f32[768,394]{0,1:T(8,128)S(1)}, u32[]{:S(2)}) copy-start(f32[768,394]{0,1:T(8,128)S(1)} %convolution_multiply_fusion.1) | copy-start | bytes 3631108
  157.2 74.4 %copy-start = (s32[768]{0:T(1024)S(1)}, s32[768]{0:T(1024)}, u32[]{:S(2)}) copy-start(s32[768]{0:T(1024)} %param.6) | copy-start | bytes 9220
  257.6 182.0 %reduce-scatter.5.cloned.1.call-start = ((), (), s32[]{:S(2)}) async-start(), calls=%async_computation.4 | async-start | bytes 1327104 | tf_op jit(solution)/shard_map/reduce_scatter | solution.py:57
Sparse Core Ops, SparseCore 0:
  9.7 59.5 all-gather.1
  257.8 106.1 reduce-scatter.2
  367.7 71.8 reduce-scatter.4
where the time goes:
time: 448 us
  waiting for transfers between devices  233 us (52%)
  blocking collectives  129 us (29%)
  matrix products  69.1 us (15%)
  between operations  13.8 us (3%)
    reduce_scatter x1, waiting for transfers between devices, body(): lax.psum_scatter(root_width * first_part + jnp.dot(gradient_half, table_p...  106 us
    pmax x1, blocking collectives, body(): highest = lax.pmax(jnp.max(logits, axis=1), ('dp', 'vocab'))  66.2 us
    reduce_scatter x1, waiting for transfers between devices, body(): lax.psum_scatter(rows_summed, 'vocab', scatter_dimension=1, tiled=True)  65 us
    psum x1, blocking collectives, body(): lax.psum((jnp.sum(weights_exp, axis=1), jnp.sum(weights_exp * tangent, ax...  63 us
    all_gather x1, waiting for transfers between devices, body(): block_rows = lax.all_gather(hidden, 'dp', axis=0, tiled=True)  61.3 us
    dot_general x4, matrix products, row_products(): lax.dot_general(matrix, weights, CONTRACT, preferred_element_type=jnp.flo...  43 us
    dot_general x1, matrix products, body(): first_part = jnp.dot(curve_half, table, preferred_element_type=jnp.float32)  14.4 us
    dot_general x1, matrix products, body(): jnp.dot(gradient_half, table_probe, preferred_element_type=jnp.float32)  11.6 us
  transfers between devices with their start and end apart: 3, of which 3 were waited for; matrix products, arithmetic and copies ran while one was open for 2% of the time, Pallas kernels for 0%

commit v1 on v0

v1 whole, which is shorter than its diff:
```python
import math

import jax
import jax.numpy as jnp
from jax import lax
from jax.experimental import pallas as pl
from jax.experimental.pallas import tpu as pltpu
from jax.sharding import PartitionSpec as P

AXES = ("dp", "vocab")
F32 = jnp.float32
BF16 = jnp.bfloat16
FIRST = 3072
BLOCK = 1024
ROWS = 48
MIB = 1 << 20
NT = (((1,), (1,)), ((), ()))


def decode(d):
    return (d >> 6) & 1, (d >> 4) & 3, (d >> 3) & 1, (d >> 2) & 1, d & 3


def encode(zl, y, c, zh, x):
    return (((zl * 4 + y) * 2 + c) * 2 + zh) * 4 + x


def pairs(axes, kind):
    out = []
    for d in range(128):
        zl, y, c, zh, x = decode(d)
        m = 1 if c == kind else 3
        for axis in axes:
            if axis == "x":
                x ^= m
            elif axis == "y":
                y ^= m
            elif axis == "z":
                z = (2 * zh + zl) ^ m
                zh, zl = z >> 1, z & 1
            else:
                c ^= 1
        out.append((d, encode(zl, y, c, zh, x)))
    return out


def swap(a, axis, kind=0):
    return lax.ppermute(a, AXES, pairs(axis, kind))


def pair_of(c, q):
    return jnp.where(c == 0, (q ^ (q >> 1)) & 1, q >> 1)


def bit_of(c, q):
    return jnp.where(c == 0, q >> 1, q & 1)


def member(c, pair, bit):
    return jnp.where(c == 0, pair * (1 + bit) + (1 - pair) * 3 * bit, 2 * pair + bit)


def slot_of(c, me, q):
    return 2 * (pair_of(c, me) ^ pair_of(c, q)) + bit_of(c, q)


def groups_of_eight():
    found = {}
    for d in range(128):
        zl, y, c, zh, x = decode(d)
        at = [2 * zh + zl, y, x]
        pair = [(q ^ (q >> 1)) & 1 if c == 0 else q >> 1 for q in at]
        bit = [q >> 1 if c == 0 else q & 1 for q in at]
        found.setdefault((c, *pair), {})[tuple(bit)] = d
    return [[g[b] for b in sorted(g)] for g in found.values()]


def groups_of_core():
    return [[d for d in range(128) if decode(d)[2] == c] for c in range(2)]


def row_place(me, slot):
    zl, y, c, _, _ = decode(me)
    zs, ys = slot // 4, slot % 4
    return (zl ^ zs) * 4 + (y ^ jnp.where(c == 0, (0, 3, 1, 2)[ys], (0, 1, 3, 2)[ys]))


def owner(me, slot):
    return row_place(me, slot) * 2 + ((me >> 3) & 1)


def tie(array, *after):
    def kernel(*refs):
        del refs

    return pl.pallas_call(
        kernel,
        in_specs=[pl.BlockSpec(memory_space=pl.ANY)] * (1 + len(after)),
        out_specs=pl.BlockSpec(memory_space=pl.ANY),
        out_shape=jax.ShapeDtypeStruct(array.shape, array.dtype),
        input_output_aliases={0: 0},
    )(array, *after)


def doubled(held, axis, kind=0):
    return jnp.concatenate([held, swap(held, axis, kind)], axis=0 if axis == "z" else 1)


def products(me, rows, tables, start, before=(), tangents=(), scale=1.0, after=()):
    picked = rows.ndim == 3
    m, k = 8 * ROWS, rows.shape[-1]
    n = tables[0].shape[0]
    count = len(tables)
    steps = k // BLOCK
    first = start // BLOCK
    row_specs = (
        [pl.BlockSpec((1, ROWS, BLOCK), lambda s, me, i=i: (owner(me[0], i), 0, s)) for i in range(8)]
        if picked
        else [pl.BlockSpec((m, BLOCK), lambda s, me: (0, s))]
    )

    def kernel(me_ref, *refs):
        refs = list(refs)

        def take(length):
            taken = refs[:length]
            del refs[:length]
            return taken

        row_refs = take(len(row_specs))
        table_refs = take(count)
        prior_refs = take(len(before))
        extra_refs = take(len(tangents))
        take(len(after))
        outs = take(count)
        step = pl.program_id(0)
        if picked:
            block = jnp.concatenate([r[0] for r in row_refs], axis=0)
        else:
            block = row_refs[0][...]

        @pl.when(step == 0)
        def _():
            for i in range(count):
                outs[i][...] = prior_refs[i][...] if before else jnp.zeros((m, n), F32)

        for i in range(count):
            outs[i][...] += lax.dot_general(block, table_refs[i][...], NT, preferred_element_type=F32)

        if tangents:
            stats_ref, packed_ref = take(2)

            @pl.when(step == steps - 1)
            def _():
                lane = lax.broadcasted_iota(jnp.int32, (ROWS, 128), 1)
                for i in range(8):
                    at = slice(i * ROWS, (i + 1) * ROWS)
                    l0, l1 = outs[0][at, :], outs[1][at, :]
                    t0 = extra_refs[0][at, :] + outs[2][at, :] * scale
                    t1 = extra_refs[1][at, :] + outs[3][at, :] * scale
                    top = jnp.maximum(
                        jnp.max(l0, axis=1, keepdims=True), jnp.max(l1, axis=1, keepdims=True)
                    )
                    e0 = jnp.exp(l0 - top)
                    e1 = jnp.exp(l1 - top)
                    total = jnp.sum(e0, axis=1, keepdims=True) + jnp.sum(e1, axis=1, keepdims=True)
                    weighted = jnp.sum(e0 * t0, axis=1, keepdims=True) + jnp.sum(
                        e1 * t1, axis=1, keepdims=True
                    )
                    place = pl.multiple_of(row_place(me_ref[0], i) * ROWS, ROWS)
                    packed_ref[pl.ds(place, ROWS), :] = jnp.where(
                        lane == 0, top, jnp.where(lane == 1, total, weighted)
                    )
                stats_ref[...] = packed_ref[...].T[0:3, :]

    whole = pl.BlockSpec((m, n), lambda s, me: (0, 0))
    out_shape = [jax.ShapeDtypeStruct((m, n), F32)] * count
    out_specs = [whole] * count
    scratch = []
    if tangents:
        out_shape.append(jax.ShapeDtypeStruct((3, m), F32))
        out_specs.append(pl.BlockSpec((3, m), lambda s, me: (0, 0)))
        scratch.append(pltpu.VMEM((m, 128), F32))
    inputs = [me, *([rows] * len(row_specs)), *tables, *before, *tangents, *after]
    return pl.pallas_call(
        kernel,
        grid_spec=pltpu.PrefetchScalarGridSpec(
            num_scalar_prefetch=1,
            grid=(steps,),
            in_specs=row_specs
            + [pl.BlockSpec((n, BLOCK), lambda s, me: (0, s + first))] * count
            + [whole] * (len(before) + len(tangents))
            + [pl.BlockSpec(memory_space=pl.ANY)] * len(after),
            out_specs=out_specs,
            scratch_shapes=scratch,
        ),
        out_shape=out_shape,
        compiler_params=pltpu.CompilerParams(vmem_limit_bytes=40 * MIB),
        cost_estimate=pl.CostEstimate(
            flops=MIB, bytes_accessed=MIB, transcendentals=0
        ),
    )(*inputs)


def coefficients(me, logits, sides, tangents, probes, stats, targets, scale):
    m, n = logits[0].shape

    def kernel(me_ref, *refs):
        l_refs, h_refs, t_refs, p_refs = refs[0:2], refs[2:4], refs[4:6], refs[6:8]
        stats_ref, targets_ref = refs[8:10]
        c_refs, g_refs, curve_ref, column_ref = refs[10:12], refs[12:14], refs[14], refs[15]
        here = me_ref[0]
        tops = stats_ref[:, 0, :]
        top = jnp.max(tops, axis=0, keepdims=True)
        factor = jnp.exp(tops - top)
        total = jnp.sum(stats_ref[:, 1, :] * factor, axis=0, keepdims=True)
        mean = jnp.sum(stats_ref[:, 2, :] * factor, axis=0, keepdims=True) / total
        inverse = 1.0 / total
        line = lax.broadcasted_iota(jnp.int32, (128, m), 0)
        column_ref[...] = jnp.where(line == 0, top, jnp.where(line == 1, inverse, mean)).T
        for i in range(2):
            vocab_start = (here ^ (8 * i)) * n
            curve_sum = jnp.zeros((1, n), F32)
            for j in range(8):
                at = slice(j * ROWS, (j + 1) * ROWS)
                place = row_place(here, j)
                values = column_ref[pl.ds(pl.multiple_of(place * ROWS, ROWS), ROWS), :]
                mine = pl.multiple_of(owner(here, j) * ROWS, ROWS)
                wanted = targets_ref[pl.ds(mine, ROWS), :]
                side = h_refs[i][at, :] * scale
                tangent = t_refs[i][at, :] + side
                probability = jnp.exp(l_refs[i][at, :] - values[:, 0:1]) * values[:, 1:2]
                curve = probability * (tangent - values[:, 2:3])
                column = lax.broadcasted_iota(jnp.int32, (ROWS, n), 1) + vocab_start
                gradient = probability - jnp.where(wanted == column, 1.0, 0.0)
                c_refs[i][at, :] = curve.astype(BF16)
                g_refs[i][at, :] = gradient.astype(BF16)
                curve_sum += jnp.sum(
                    curve * side + gradient * (p_refs[i][at, :] * scale), axis=0, keepdims=True
                )
            curve_ref[i : i + 1, :] = curve_sum

    vmem = pl.BlockSpec(memory_space=pltpu.VMEM)
    return pl.pallas_call(
        kernel,
        in_specs=[pl.BlockSpec(memory_space=pltpu.SMEM)] + [vmem] * 10,
        out_specs=[vmem] * 5,
        out_shape=[jax.ShapeDtypeStruct((m, n), BF16)] * 4 + [jax.ShapeDtypeStruct((2, n), F32)],
        scratch_shapes=[pltpu.VMEM((m, 128), F32)],
        compiler_params=pltpu.CompilerParams(vmem_limit_bytes=40 * MIB),
    )(me, *logits, *sides, *tangents, *probes, stats, targets)


def back(me, curves, gradients, tables, probes, root):
    m, n = curves[0].shape
    width = 768
    part = width // 3
    kept_type = F32

    def kernel(me_ref, c0, c1, g0, g1, t0, t1, p0, p1, *outs):
        step = pl.program_id(0)
        zl, y, c, zh, _ = decode(me_ref[0])
        total = jnp.dot(c0[...], t0[...], preferred_element_type=F32)
        total += jnp.dot(c1[...], t1[...], preferred_element_type=F32)
        total *= root
        total += jnp.dot(g0[...], p0[...], preferred_element_type=F32)
        total += jnp.dot(g1[...], p1[...], preferred_element_type=F32)
        def places(slot):
            place = row_place(me_ref[0], slot)
            zs = slot_of(c, 2 * zh + zl, 2 * (zh ^ (step & 1)) + (place >> 2))
            return zs, slot_of(c, y, place & 3), slice(slot * ROWS, (slot + 1) * ROWS)

        for slot in range(8):
            zs, ys, at = places(slot)
            if slot % 4 < 2:
                outs[3][zs, ys, 0] = total[at, part : 2 * part]
            else:
                outs[2][zs, ys - 2, 0] = total[at, part : 2 * part].astype(BF16)

        @pl.when(step < 4)
        def _():
            for slot in range(8):
                zs, ys, at = places(slot)
                outs[0][zs, ys, 0] = total[at, :part].astype(BF16)

        @pl.when(step >= 4)
        def _():
            for slot in range(8):
                zs, ys, at = places(slot)
                outs[1][zs, ys, 0] = total[at, :part]

        for half_rows in range(2):
            z_slot = places(4 * half_rows)[0]

            @pl.when(z_slot >= 2)
            def _():
                for slot in range(4 * half_rows, 4 * half_rows + 4):
                    zs, ys, at = places(slot)
                    outs[4][zs - 2, ys, 0] = total[at, 2 * part :].astype(BF16)

            @pl.when(z_slot < 2)
            def _():
                for slot in range(4 * half_rows, 4 * half_rows + 4):
                    zs, ys, at = places(slot)
                    outs[5][zs, ys, 0] = total[at, 2 * part :]

    def columns(s, me):
        _, _, c, zh, x = decode(me[0])
        slot = ((s >> 1) + 2) & 3
        return (0, (zh ^ (s & 1)) * 4 + member(c, pair_of(c, x) ^ (slot >> 1), slot & 1))

    left = pl.BlockSpec((m, n), lambda s, me: (0, 0))
    right = pl.BlockSpec((n, width), columns)
    shapes, specs = [], []
    for axis in range(3):
        half = [[4, 4, 2], [4, 2, 4], [2, 4, 4]][axis]
        for kept in range(2):
            shapes.append(jax.ShapeDtypeStruct((*half, ROWS, part), kept_type if kept else BF16))

            def out_block(s, me, axis=axis, kept=kept):
                turn = s >> 1
                if axis > 0:
                    x_slot = (turn + 2) & 3
                elif kept:
                    x_slot = jnp.maximum(turn - 2, 0)
                else:
                    x_slot = jnp.minimum(turn, 1)
                return (0, 0, x_slot, 0, 0)

            specs.append(pl.BlockSpec((half[0], half[1], 1, ROWS, part), out_block))
    return pl.pallas_call(
        kernel,
        grid_spec=pltpu.PrefetchScalarGridSpec(
            num_scalar_prefetch=1,
            grid=(8,),
            in_specs=[left] * 4 + [right] * 4,
            out_specs=specs,
        ),
        out_shape=shapes,
        compiler_params=pltpu.CompilerParams(vmem_limit_bytes=40 * MIB),
        cost_estimate=pl.CostEstimate(
            flops=MIB, bytes_accessed=MIB, transcendentals=0
        ),
    )(me, *curves, *gradients, *tables, *probes)


def body(hidden, targets, hidden_probe, table, table_probe):
    vocab_rows, width = table.shape
    token_count = targets.shape[0]
    vocab_total = vocab_rows * 128
    scale = 1.0 / math.sqrt(width)
    root = math.sqrt(width)
    me = lax.axis_index(AXES).astype(jnp.int32).reshape(1)

    first = hidden[:, :FIRST].reshape(1, 1, ROWS, FIRST)
    second = hidden[:, FIRST:].reshape(1, 1, ROWS, width - FIRST)
    probe_rows = hidden_probe.reshape(token_count // ROWS, ROWS, width)
    first = doubled(first, "y", 1)
    second = doubled(second, "z")
    table_other = swap(table, "c")
    probe_other = swap(table_probe, "c")
    t0, p0 = products(me, probe_rows, (table, table_probe), 0, after=(first,))
    first = doubled(first, "y", 0)
    second = doubled(tie(second, first, t0), "y", 1)
    (t1,) = products(me, probe_rows, (table_other,), 0, after=(first,))
    first = doubled(first, "z").reshape(8 * ROWS, FIRST)
    second = doubled(tie(second, t1), "y", 0).reshape(8 * ROWS, width - FIRST)
    (p1,) = products(me, probe_rows, (probe_other,), 0)
    all_tables = (table, table_other, table_probe, probe_other)
    early = products(me, first, all_tables, 0)
    l0, l1, h0, h1, stats = products(
        me, second, all_tables, FIRST, before=early, tangents=(t0, t1), scale=scale
    )
    stats = lax.all_to_all(
        jnp.broadcast_to(stats[None], (64, *stats.shape)),
        AXES,
        0,
        0,
        axis_index_groups=groups_of_core(),
        tiled=True,
    )
    c0, c1, g0, g1, curve = coefficients(
        me, (l0, l1), (h0, h1), (t0, t1), (p0, p1), stats, targets.reshape(token_count, 1), scale
    )
    curvature = (curve[0] + swap(curve[1], "c")) * (vocab_total / token_count)

    axis_of = {"z": 0, "y": 1, "x": 2}
    summed = []
    halves = back(me, (c0, c1), (g0, g1), (table, table_other), (table_probe, probe_other), root)
    for part, axes in enumerate(("xyz", "yzx", "zxy")):
        send, keep = halves[2 * part], halves[2 * part + 1]
        for i, axis in enumerate(axes):
            keep = keep + swap(send, axis, 0).astype(F32)
            if i < 2:
                k = axis_of[axes[i + 1]]
                send = lax.slice_in_dim(keep, 2, 4, axis=k).astype(BF16)
                keep = lax.slice_in_dim(keep, 0, 2, axis=k)
        summed.append(keep)
    total = jnp.concatenate(summed, axis=-1).astype(BF16).reshape(8, ROWS, width // 8)
    total = lax.all_to_all(total, AXES, 0, 0, axis_index_groups=groups_of_eight(), tiled=True)
    return jnp.sum(total.astype(F32), axis=0).astype(BF16), curvature


def solution(mesh):
    placed = (P("dp", None), P(), P(), P(("dp", "vocab"), None), P(("dp", "vocab"), None))
    return jax.shard_map(
        body,
        mesh=mesh,
        in_specs=placed,
        out_specs=(P("dp", "vocab"), P(("dp", "vocab"))),
        check_vma=False,
    )
```

time: 448 us -> 175 us (0.39)
  waiting for transfers between devices: 233 us -> 48.3 us
  blocking collectives: 129 us -> 0 us
  matrix products: 69.1 us -> 0 us
  Pallas kernels: 0 us -> 58.2 us
  starting transfers between devices: 0.12 us -> 36.6 us
  local copies, waits for them, and re-layouts: 0.01 us -> 21.9 us
  between operations: 13.8 us -> 0.99 us
  other arithmetic: 2.15 us -> 8.1 us
    reduce_scatter x2 -> x0, waiting for transfers between devices: 171 us -> none  [the longest x1 106 us: body(): lax.psum_scatter(root_width * first_part + jnp.dot(gradient_half, table_p...]
    dot_general x6 -> x0, matrix products: 69.1 us -> none  [the longest x4 43 us: row_products(): lax.dot_general(matrix, weights, CONTRACT, preferred_element_type=jnp.flo...]
    pmax x1 -> x0, blocking collectives: 66.2 us -> none  [body(): highest = lax.pmax(jnp.max(logits, axis=1), ('dp', 'vocab'))]
    psum x1 -> x0, blocking collectives: 63 us -> none  [body(): lax.psum((jnp.sum(weights_exp, axis=1), jnp.sum(weights_exp * tangent, ax...]
    all_gather x1 -> x0, waiting for transfers between devices: 61.3 us -> none  [body(): block_rows = lax.all_gather(hidden, 'dp', axis=0, tiled=True)]
    pallas_call x0 -> x9, Pallas kernels: none -> 58.2 us  [the longest x5 41 us: products(): pl.pallas_call(kernel, grid_spec=pltpu.PrefetchScalarGridSpec(num_scalar_...]
    ppermute x0 -> x18, waiting for transfers between devices: none -> 34.8 us  [swap(): return lax.ppermute(a, AXES, pairs(axis, kind))]
    ppermute x0 -> x18, starting transfers between devices: none -> 19.8 us  [swap(): return lax.ppermute(a, AXES, pairs(axis, kind))]
  transfers between devices with their start and end apart: 3 -> 20, of which waited for: 3 -> 11; matrix products, arithmetic and copies ran while one was open for 2% -> 4% of each run, Pallas kernels for 0% -> 18%
where the time goes in v1:
time: 175 us; the launch traced here: 174 us
  Pallas kernels  58.2 us (33%)
  waiting for transfers between devices  48.3 us (28%)
  starting transfers between devices  36.6 us (21%)
  local copies, waits for them, and re-layouts  21.9 us (13%)
  other arithmetic  8.1 us (5%)
    pallas_call x5, Pallas kernels, products(): pl.pallas_call(kernel, grid_spec=pltpu.PrefetchScalarGridSpec(num_scalar_...  41 us
    ppermute x18, waiting for transfers between devices, swap(): return lax.ppermute(a, AXES, pairs(axis, kind))  34.8 us
    ppermute x18, starting transfers between devices, swap(): return lax.ppermute(a, AXES, pairs(axis, kind))  19.8 us
    unnamed x42, local copies, waits for them, and re-layouts  19.7 us
    pallas_call x1, Pallas kernels, back(): pl.pallas_call(kernel, grid_spec=pltpu.PrefetchScalarGridSpec(num_scalar_...  15.8 us
    all_to_all x1, starting transfers between devices, body(): lax.all_to_all(jnp.broadcast_to(stats[None], (64, *stats.shape)), AXES, 0...  11.3 us
    all_to_all x1, waiting for transfers between devices, body(): lax.all_to_all(total, AXES, 0, 0, axis_index_groups=groups_of_eight(), ti...  10.5 us
    all_to_all x1, starting transfers between devices, body(): lax.all_to_all(total, AXES, 0, 0, axis_index_groups=groups_of_eight(), ti...  5.47 us
  transfers between devices with their start and end apart: 20, of which 11 were waited for; matrix products, arithmetic and copies ran while one was open for 4% of the time, Pallas kernels for 18%

profile of v1, /device:TPU:0, one launch (start us, length us, event | category | flops | bytes accessed | tf_op | source)
XLA Modules:
  0.0 174.1 jit_solution(4615243805413219886)
XLA Ops:
  2.3 3.2 %collective-permute-start.1 = (bf16[1,1,48,3072]{3,2,1,0:T(8,128)(2,1)S(1)}, bf16[1,1,48,3072]{3,2,1,0:T(8,128)(2,1)S(1)}, u32[]{:S(2)}, u32[]{:S(2)}) collective-permute-start(bf16[1,1,48,3072]{3,2,1,0:T(8,128)(2,1)S(1)} %get-tuple-element.46), channel_id=1, source_target_pairs={{0,48},{1,49},{2,50},{3,51},{4,52},{5,53},{6,54},{7,55},{8,24},{9,... | collective-permute-start | bytes 884744 | tf_op jit(solution)/shard_map/ppermute | solution.py:48
  5.5 1.9 %collective-permute-start = (bf16[1,1,48,3072]{3,2,1,0:T(8,128)(2,1)S(1)}, bf16[1,1,48,3072]{3,2,1,0:T(8,128)(2,1)S(1)}, u32[]{:S(2)}, u32[]{:S(2)}) collective-permute-start(bf16[1,1,48,3072]{3,2,1,0:T(8,128)(2,1)S(1)} %get-tuple-element.47), channel_id=1, source_target_pairs={{0,64},{1,65},{2,66},{3,67},{4,68},{5,69},{6,70},{7,71},{8,76},{9,... | collective-permute-start | bytes 884744 | tf_op jit(solution)/shard_map/ppermute | solution.py:48
  7.4 2.9 %collective-permute-done.1 = bf16[1,1,48,3072]{3,2,1,0:T(8,128)(2,1)S(1)} collective-permute-done((bf16[1,1,48,3072]{3,2,1,0:T(8,128)(2,1)S(1)}, bf16[1,1,48,3072]{3,2,1,0:T(8,128)(2,1)S(1)}, u32[]{:S(2)}, u32[]{:S(2)}) %collective-permute-start.1) | collective-permute-done | bytes 294944 | tf_op jit(solution)/shard_map/ppermute | solution.py:48
  10.9 2.4 %copy-done = bf16[394,6144]{1,0:T(8,128)(2,1)S(1)} copy-done((bf16[394,6144]{1,0:T(8,128)(2,1)S(1)}, bf16[394,6144]{1,0:T(8,128)(2,1)}, u32[]{:S(2)}) %copy-start) | copy-done | bytes 4841496
  13.3 2.4 %copy-done.3 = bf16[394,6144]{1,0:T(8,128)(2,1)S(1)} copy-done((bf16[394,6144]{1,0:T(8,128)(2,1)S(1)}, bf16[394,6144]{1,0:T(8,128)(2,1)}, u32[]{:S(2)}) %copy-start.3) | copy-done | bytes 4841496
  15.7 8.9 %shard_map.68 = (f32[384,394]{1,0:T(8,128)S(1)}, f32[384,394]{1,0:T(8,128)S(1)}) custom-call(s32[1]{0:T(128)} %bitcast.me_ref, bf16[16,48,6144]{2,1,0:T(8,128)(2,1)} %bitcast.15, bf16[16,48,6144]{2,1,0:T(8,128)(2,1)} %bitcast.16, bf16[16,48,6144]{2,1,0:T(8,128)(2,1)} %bitcast.17, bf16[16,48,6144]{2,1,0:T(8,128)(2,1)} %bitcast.18, ...), custom_call_target="tpu_custom_call" | custom-call | flops 1048576 | bytes 1048576 | tf_op jit(solution)/shard_map/pallas_call | solution.py:185
  25.6 1.2 pad_maximum_fusion.2.refs_1_.refs_9_
  26.8 2.8 %collective-permute-start.3 = (bf16[2,1,48,3072]{3,2,1,0:T(8,128)(2,1)}, bf16[2,1,48,3072]{3,2,1,0:T(8,128)(2,1)S(1)}, u32[]{:S(2)}, u32[]{:S(2)}) collective-permute-start(bf16[2,1,48,3072]{3,2,1,0:T(8,128)(2,1)} %shard_map.69), channel_id=1, source_target_pairs={{0,48},{1,49},{2,50},{3,51},{4,52},{5,53},{6,54},{7,55},{8,24},{9,... | collective-permute-start | bytes 1769480 | tf_op jit(solution)/shard_map/ppermute | solution.py:48
  29.5 1.9 %collective-permute-start.7 = (bf16[1,4,48,3072]{3,2,1,0:T(8,128)(2,1)S(1)}, bf16[1,4,48,3072]{3,2,1,0:T(8,128)(2,1)S(1)}, u32[]{:S(2)}, u32[]{:S(2)}) collective-permute-start(bf16[1,4,48,3072]{3,2,1,0:T(8,128)(2,1)S(1)} %copy-done.6), channel_id=1, source_target_pairs={{0,64},{1,65},{2,66},{3,67},{4,68},{5,69},{6,70},{7,71},{8,76},{9,... | collective-permute-start | bytes 3538952 | tf_op jit(solution)/shard_map/ppermute | solution.py:48
  31.4 6.7 %collective-permute-done.3 = bf16[2,1,48,3072]{3,2,1,0:T(8,128)(2,1)S(1)} collective-permute-done((bf16[2,1,48,3072]{3,2,1,0:T(8,128)(2,1)}, bf16[2,1,48,3072]{3,2,1,0:T(8,128)(2,1)S(1)}, u32[]{:S(2)}, u32[]{:S(2)}) %collective-permute-start.3) | collective-permute-done | bytes 589856 | tf_op jit(solution)/shard_map/ppermute | solution.py:48
  38.1 2.2 %pad_maximum_fusion.3.refs_0_ = bf16[2,2,48,3072]{3,2,1,0:T(8,128)(2,1)} fusion(bf16[2,1,48,3072]{3,2,1,0:T(8,128)(2,1)S(1)} %collective-permute-done.3, bf16[2,1,48,3072]{3,2,1,0:T(8,128)(2,1)} %shard_map.69), kind=kLoop, calls=%fused_computation.6 | loop fusion | flops 589824 | bytes 2359296 | tf_op jit(solution)/shard_map/concatenate | solution.py:106
  40.4 7.7 %shard_map.70.refs_1_.refs_10_.refs_5_ = f32[384,394]{1,0:T(8,128)S(1)} custom-call(s32[1]{0:T(128)} %bitcast.me_ref, bf16[16,48,6144]{2,1,0:T(8,128)(2,1)} %bitcast.26, bf16[16,48,6144]{2,1,0:T(8,128)(2,1)} %bitcast.24, bf16[16,48,6144]{2,1,0:T(8,128)(2,1)} %bitcast.25, bf16[16,48,6144]{2,1,0:T(8,128)(2,1)} %bitcast.23, bf16[16,48,6144]{2,1,0:T(8,128)(2,1)} %bitcast.27, ...), custom_call_target="tpu_custom_call" | custom-call | flops 1048576 | bytes 1048576 | tf_op jit(solution)/shard_map/pallas_call | solution.py:185
  50.0 2.4 %copy-done.1 = bf16[394,6144]{1,0:T(8,128)(2,1)S(1)} copy-done((bf16[394,6144]{1,0:T(8,128)(2,1)S(1)}, bf16[394,6144]{1,0:T(8,128)(2,1)}, u32[]{:S(2)}) %copy-start.1) | copy-done | bytes 4841496
  52.4 7.8 %shard_map.72 = (f32[384,394]{1,0:T(8,128)S(1)}, f32[384,394]{1,0:T(8,128)S(1)}, f32[384,394]{1,0:T(8,128)S(1)}, f32[384,394]{1,0:T(8,128)S(1)}) custom-call(s32[1]{0:T(128)} %bitcast.me_ref, bf16[384,3072]{1,0:T(8,128)(2,1)S(1)} %bitcast.14, bf16[394,6144]{1,0:T(8,128)(2,1)S(1)} %copy-done.1, bf16[394,6144]{1,0:T(8,128)(2,1)} %collective-permute-done.4.refs_8_.refs_2_.t1, ...), custom_call_target="tpu_custom_call" | custom-call | flops 1048576 | bytes 1048576 | tf_op jit(solution)/shard_map/pallas_call | solution.py:185
  60.3 5.1 %collective-permute-done.5 = bf16[2,2,48,3072]{3,2,1,0:T(8,128)(2,1)S(1)} collective-permute-done((bf16[2,2,48,3072]{3,2,1,0:T(8,128)(2,1)}, bf16[2,2,48,3072]{3,2,1,0:T(8,128)(2,1)S(1)}, u32[]{:S(2)}, u32[]{:S(2)}) %collective-permute-start.5) | collective-permute-done | bytes 1179680 | tf_op jit(solution)/shard_map/ppermute | solution.py:48
  65.6 9.0 %shard_map.73 = (f32[384,394]{1,0:T(8,128)S(1)}, f32[384,394]{1,0:T(8,128)S(1)}, f32[384,394]{1,0:T(8,128)S(1)}, f32[384,394]{1,0:T(8,128)S(1)}, f32[3,384]{1,0:T(4,128)S(1)}) custom-call(s32[1]{0:T(128)} %bitcast.me_ref, bf16[384,3072]{1,0:T(8,128)(2,1)S(1)} %bitcast.13, bf16[394,6144]{1,0:T(8,128)(2,1)} %t0.1, ...), custom_call_target="tpu_custom_call" | custom-call | flops 1048576 | bytes 1048576 | tf_op jit(solution)/shard_map/pallas_call | solution.py:185
  78.9 11.3 %all-to-all-start = ((f32[64,3,384]{2,1,0:T(4,128)}), f32[64,3,384]{2,1,0:T(4,128)S(1)}, u32[]{:S(2)}, u32[]{:S(2)}) async-start(f32[64,3,384]{2,1,0:T(4,128)} %broadcast_in_dim.2), calls=%async_computation | async-start | bytes 786432 | tf_op jit(solution)/shard_map/all_to_all | solution.py:374
  90.4 7.7 %shard_map.74.refs_7_ = f32[384,394]{1,0:T(8,128)S(1)} custom-call(s32[1]{0:T(128)} %bitcast.me_ref, bf16[16,48,6144]{2,1,0:T(8,128)(2,1)} %bitcast.31, bf16[16,48,6144]{2,1,0:T(8,128)(2,1)} %bitcast.32, bf16[16,48,6144]{2,1,0:T(8,128)(2,1)} %bitcast.33, bf16[16,48,6144]{2,1,0:T(8,128)(2,1)} %bitcast.34, bf16[16,48,6144]{2,1,0:T(8,128)(2,1)} %bitcast.35, ...), custom_call_target="tpu_custom_call" | custom-call | flops 1048576 | bytes 1048576 | tf_op jit(solution)/shard_map/pallas_call | solution.py:185
  98.1 3.0 %all-to-all-done.refs_8_ = f32[64,3,384]{2,1,0:T(4,128)S(1)} async-done(((f32[64,3,384]{2,1,0:T(4,128)}), f32[64,3,384]{2,1,0:T(4,128)S(1)}, u32[]{:S(2)}, u32[]{:S(2)}) %all-to-all-start) | async-done | bytes 294944 | tf_op jit(solution)/shard_map/all_to_all | solution.py:374
  101.0 1.1 copy-done.10
  102.2 1.1 copy-done.12
  106.7 1.4 shard_map.75
  108.1 2.4 %copy-done.2 = bf16[394,6144]{1,0:T(8,128)(2,1)S(1)} copy-done((bf16[394,6144]{1,0:T(8,128)(2,1)S(1)}, bf16[394,6144]{1,0:T(8,128)(2,1)}, u32[]{:S(2)}) %copy-start.2) | copy-done | bytes 4841496
  110.5 15.8 %shard_map.76 = (bf16[4,4,2,48,256]{4,3,2,1,0:T(8,128)(2,1)S(1)}, f32[4,4,2,48,256]{4,3,2,1,0:T(8,128)S(1)}, bf16[4,2,4,48,256]{4,3,2,1,0:T(8,128)(2,1)S(1)}, f3...) custom-call(s32[1]{0:T(128)} %bitcast.me_ref, ...), custom_call_target="tpu_custom_call" | custom-call | flops 1048576 | bytes 1048576 | tf_op jit(solution)/shard_map/pallas_call | solution.py:331
  128.3 10.1 %collective-permute-done.8 = bf16[4,4,2,48,256]{4,3,2,1,0:T(8,128)(2,1)S(1)} collective-permute-done((bf16[4,4,2,48,256]{4,3,2,1,0:T(8,128)(2,1)S(1)}, bf16[4,4,2,48,256]{4,3,2,1,0:T(8,128)(2,1)S(1)}, u32[]{:S(2)}, u32[]{:S(2)}) %collective-permute-start.8) | collective-permute-done | bytes 786464 | tf_op jit(solution)/shard_map/ppermute | solution.py:48
  142.0 4.6 %collective-permute-done.9 = bf16[4,2,2,48,256]{4,3,2,1,0:T(8,128)(2,1)S(1)} collective-permute-done((bf16[4,2,2,48,256]{4,3,2,1,0:T(8,128)(2,1)S(1)}, bf16[4,2,2,48,256]{4,3,2,1,0:T(8,128)(2,1)S(1)}, u32[]{:S(2)}, u32[]{:S(2)}) %collective-permute-start.9) | collective-permute-done | bytes 393248 | tf_op jit(solution)/shard_map/ppermute | solution.py:48
  148.9 1.4 collective-permute-start.16
  150.3 2.1 %collective-permute-done.10 = bf16[2,2,2,48,256]{4,3,2,1,0:T(8,128)(2,1)S(1)} collective-permute-done((bf16[2,2,2,48,256]{4,3,2,1,0:T(8,128)(2,1)S(1)}, bf16[2,2,2,48,256]{4,3,2,1,0:T(8,128)(2,1)S(1)}, u32[]{:S(2)}, u32[]{:S(2)}) %collective-permute-start.10) | collective-permute-done | bytes 196640 | tf_op jit(solution)/shard_map/ppermute | solution.py:48
  153.5 1.2 collective-permute-done.16
  155.6 5.5 %all-to-all-start.1 = ((bf16[8,48,768]{2,1,0:T(8,128)(2,1)}), bf16[8,48,768]{2,1,0:T(8,128)(2,1)S(1)}, u32[]{:S(2)}, u32[]{:S(2)}) async-start(bf16[8,48,768]{2,1,0:T(8,128)(2,1)} %pad_maximum_fusion.6), calls=%async_computation.1 | async-start | bytes 1179648 | tf_op jit(solution)/shard_map/all_to_all | solution.py:400
  161.2 1.1 collective-permute-done.17
  162.9 10.5 %all-to-all-done.1 = bf16[8,48,768]{2,1,0:T(8,128)(2,1)S(1)} async-done(((bf16[8,48,768]{2,1,0:T(8,128)(2,1)}), bf16[8,48,768]{2,1,0:T(8,128)(2,1)S(1)}, u32[]{:S(2)}, u32[]{:S(2)}) %all-to-all-start.1) | async-done | bytes 589856 | tf_op jit(solution)/shard_map/all_to_all | solution.py:400
  (87 shorter events, 24.5 us)
Async XLA Ops:
  0.6 39.7 %collective-permute-start.4 = (bf16[394,6144]{1,0:T(8,128)(2,1)}, bf16[394,6144]{1,0:T(8,128)(2,1)}, u32[]{:S(2)}, u32[]{:S(2)}) collective-permute-start(bf16[394,6144]{1,0:T(8,128)(2,1)} %t0.1), channel_id=1, source_target_pairs={{0,8},{1,9},{2,10},{3,11},{4,12},{5,13},{6,14},{7,15},{8,0},{9,1},... | collective-permute-start | bytes 14524424 | tf_op jit(solution)/shard_map/ppermute | solution.py:48
  0.7 49.3 %collective-permute-start.6 = (bf16[394,6144]{1,0:T(8,128)(2,1)}, bf16[394,6144]{1,0:T(8,128)(2,1)}, u32[]{:S(2)}, u32[]{:S(2)}) collective-permute-start(bf16[394,6144]{1,0:T(8,128)(2,1)} %p0.1), channel_id=1, source_target_pairs={{0,8},{1,9},{2,10},{3,11},{4,12},{5,13},{6,14},{7,15},{8,0},{9,1},... | collective-permute-start | bytes 14524424 | tf_op jit(solution)/shard_map/ppermute | solution.py:48
  2.3 8.0 %collective-permute-start.1 = (bf16[1,1,48,3072]{3,2,1,0:T(8,128)(2,1)S(1)}, bf16[1,1,48,3072]{3,2,1,0:T(8,128)(2,1)S(1)}, u32[]{:S(2)}, u32[]{:S(2)}) collective-permute-start(bf16[1,1,48,3072]{3,2,1,0:T(8,128)(2,1)S(1)} %get-tuple-element.46), channel_id=1, source_target_pairs={{0,48},{1,49},{2,50},{3,51},{4,52},{5,53},{6,54},{7,55},{8,24},{9,... | collective-permute-start | bytes 884744 | tf_op jit(solution)/shard_map/ppermute | solution.py:48
  5.5 19.1 %collective-permute-start = (bf16[1,1,48,3072]{3,2,1,0:T(8,128)(2,1)S(1)}, bf16[1,1,48,3072]{3,2,1,0:T(8,128)(2,1)S(1)}, u32[]{:S(2)}, u32[]{:S(2)}) collective-permute-start(bf16[1,1,48,3072]{3,2,1,0:T(8,128)(2,1)S(1)} %get-tuple-element.47), channel_id=1, source_target_pairs={{0,64},{1,65},{2,66},{3,67},{4,68},{5,69},{6,70},{7,71},{8,76},{9,... | collective-permute-start | bytes 884744 | tf_op jit(solution)/shard_map/ppermute | solution.py:48
  10.4 15.2 %collective-permute-start.2 = (bf16[1,2,48,3072]{3,2,1,0:T(8,128)(2,1)S(1)}, bf16[1,2,48,3072]{3,2,1,0:T(8,128)(2,1)S(1)}, u32[]{:S(2)}, u32[]{:S(2)}) collective-permute-start(bf16[1,2,48,3072]{3,2,1,0:T(8,128)(2,1)S(1)} %pad_maximum_fusion.5.refs_10_), channel_id=1, source_target_pairs={{0,16},{1,17},{2,18},{3,19},{4,20},{5,21},{6,22},{7,23},{8,56},{9,... | collective-permute-start | bytes 1769480 | tf_op jit(solution)/shard_map/ppermute | solution.py:48
  10.9 2.4 %copy-start = (bf16[394,6144]{1,0:T(8,128)(2,1)S(1)}, bf16[394,6144]{1,0:T(8,128)(2,1)}, u32[]{:S(2)}) copy-start(bf16[394,6144]{1,0:T(8,128)(2,1)} %t0.1) | copy-start | bytes 14524420
  13.3 2.4 %copy-start.3 = (bf16[394,6144]{1,0:T(8,128)(2,1)S(1)}, bf16[394,6144]{1,0:T(8,128)(2,1)}, u32[]{:S(2)}) copy-start(bf16[394,6144]{1,0:T(8,128)(2,1)} %p0.1) | copy-start | bytes 14524420
  24.6 2.2 %copy-start.7 = (f32[384,394]{1,0:T(8,128)}, f32[384,394]{1,0:T(8,128)S(1)}, u32[]{:S(2)}) copy-start(f32[384,394]{1,0:T(8,128)S(1)} %get-tuple-element.24.refs_2_.refs_9_.refs_4_) | copy-start | bytes 1815556
  24.6 2.2 %copy-start.9 = (f32[384,394]{1,0:T(8,128)}, f32[384,394]{1,0:T(8,128)S(1)}, u32[]{:S(2)}) copy-start(f32[384,394]{1,0:T(8,128)S(1)} %get-tuple-element.33.refs_6_) | copy-start | bytes 1815556
  26.8 2.8 %copy-start.6 = (bf16[1,4,48,3072]{3,2,1,0:T(8,128)(2,1)S(1)}, bf16[1,4,48,3072]{3,2,1,0:T(8,128)(2,1)}, u32[]{:S(2)}) copy-start(bf16[1,4,48,3072]{3,2,1,0:T(8,128)(2,1)} %pad_maximum_fusion.2.refs_1_.refs_9_) | copy-start | bytes 3538948
  26.8 11.4 %collective-permute-start.3 = (bf16[2,1,48,3072]{3,2,1,0:T(8,128)(2,1)}, bf16[2,1,48,3072]{3,2,1,0:T(8,128)(2,1)S(1)}, u32[]{:S(2)}, u32[]{:S(2)}) collective-permute-start(bf16[2,1,48,3072]{3,2,1,0:T(8,128)(2,1)} %shard_map.69), channel_id=1, source_target_pairs={{0,48},{1,49},{2,50},{3,51},{4,52},{5,53},{6,54},{7,55},{8,24},{9,... | collective-permute-start | bytes 1769480 | tf_op jit(solution)/shard_map/ppermute | solution.py:48
  29.5 20.2 %collective-permute-start.7 = (bf16[1,4,48,3072]{3,2,1,0:T(8,128)(2,1)S(1)}, bf16[1,4,48,3072]{3,2,1,0:T(8,128)(2,1)S(1)}, u32[]{:S(2)}, u32[]{:S(2)}) collective-permute-start(bf16[1,4,48,3072]{3,2,1,0:T(8,128)(2,1)S(1)} %copy-done.6), channel_id=1, source_target_pairs={{0,64},{1,65},{2,66},{3,67},{4,68},{5,69},{6,70},{7,71},{8,76},{9,... | collective-permute-start | bytes 3538952 | tf_op jit(solution)/shard_map/ppermute | solution.py:48
  48.9 16.4 %collective-permute-start.5 = (bf16[2,2,48,3072]{3,2,1,0:T(8,128)(2,1)}, bf16[2,2,48,3072]{3,2,1,0:T(8,128)(2,1)S(1)}, u32[]{:S(2)}, u32[]{:S(2)}) collective-permute-start(bf16[2,2,48,3072]{3,2,1,0:T(8,128)(2,1)} %shard_map.71), channel_id=1, source_target_pairs={{0,16},{1,17},{2,18},{3,19},{4,20},{5,21},{6,22},{7,23},{8,56},{9,... | collective-permute-start | bytes 3538952 | tf_op jit(solution)/shard_map/ppermute | solution.py:48
  50.0 2.4 %copy-start.1 = (bf16[394,6144]{1,0:T(8,128)(2,1)S(1)}, bf16[394,6144]{1,0:T(8,128)(2,1)}, u32[]{:S(2)}) copy-start(bf16[394,6144]{1,0:T(8,128)(2,1)} %t0.1) | copy-start | bytes 14524420
  52.4 12.9 %copy-start.19 = (bf16[2,2,48,3072]{3,2,1,0:T(8,128)(2,1)S(1)}, bf16[2,2,48,3072]{3,2,1,0:T(8,128)(2,1)}, u32[]{:S(2)}) copy-start(bf16[2,2,48,3072]{3,2,1,0:T(8,128)(2,1)} %shard_map.71) | copy-start | bytes 3538948
  60.2 5.3 %copy-start.5 = (f32[384,394]{1,0:T(8,128)S(1)}, f32[384,394]{1,0:T(8,128)}, u32[]{:S(2)}) copy-start(f32[384,394]{1,0:T(8,128)} %copy-done.4) | copy-start | bytes 1815556
  60.2 5.3 %copy-start.8 = (f32[384,394]{1,0:T(8,128)S(1)}, f32[384,394]{1,0:T(8,128)}, u32[]{:S(2)}) copy-start(f32[384,394]{1,0:T(8,128)} %copy-done.7) | copy-start | bytes 1815556
  65.6 24.7 %copy-start.20 = (s32[768]{0:T(1024)S(1)}, s32[768]{0:T(1024)}, u32[]{:S(2)}) copy-start(s32[768]{0:T(1024)} %param.6) | copy-start | bytes 9220
  78.9 22.1 %all-to-all-start = ((f32[64,3,384]{2,1,0:T(4,128)}), f32[64,3,384]{2,1,0:T(4,128)S(1)}, u32[]{:S(2)}, u32[]{:S(2)}) async-start(f32[64,3,384]{2,1,0:T(4,128)} %broadcast_in_dim.2), calls=%async_computation | async-start | bytes 786432 | tf_op jit(solution)/shard_map/all_to_all | solution.py:374
  101.0 1.1 copy-start.10
  108.1 2.4 %copy-start.2 = (bf16[394,6144]{1,0:T(8,128)(2,1)S(1)}, bf16[394,6144]{1,0:T(8,128)(2,1)}, u32[]{:S(2)}) copy-start(bf16[394,6144]{1,0:T(8,128)(2,1)} %t0.1) | copy-start | bytes 14524420
  126.3 12.1 %collective-permute-start.8 = (bf16[4,4,2,48,256]{4,3,2,1,0:T(8,128)(2,1)S(1)}, bf16[4,4,2,48,256]{4,3,2,1,0:T(8,128)(2,1)S(1)}, u32[]{:S(2)}, u32[]{:S(2)}) collective-permute-start(bf16[4,4,2,48,256]{4,3,2,1,0:T(8,128)(2,1)S(1)} %get-tuple-element.40), channel_id=1, source_target_pairs={{0,1},{1,0},{2,3},{3,2},{4,5},{5,4},{6,7},{7,6},{8,11},{9,10},{10,... | collective-permute-start | bytes 2359304 | tf_op jit(solution)/shard_map/ppermute | solution.py:48
  126.9 12.5 %collective-permute-start.11 = (bf16[4,2,4,48,256]{4,3,2,1,0:T(8,128)(2,1)S(1)}, bf16[4,2,4,48,256]{4,3,2,1,0:T(8,128)(2,1)S(1)}, u32[]{:S(2)}, u32[]{:S(2)}) collective-permute-start(bf16[4,2,4,48,256]{4,3,2,1,0:T(8,128)(2,1)S(1)} %get-tuple-element.42), channel_id=1, source_target_pairs={{0,16},{1,17},{2,18},{3,19},{4,20},{5,21},{6,22},{7,23},{8,56},{9,... | collective-permute-start | bytes 2359304 | tf_op jit(solution)/shard_map/ppermute | solution.py:48
  127.5 13.0 %collective-permute-start.14 = (bf16[2,4,4,48,256]{4,3,2,1,0:T(8,128)(2,1)S(1)}, bf16[2,4,4,48,256]{4,3,2,1,0:T(8,128)(2,1)S(1)}, u32[]{:S(2)}, u32[]{:S(2)}) collective-permute-start(bf16[2,4,4,48,256]{4,3,2,1,0:T(8,128)(2,1)S(1)} %get-tuple-element.44), channel_id=1, source_target_pairs={{0,64},{1,65},{2,66},{3,67},{4,68},{5,69},{6,70},{7,71},{8,76},{9,... | collective-permute-start | bytes 2359304 | tf_op jit(solution)/shard_map/ppermute | solution.py:48
  138.7 7.9 %collective-permute-start.9 = (bf16[4,2,2,48,256]{4,3,2,1,0:T(8,128)(2,1)S(1)}, bf16[4,2,2,48,256]{4,3,2,1,0:T(8,128)(2,1)S(1)}, u32[]{:S(2)}, u32[]{:S(2)}) collective-permute-start(bf16[4,2,2,48,256]{4,3,2,1,0:T(8,128)(2,1)S(1)} %slice.104), channel_id=1, source_target_pairs={{0,16},{1,17},{2,18},{3,19},{4,20},{5,21},{6,22},{7,23},{8,56},{9,... | collective-permute-start | bytes 1179656 | tf_op jit(solution)/shard_map/ppermute | solution.py:48
  139.7 7.9 %collective-permute-start.12 = (bf16[2,2,4,48,256]{4,3,2,1,0:T(8,128)(2,1)S(1)}, bf16[2,2,4,48,256]{4,3,2,1,0:T(8,128)(2,1)S(1)}, u32[]{:S(2)}, u32[]{:S(2)}) collective-permute-start(bf16[2,2,4,48,256]{4,3,2,1,0:T(8,128)(2,1)S(1)} %slice.103), channel_id=1, source_target_pairs={{0,64},{1,65},{2,66},{3,67},{4,68},{5,69},{6,70},{7,71},{8,76},{9,... | collective-permute-start | bytes 1179656 | tf_op jit(solution)/shard_map/ppermute | solution.py:48
  140.8 8.0 %collective-permute-start.15 = (bf16[2,4,2,48,256]{4,3,2,1,0:T(8,128)(2,1)S(1)}, bf16[2,4,2,48,256]{4,3,2,1,0:T(8,128)(2,1)S(1)}, u32[]{:S(2)}, u32[]{:S(2)}) collective-permute-start(bf16[2,4,2,48,256]{4,3,2,1,0:T(8,128)(2,1)S(1)} %slice.102), channel_id=1, source_target_pairs={{0,1},{1,0},{2,3},{3,2},{4,5},{5,4},{6,7},{7,6},{8,11},{9,10},{10,... | collective-permute-start | bytes 1179656 | tf_op jit(solution)/shard_map/ppermute | solution.py:48
  146.7 5.8 %collective-permute-start.10 = (bf16[2,2,2,48,256]{4,3,2,1,0:T(8,128)(2,1)S(1)}, bf16[2,2,2,48,256]{4,3,2,1,0:T(8,128)(2,1)S(1)}, u32[]{:S(2)}, u32[]{:S(2)}) collective-permute-start(bf16[2,2,2,48,256]{4,3,2,1,0:T(8,128)(2,1)S(1)} %slice.107), channel_id=1, source_target_pairs={{0,64},{1,65},{2,66},{3,67},{4,68},{5,69},{6,70},{7,71},{8,76},{9,... | collective-permute-start | bytes 589832 | tf_op jit(solution)/shard_map/ppermute | solution.py:48
  147.7 5.7 %collective-permute-start.13 = (bf16[2,2,2,48,256]{4,3,2,1,0:T(8,128)(2,1)S(1)}, bf16[2,2,2,48,256]{4,3,2,1,0:T(8,128)(2,1)S(1)}, u32[]{:S(2)}, u32[]{:S(2)}) collective-permute-start(bf16[2,2,2,48,256]{4,3,2,1,0:T(8,128)(2,1)S(1)} %slice.106), channel_id=1, source_target_pairs={{0,1},{1,0},{2,3},{3,2},{4,5},{5,4},{6,7},{7,6},{8,11},{9,10},{10,... | collective-permute-start | bytes 589832 | tf_op jit(solution)/shard_map/ppermute | solution.py:48
  148.9 5.7 %collective-permute-start.16 = (bf16[2,2,2,48,256]{4,3,2,1,0:T(8,128)(2,1)S(1)}, bf16[2,2,2,48,256]{4,3,2,1,0:T(8,128)(2,1)S(1)}, u32[]{:S(2)}, u32[]{:S(2)}) collective-permute-start(bf16[2,2,2,48,256]{4,3,2,1,0:T(8,128)(2,1)S(1)} %slice.105), channel_id=1, source_target_pairs={{0,16},{1,17},{2,18},{3,19},{4,20},{5,21},{6,22},{7,23},{8,56},{9,... | collective-permute-start | bytes 589832 | tf_op jit(solution)/shard_map/ppermute | solution.py:48
  155.6 17.8 %all-to-all-start.1 = ((bf16[8,48,768]{2,1,0:T(8,128)(2,1)}), bf16[8,48,768]{2,1,0:T(8,128)(2,1)S(1)}, u32[]{:S(2)}, u32[]{:S(2)}) async-start(bf16[8,48,768]{2,1,0:T(8,128)(2,1)} %pad_maximum_fusion.6), calls=%async_computation.1 | async-start | bytes 1179648 | tf_op jit(solution)/shard_map/all_to_all | solution.py:400
  161.1 1.2 collective-permute-start.17
  (9 other events, 9.0 us)

commit v2 on v1

v2 whole, which is shorter than its diff:
```python
import math

import jax
import jax.numpy as jnp
from jax import lax
from jax.experimental import pallas as pl
from jax.experimental.pallas import tpu as pltpu
from jax.sharding import PartitionSpec as P

AXES = ("dp", "vocab")
F32 = jnp.float32
BF16 = jnp.bfloat16
FIRST = 3072
BLOCK = 1024
PROBE_BLOCK = 2048
ROWS = 48
MIB = 1 << 20
NT = (((1,), (1,)), ((), ()))


def decode(d):
    return (d >> 6) & 1, (d >> 4) & 3, (d >> 3) & 1, (d >> 2) & 1, d & 3


def encode(zl, y, c, zh, x):
    return (((zl * 4 + y) * 2 + c) * 2 + zh) * 4 + x


def pairs(axes, kind):
    out = []
    for d in range(128):
        zl, y, c, zh, x = decode(d)
        m = 1 if c == kind else 3
        for axis in axes:
            if axis == "x":
                x ^= m
            elif axis == "y":
                y ^= m
            elif axis == "z":
                z = (2 * zh + zl) ^ m
                zh, zl = z >> 1, z & 1
            else:
                c ^= 1
        out.append((d, encode(zl, y, c, zh, x)))
    return out


def swap(a, axis, kind=0):
    return lax.ppermute(a, AXES, pairs(axis, kind))


def pair_of(c, q):
    return jnp.where(c == 0, (q ^ (q >> 1)) & 1, q >> 1)


def bit_of(c, q):
    return jnp.where(c == 0, q >> 1, q & 1)


def member(c, pair, bit):
    return jnp.where(c == 0, pair * (1 + bit) + (1 - pair) * 3 * bit, 2 * pair + bit)


def slot_of(c, me, q):
    return 2 * (pair_of(c, me) ^ pair_of(c, q)) + bit_of(c, q)


def groups_of_eight():
    found = {}
    for d in range(128):
        zl, y, c, zh, x = decode(d)
        at = [2 * zh + zl, y, x]
        pair = [(q ^ (q >> 1)) & 1 if c == 0 else q >> 1 for q in at]
        bit = [q >> 1 if c == 0 else q & 1 for q in at]
        found.setdefault((c, *pair), {})[tuple(bit)] = d
    return [[g[b] for b in sorted(g)] for g in found.values()]


def groups_of_core():
    return [[d for d in range(128) if decode(d)[2] == c] for c in range(2)]


def row_place(me, slot):
    zl, y, c, _, _ = decode(me)
    zs, ys = slot // 4, slot % 4
    return (zl ^ zs) * 4 + (y ^ jnp.where(c == 0, (0, 3, 1, 2)[ys], (0, 1, 3, 2)[ys]))


def owner(me, slot):
    return row_place(me, slot) * 2 + ((me >> 3) & 1)


def tie(array, *after):
    def kernel(*refs):
        del refs

    return pl.pallas_call(
        kernel,
        in_specs=[pl.BlockSpec(memory_space=pl.ANY)] * (1 + len(after)),
        out_specs=pl.BlockSpec(memory_space=pl.ANY),
        out_shape=jax.ShapeDtypeStruct(array.shape, array.dtype),
        input_output_aliases={0: 0},
    )(array, *after)


def probe_products(me, rows, table, after=()):
    m, k = 8 * ROWS, rows.shape[-1]
    n = table.shape[0]

    def kernel(me_ref, *refs):
        row_refs, table_ref, out_ref = refs[:8], refs[8], refs[-1]
        block = jnp.concatenate([r[0] for r in row_refs], axis=0)

        @pl.when(pl.program_id(0) == 0)
        def _():
            out_ref[...] = jnp.zeros((m, n), F32)

        out_ref[...] += lax.dot_general(block, table_ref[...], NT, preferred_element_type=F32)

    return pl.pallas_call(
        kernel,
        grid_spec=pltpu.PrefetchScalarGridSpec(
            num_scalar_prefetch=1,
            grid=(k // PROBE_BLOCK,),
            in_specs=[
                pl.BlockSpec((1, ROWS, PROBE_BLOCK), lambda s, me, i=i: (owner(me[0], i), 0, s)) for i in range(8)
            ]
            + [pl.BlockSpec((n, PROBE_BLOCK), lambda s, me: (0, s))]
            + [pl.BlockSpec(memory_space=pl.ANY)] * len(after),
            out_specs=pl.BlockSpec((m, n), lambda s, me: (0, 0)),
        ),
        out_shape=jax.ShapeDtypeStruct((m, n), F32),
        compiler_params=pltpu.CompilerParams(vmem_limit_bytes=60 * MIB),
        cost_estimate=pl.CostEstimate(flops=MIB, bytes_accessed=MIB, transcendentals=0),
    )(me, *([rows] * 8), table, *after)


def hidden_products(me, pieces, tables, tangents, scale):
    m = 8 * ROWS
    k = pieces[0].shape[1] + pieces[2].shape[1]
    n = tables[0].shape[0]
    steps = k // BLOCK
    split = FIRST // BLOCK
    pair = 2 * ROWS

    def kernel(me_ref, *refs):
        piece_refs, table_refs, tangent_refs = refs[0:4], refs[4:8], refs[8:10]
        outs, stats_ref = refs[10:14], refs[14]
        rows_ref, tables_ref, packed_ref, held_ref, sems, row_sems, table_sems = refs[15:22]
        step = pl.program_id(0)
        copies = [pltpu.make_async_copy(tangent_refs[i], held_ref.at[i], sems.at[i]) for i in range(2)]

        def row_copies(at):
            if at < split:
                parts = [(0, 0, 0, m // 2), (1, 0, m // 2, m // 2)]
                column = at * BLOCK
            else:
                parts = [(2 + i % 2, i // 2 * pair, i * pair, pair) for i in range(4)]
                column = (at - split) * BLOCK
            return [
                pltpu.make_async_copy(
                    piece_refs[p].at[pl.ds(source, length), pl.ds(column, BLOCK)],
                    rows_ref.at[at, pl.ds(target, length)],
                    row_sems.at[at, i],
                )
                for i, (p, source, target, length) in enumerate(parts)
            ]

        def table_copies(at):
            column = at * BLOCK
            return [
                pltpu.make_async_copy(
                    table_refs[i].at[:, pl.ds(column, BLOCK)], tables_ref.at[at, i], table_sems.at[at, i]
                )
                for i in range(4)
            ]

        @pl.when(step == 0)
        def _():
            for copy in row_copies(0) + table_copies(0):
                copy.start()
            for i in range(4):
                outs[i][...] = jnp.zeros((m, n), F32)

        for at in range(steps):

            @pl.when(step == at)
            def _():
                for copy in row_copies(at) + table_copies(at):
                    copy.wait()
                for then in ((1, 2) if at == 0 else (at + 2,)):
                    if then < steps:
                        for copy in row_copies(then) + table_copies(then):
                            copy.start()
                if at == 1:
                    for copy in copies:
                        copy.start()

        for i in range(4):
            outs[i][...] += lax.dot_general(
                rows_ref[step], tables_ref[step, i], NT, preferred_element_type=F32
            )

        @pl.when(step == steps - 1)
        def _():
            for copy in copies:
                copy.wait()
            lane = lax.broadcasted_iota(jnp.int32, (ROWS, 128), 1)
            for i in range(8):
                at = slice(i * ROWS, (i + 1) * ROWS)
                l0, l1 = outs[0][at, :], outs[1][at, :]
                t0 = held_ref[0, at, :] + outs[2][at, :] * scale
                t1 = held_ref[1, at, :] + outs[3][at, :] * scale
                top = jnp.maximum(jnp.max(l0, axis=1, keepdims=True), jnp.max(l1, axis=1, keepdims=True))
                e0 = jnp.exp(l0 - top)
                e1 = jnp.exp(l1 - top)
                total = jnp.sum(e0, axis=1, keepdims=True) + jnp.sum(e1, axis=1, keepdims=True)
                weighted = jnp.sum(e0 * t0, axis=1, keepdims=True) + jnp.sum(
                    e1 * t1, axis=1, keepdims=True
                )
                place = pl.multiple_of(row_place(me_ref[0], i) * ROWS, ROWS)
                packed_ref[pl.ds(place, ROWS), :] = jnp.where(
                    lane == 0, top, jnp.where(lane == 1, total, weighted)
                )
            stats_ref[...] = jnp.broadcast_to(packed_ref[...].T[0:3, :][None], (64, 3, m))

    return pl.pallas_call(
        kernel,
        grid_spec=pltpu.PrefetchScalarGridSpec(
            num_scalar_prefetch=1,
            grid=(steps,),
            in_specs=[pl.BlockSpec(memory_space=pl.ANY)] * 10,
            out_specs=[pl.BlockSpec((m, n), lambda s, me: (0, 0))] * 4
            + [pl.BlockSpec((64, 3, m), lambda s, me: (0, 0, 0))],
            scratch_shapes=[
                pltpu.VMEM((steps, m, BLOCK), BF16),
                pltpu.VMEM((steps, 4, n, BLOCK), BF16),
                pltpu.VMEM((m, 128), F32),
                pltpu.VMEM((2, m, n), F32),
                pltpu.SemaphoreType.DMA((2,)),
                pltpu.SemaphoreType.DMA((steps, 4)),
                pltpu.SemaphoreType.DMA((steps, 4)),
            ],
        ),
        out_shape=[jax.ShapeDtypeStruct((m, n), F32)] * 4 + [jax.ShapeDtypeStruct((64, 3, m), F32)],
        compiler_params=pltpu.CompilerParams(vmem_limit_bytes=60 * MIB),
        cost_estimate=pl.CostEstimate(flops=MIB, bytes_accessed=MIB, transcendentals=0),
    )(me, *pieces, *tables, *tangents)


def coefficients(me, logits, sides, tangents, probes, stats, targets, scale):
    m, n = logits[0].shape

    def kernel(me_ref, *refs):
        l_refs, h_refs, t_refs, p_refs = refs[0:2], refs[2:4], refs[4:6], refs[6:8]
        stats_ref, targets_ref = refs[8:10]
        c_refs, g_refs, curve_ref, column_ref = refs[10:12], refs[12:14], refs[14], refs[15]
        here = me_ref[0]
        tops = stats_ref[:, 0, :]
        top = jnp.max(tops, axis=0, keepdims=True)
        factor = jnp.exp(tops - top)
        total = jnp.sum(stats_ref[:, 1, :] * factor, axis=0, keepdims=True)
        mean = jnp.sum(stats_ref[:, 2, :] * factor, axis=0, keepdims=True) / total
        inverse = 1.0 / total
        line = lax.broadcasted_iota(jnp.int32, (128, m), 0)
        column_ref[...] = jnp.where(line == 0, top, jnp.where(line == 1, inverse, mean)).T
        for i in range(2):
            vocab_start = (here ^ (8 * i)) * n
            curve_sum = jnp.zeros((1, n), F32)
            for j in range(8):
                at = slice(j * ROWS, (j + 1) * ROWS)
                place = row_place(here, j)
                values = column_ref[pl.ds(pl.multiple_of(place * ROWS, ROWS), ROWS), :]
                mine = pl.multiple_of(owner(here, j) * ROWS, ROWS)
                wanted = targets_ref[pl.ds(mine, ROWS), :]
                side = h_refs[i][at, :] * scale
                tangent = t_refs[i][at, :] + side
                probability = jnp.exp(l_refs[i][at, :] - values[:, 0:1]) * values[:, 1:2]
                curve = probability * (tangent - values[:, 2:3])
                column = lax.broadcasted_iota(jnp.int32, (ROWS, n), 1) + vocab_start
                gradient = probability - jnp.where(wanted == column, 1.0, 0.0)
                c_refs[i][at, :] = curve.astype(BF16)
                g_refs[i][at, :] = gradient.astype(BF16)
                curve_sum += jnp.sum(
                    curve * side + gradient * (p_refs[i][at, :] * scale), axis=0, keepdims=True
                )
            curve_ref[i : i + 1, :] = curve_sum

    vmem = pl.BlockSpec(memory_space=pltpu.VMEM)
    return pl.pallas_call(
        kernel,
        in_specs=[pl.BlockSpec(memory_space=pltpu.SMEM)] + [vmem] * 10,
        out_specs=[vmem] * 5,
        out_shape=[jax.ShapeDtypeStruct((m, n), BF16)] * 4 + [jax.ShapeDtypeStruct((2, n), F32)],
        scratch_shapes=[pltpu.VMEM((m, 128), F32)],
        compiler_params=pltpu.CompilerParams(vmem_limit_bytes=60 * MIB),
    )(me, *logits, *sides, *tangents, *probes, stats, targets)


def back(me, curves, gradients, tables, probes, root, turn, after=()):
    m, n = curves[0].shape
    width = 768
    part = width // 3
    steps = 4

    def kernel(me_ref, c0, c1, g0, g1, *refs):
        table_refs, outs, (held, sems) = refs[0:4], refs[4 + len(after) : 9 + len(after)], refs[-2:]
        step = pl.program_id(0)
        zl, y, c, zh, x = decode(me_ref[0])

        def copies(at):
            slot = 2 * (1 - turn) + (at >> 1)
            to_x = member(c, pair_of(c, x) ^ (slot >> 1), slot & 1)
            column = pl.multiple_of(((zh ^ (at & 1)) * 4 + to_x) * width, width)
            return [
                pltpu.make_async_copy(
                    table_refs[i].at[:, pl.ds(column, width)], held.at[at, i], sems.at[at, i]
                )
                for i in range(4)
            ]

        @pl.when(step == 0)
        def _():
            for copy in copies(0):
                copy.start()

        for copy in copies(step):
            copy.wait()

        @pl.when(step == 0)
        def _():
            for copy in copies(1):
                copy.start()

        @pl.when(step < steps - 2)
        def _():
            for copy in copies(step + 2):
                copy.start()

        total = jnp.dot(c0[...], held[step, 0], preferred_element_type=F32)
        total += jnp.dot(c1[...], held[step, 1], preferred_element_type=F32)
        total *= root
        total += jnp.dot(g0[...], held[step, 2], preferred_element_type=F32)
        total += jnp.dot(g1[...], held[step, 3], preferred_element_type=F32)

        def places(slot):
            place = row_place(me_ref[0], slot)
            zs = slot_of(c, 2 * zh + zl, 2 * (zh ^ (step & 1)) + (place >> 2))
            return zs, slot_of(c, y, place & 3), slice(slot * ROWS, (slot + 1) * ROWS)

        for slot in range(8):
            zs, ys, at = places(slot)
            outs[0][zs, ys, 0] = total[at, :part].astype(outs[0].dtype)
            if slot % 4 < 2:
                outs[2][zs, ys, 0] = total[at, part : 2 * part]
            else:
                outs[1][zs, ys - 2, 0] = total[at, part : 2 * part].astype(BF16)

        for half_rows in range(2):
            z_slot = places(4 * half_rows)[0]

            @pl.when(z_slot >= 2)
            def _():
                for slot in range(4 * half_rows, 4 * half_rows + 4):
                    zs, ys, at = places(slot)
                    outs[3][zs - 2, ys, 0] = total[at, 2 * part :].astype(BF16)

            @pl.when(z_slot < 2)
            def _():
                for slot in range(4 * half_rows, 4 * half_rows + 4):
                    zs, ys, at = places(slot)
                    outs[4][zs, ys, 0] = total[at, 2 * part :]

    shapes, specs = [], []
    for z, y, dtype in ((4, 4, F32 if turn else BF16), (4, 2, BF16), (4, 2, F32), (2, 4, BF16), (2, 4, F32)):
        shapes.append(jax.ShapeDtypeStruct((z, y, 2, ROWS, part), dtype))
        specs.append(pl.BlockSpec((z, y, 1, ROWS, part), lambda s, me: (0, 0, s >> 1, 0, 0)))
    return pl.pallas_call(
        kernel,
        grid_spec=pltpu.PrefetchScalarGridSpec(
            num_scalar_prefetch=1,
            grid=(steps,),
            in_specs=[pl.BlockSpec((m, n), lambda s, me: (0, 0))] * 4
            + [pl.BlockSpec(memory_space=pl.ANY)] * (4 + len(after)),
            out_specs=specs,
            scratch_shapes=[pltpu.VMEM((steps, 4, n, width), BF16), pltpu.SemaphoreType.DMA((steps, 4))],
        ),
        out_shape=shapes,
        compiler_params=pltpu.CompilerParams(vmem_limit_bytes=60 * MIB),
        cost_estimate=pl.CostEstimate(flops=MIB, bytes_accessed=MIB, transcendentals=0),
    )(me, *curves, *gradients, *tables, *probes, *after)


def body(hidden, targets, hidden_probe, table, table_probe):
    vocab_rows, width = table.shape
    token_count = targets.shape[0]
    vocab_total = vocab_rows * 128
    scale = 1.0 / math.sqrt(width)
    root = math.sqrt(width)
    me = lax.axis_index(AXES).astype(jnp.int32).reshape(1)

    own = hidden.reshape(1, 1, ROWS, width)
    got = swap(own, "y", 1)
    table_other = swap(table, "c")
    probe_other = swap(table_probe, "c")
    probe_rows = hidden_probe.reshape(token_count // ROWS, ROWS, width)
    t0 = probe_products(me, probe_rows, table)
    got = tie(got, t0)
    first = jnp.concatenate([own[..., :FIRST], got[..., :FIRST]], axis=1)
    second = jnp.concatenate([own[..., FIRST:], got[..., FIRST:]], axis=1)
    first_got, second_got = swap(first, "y", 0), swap(second, "z")
    p0 = probe_products(me, probe_rows, table_probe, after=(first, second))
    first = jnp.concatenate([first, tie(first_got, p0)], axis=1)
    second = jnp.concatenate([second, tie(second_got, p0)], axis=0)
    first_got, second_got = swap(first, "z"), swap(second, "y", 0)
    t1 = probe_products(me, probe_rows, table_other, after=(first, second))
    pieces = [a.reshape(4 * ROWS, -1) for a in (first, tie(first_got, t1), second, tie(second_got, t1))]
    p1 = probe_products(me, probe_rows, probe_other)
    l0, l1, h0, h1, stats = hidden_products(
        me, pieces, (table, table_other, table_probe, probe_other), (t0, t1), scale
    )
    stats = lax.all_to_all(
        stats,
        AXES,
        0,
        0,
        axis_index_groups=groups_of_core(),
        tiled=True,
    )
    c0, c1, g0, g1, curve = coefficients(
        me, (l0, l1), (h0, h1), (t0, t1), (p0, p1), stats, targets.reshape(token_count, 1), scale
    )
    curvature = (curve[0] + swap(curve[1], "c")) * (vocab_total / token_count)

    operands = (me, (c0, c1), (g0, g1), (table, table_other), (table_probe, probe_other), root)
    x_send, *early = back(*operands, 0)
    x_keep, *late = back(*operands, 1, after=(x_send,))

    def wide(a):
        return a.astype(F32)

    def halve(keep, axis):
        k = "zyx".index(axis)
        send = lax.slice_in_dim(keep, 2, 4, axis=k).astype(BF16)
        return lax.slice_in_dim(keep, 0, 2, axis=k) + wide(swap(send, axis))

    summed = [halve(halve(x_keep + wide(swap(x_send, "x")), "z"), "y")]
    for i, (axis, last) in enumerate((("y", "z"), ("z", "y"))):
        send = early[2 * i + 1] + wide(swap(early[2 * i], axis))
        keep = late[2 * i + 1] + wide(swap(late[2 * i], axis))
        summed.append(halve(keep + wide(swap(send.astype(BF16), "x")), last))
    total = jnp.concatenate(summed, axis=-1).astype(BF16).reshape(8, ROWS, width // 8)
    total = lax.all_to_all(total, AXES, 0, 0, axis_index_groups=groups_of_eight(), tiled=True)
    return jnp.sum(total.astype(F32), axis=0).astype(BF16), curvature


def solution(mesh):
    placed = (P("dp", None), P(), P(), P(("dp", "vocab"), None), P(("dp", "vocab"), None))
    return jax.shard_map(
        body,
        mesh=mesh,
        in_specs=placed,
        out_specs=(P("dp", "vocab"), P(("dp", "vocab"))),
        check_vma=False,
    )
```

time: 175 us -> 158 us (0.903)
  local copies, waits for them, and re-layouts: 21.9 us -> 5.47 us
  Pallas kernels: 58.2 us -> 73.4 us
  waiting for transfers between devices: 48.3 us -> 35.8 us
  other arithmetic: 8.1 us -> 5.8 us
    unnamed x42 -> x34, local copies, waits for them, and re-layouts: 19.7 us -> 3.3 us
    ppermute x18 -> x19, waiting for transfers between devices: 34.8 us -> 22.7 us  [swap(): return lax.ppermute(a, AXES, pairs(axis, kind))]
    pallas_call x5, Pallas kernels: 41 us -> 46.6 us  [the longest x4 29.4 us: probe_products(): pl.pallas_call(kernel, grid_spec=pltpu.PrefetchScalarGridSpec(num_scalar_...]
    pallas_call x1 -> x2, Pallas kernels: 15.8 us -> 21.4 us  [back(): pl.pallas_call(kernel, grid_spec=pltpu.PrefetchScalarGridSpec(num_scalar_...]
    pallas_call x1, Pallas kernels: 1.4 us -> 5.39 us  [coefficients(): pl.pallas_call(kernel, in_specs=[pl.BlockSpec(memory_space=pltpu.SMEM)] +...]
    concatenate x6 -> x4, other arithmetic: 4.83 us -> 2.64 us  [the longest x1 1.34 us: body(): first = jnp.concatenate([first, tie(first_got, p0)], axis=1)]
    ppermute x18 -> x19, starting transfers between devices: 19.8 us -> 18.5 us  [swap(): return lax.ppermute(a, AXES, pairs(axis, kind))]
  transfers between devices with their start and end apart: 20 -> 21, of which waited for: 11 -> 12; matrix products, arithmetic and copies ran while one was open for 4% -> 4% of each run, Pallas kernels for 18% -> 25%
where the time goes in v2:
time: 158 us; the launch traced here: 157 us
  Pallas kernels  73.4 us (46%)
  starting transfers between devices  36 us (23%)
  waiting for transfers between devices  35.8 us (23%)
  other arithmetic  5.8 us (4%)
  local copies, waits for them, and re-layouts  5.47 us (3%)
    pallas_call x4, Pallas kernels, probe_products(): pl.pallas_call(kernel, grid_spec=pltpu.PrefetchScalarGridSpec(num_scalar_...  29.4 us
    ppermute x19, waiting for transfers between devices, swap(): return lax.ppermute(a, AXES, pairs(axis, kind))  22.7 us
    pallas_call x2, Pallas kernels, back(): pl.pallas_call(kernel, grid_spec=pltpu.PrefetchScalarGridSpec(num_scalar_...  21.4 us
    ppermute x19, starting transfers between devices, swap(): return lax.ppermute(a, AXES, pairs(axis, kind))  18.5 us
    pallas_call x1, Pallas kernels, hidden_products(): pl.pallas_call(kernel, grid_spec=pltpu.PrefetchScalarGridSpec(num_scalar_...  17.2 us
    all_to_all x1, starting transfers between devices, body(): lax.all_to_all(stats, AXES, 0, 0, axis_index_groups=groups_of_core(), til...  11.3 us
    all_to_all x1, waiting for transfers between devices, body(): lax.all_to_all(total, AXES, 0, 0, axis_index_groups=groups_of_eight(), ti...  10.5 us
    all_to_all x1, starting transfers between devices, body(): lax.all_to_all(total, AXES, 0, 0, axis_index_groups=groups_of_eight(), ti...  6.2 us
  transfers between devices with their start and end apart: 21, of which 12 were waited for; matrix products, arithmetic and copies ran while one was open for 4% of the time, Pallas kernels for 25%

profile of v2, /device:TPU:0, one launch (start us, length us, event | category | flops | bytes accessed | tf_op | source)
XLA Modules:
  0.0 157.4 jit_solution(18332784658280909035)
XLA Ops:
  1.2 3.1 %collective-permute-start = (bf16[1,1,48,6144]{3,2,1,0:T(8,128)(2,1)}, bf16[1,1,48,6144]{3,2,1,0:T(8,128)(2,1)}, u32[]{:S(2)}, u32[]{:S(2)}) collective-permute-start(bf16[1,1,48,6144]{3,2,1,0:T(8,128)(2,1)} %bitcast.50), channel_id=1, source_target_pairs={{0,48},{1,49},{2,50},{3,51},{4,52},{5,53},{6,54},{7,55},{8,24},{9,... | collective-permute-start | bytes 1769480 | tf_op jit(solution)/shard_map/ppermute | solution.py:49
  4.3 7.4 %shard_map.68.refs_1_.refs_8_.refs_4_ = f32[384,394]{1,0:T(8,128)} custom-call(s32[1]{0:T(128)} %bitcast.me_ref, bf16[16,48,6144]{2,1,0:T(8,128)(2,1)} %bitcast.12, bf16[16,48,6144]{2,1,0:T(8,128)(2,1)} %bitcast.13, bf16[16,48,6144]{2,1,0:T(8,128)(2,1)} %bitcast.14, bf16[16,48,6144]{2,1,0:T(8,128)(2,1)} %bitcast.15, bf16[16,48,6144]{2,1,0:T(8,128)(2,1)} %bitcast.16, ...), custom_call_target="tpu_custom_call" | custom-call | flops 1048576 | bytes 1048576 | tf_op jit(solution)/shard_map/pallas_call | solution.py:120
  12.6 1.1 fusion.4
  13.8 2.1 %collective-permute-start.4 = (bf16[1,2,48,3072]{3,2,1,0:T(8,128)(2,1)S(1)}, bf16[1,2,48,3072]{3,2,1,0:T(8,128)(2,1)S(1)}, u32[]{:S(2)}, u32[]{:S(2)}) collective-permute-start(bf16[1,2,48,3072]{3,2,1,0:T(8,128)(2,1)S(1)} %pad_maximum_fusion.3.refs_10_), channel_id=1, source_target_pairs={{0,64},{1,65},{2,66},{3,67},{4,68},{5,69},{6,70},{7,71},{8,76},{9,... | collective-permute-start | bytes 1769480 | tf_op jit(solution)/shard_map/ppermute | solution.py:49
  16.8 7.3 %shard_map.70.refs_1_.refs_6_ = f32[384,394]{1,0:T(8,128)} custom-call(s32[1]{0:T(128)} %bitcast.me_ref, bf16[16,48,6144]{2,1,0:T(8,128)(2,1)} %bitcast.27, bf16[16,48,6144]{2,1,0:T(8,128)(2,1)} %bitcast.21, bf16[16,48,6144]{2,1,0:T(8,128)(2,1)} %bitcast.22, bf16[16,48,6144]{2,1,0:T(8,128)(2,1)} %bitcast.23, bf16[16,48,6144]{2,1,0:T(8,128)(2,1)} %bitcast.24, ...), custom_call_target="tpu_custom_call" | custom-call | flops 1048576 | bytes 1048576 | tf_op jit(solution)/shard_map/pallas_call | solution.py:120
  24.9 1.2 pad_maximum_fusion.1.refs_10_
  26.1 1.5 collective-permute-start.5
  27.6 1.3 pad_maximum_fusion.refs_9_
  30.0 7.3 %shard_map.73.refs_1_.refs_9_.refs_5_ = f32[384,394]{1,0:T(8,128)} custom-call(s32[1]{0:T(128)} %bitcast.me_ref, bf16[16,48,6144]{2,1,0:T(8,128)(2,1)} %bitcast.28, bf16[16,48,6144]{2,1,0:T(8,128)(2,1)} %bitcast.29, bf16[16,48,6144]{2,1,0:T(8,128)(2,1)} %bitcast.30, bf16[16,48,6144]{2,1,0:T(8,128)(2,1)} %bitcast.31, bf16[16,48,6144]{2,1,0:T(8,128)(2,1)} %bitcast.32, ...), custom_call_target="tpu_custom_call" | custom-call | flops 1048576 | bytes 1048576 | tf_op jit(solution)/shard_map/pallas_call | solution.py:120
  37.3 5.1 %collective-permute-done.5.refs_0_ = bf16[2,2,48,3072]{3,2,1,0:T(8,128)(2,1)S(1)} collective-permute-done((bf16[2,2,48,3072]{3,2,1,0:T(8,128)(2,1)S(1)}, bf16[2,2,48,3072]{3,2,1,0:T(8,128)(2,1)S(1)}, u32[]{:S(2)}, u32[]{:S(2)}) %collective-permute-start.5) | collective-permute-done | bytes 1179680 | tf_op jit(solution)/shard_map/ppermute | solution.py:49
  42.4 1.0 copy-done.2
  43.4 1.9 %collective-permute-done.2.refs_0_ = bf16[1,4,48,3072]{3,2,1,0:T(8,128)(2,1)} collective-permute-done((bf16[1,4,48,3072]{3,2,1,0:T(8,128)(2,1)S(1)}, bf16[1,4,48,3072]{3,2,1,0:T(8,128)(2,1)}, u32[]{:S(2)}, u32[]{:S(2)}) %collective-permute-start.2) | collective-permute-done | bytes 1179680 | tf_op jit(solution)/shard_map/ppermute | solution.py:49
  45.3 17.2 %shard_map.76 = (f32[384,394]{1,0:T(8,128)}, f32[384,394]{1,0:T(8,128)}, f32[384,394]{1,0:T(8,128)}, f32[384,394]{1,0:T(8,128)}, f32[64,3,384]{2,1,0:T(4,128)}) custom-call(s32[1]{0:T(128)} %bitcast.me_ref, bf16[192,3072]{1,0:T(8,128)(2,1)} %bitcast.45, bf16[192,3072]{1,0:T(8,128)(2,1)} %bitcast.4.refs_1_, bf16[192,3072]{1,0:T(8,128)(2,1)} %bitcast.44, ...), custom_call_target="tpu_custom_call" | custom-call | flops 1048576 | bytes 1048576 | tf_op jit(solution)/shard_map/pallas_call | solution.py:227
  62.6 11.3 %all-to-all-start = ((f32[64,3,384]{2,1,0:T(4,128)}), f32[64,3,384]{2,1,0:T(4,128)S(1)}, u32[]{:S(2)}, u32[]{:S(2)}) async-start(f32[64,3,384]{2,1,0:T(4,128)} %get-tuple-element.26), calls=%async_computation | async-start | bytes 786432 | tf_op jit(solution)/shard_map/all_to_all | solution.py:422
  73.9 0.9 reshape.43.refs_9_
  74.8 7.3 %shard_map.77.refs_7_ = f32[384,394]{1,0:T(8,128)} custom-call(s32[1]{0:T(128)} %bitcast.me_ref, bf16[16,48,6144]{2,1,0:T(8,128)(2,1)} %bitcast.36, bf16[16,48,6144]{2,1,0:T(8,128)(2,1)} %bitcast.37, bf16[16,48,6144]{2,1,0:T(8,128)(2,1)} %bitcast.38, bf16[16,48,6144]{2,1,0:T(8,128)(2,1)} %bitcast.39, bf16[16,48,6144]{2,1,0:T(8,128)(2,1)} %bitcast.40, ...), custom_call_target="tpu_custom_call" | custom-call | flops 1048576 | bytes 1048576 | tf_op jit(solution)/shard_map/pallas_call | solution.py:120
  82.1 2.6 %all-to-all-done.refs_8_ = f32[64,3,384]{2,1,0:T(4,128)S(1)} async-done(((f32[64,3,384]{2,1,0:T(4,128)}), f32[64,3,384]{2,1,0:T(4,128)S(1)}, u32[]{:S(2)}, u32[]{:S(2)}) %all-to-all-start) | async-done | bytes 294944 | tf_op jit(solution)/shard_map/all_to_all | solution.py:422
  85.4 5.4 %shard_map.78 = (bf16[384,394]{1,0:T(8,128)(2,1)}, bf16[384,394]{1,0:T(8,128)(2,1)}, bf16[384,394]{1,0:T(8,128)(2,1)}, bf16[384,394]{1,0:T(8,128)(2,1)}, f32[2,394]{1,0:T(2,128)}) custom-call(s32[1]{0:T(128)} %bitcast.me_ref, f32[384,394]{1,0:T(8,128)} %get-tuple-element.22.refs_0_, f32[384,394]{1,0:T(8,128)} %get-tuple-element.23.refs_1_, ...), custom_call_target="tpu_custom_call" | custom-call | tf_op jit(solution)/shard_map/pallas_call | solution.py:290
  90.8 10.7 %shard_map.79 = (bf16[4,4,2,48,256]{4,3,2,1,0:T(8,128)(2,1)}, bf16[4,2,2,48,256]{4,3,2,1,0:T(8,128)(2,1)}, f32[4,2,2,48,256]{4,3,2,1,0:T(8,128)}, bf16[2,4,2,48,...) custom-call(s32[1]{0:T(128)} %bitcast.me_ref, bf16[384,394]{1,0:T(8,128)(2,1)} %get-tuple-element.27.c0, ...), custom_call_target="tpu_custom_call" | custom-call | flops 1048576 | bytes 1048576 | tf_op jit(solution)/shard_map/pallas_call | solution.py:378
  103.5 10.7 %shard_map.80 = (f32[4,4,2,48,256]{4,3,2,1,0:T(8,128)}, bf16[4,2,2,48,256]{4,3,2,1,0:T(8,128)(2,1)}, f32[4,2,2,48,256]{4,3,2,1,0:T(8,128)}, bf16[2,4,2,48,256]{4,3,2,1,0:T(8,128)(2,1)}, f32[2,4,2,48,256]{4,3,2,1,0:T(8,128)}) custom-call(s32[1]{0:T(128)} %bitcast.me_ref, bf16[384,394]{1,0:T(8,128)(2,1)} %get-tuple-element.27.c0, ...), custom_call_target="tpu_custom_call" | custom-call | flops 1048576 | bytes 1048576 | tf_op jit(solution)/shard_map/pallas_call | solution.py:378
  114.2 1.5 collective-permute-start.10
  115.7 1.2 collective-permute-start.14
  117.1 1.6 %collective-permute-start.12 = (bf16[4,2,2,48,256]{4,3,2,1,0:T(8,128)(2,1)S(1)}, bf16[4,2,2,48,256]{4,3,2,1,0:T(8,128)(2,1)S(1)}, u32[]{:S(2)}, u32[]{:S(2)}) collective-permute-start(bf16[4,2,2,48,256]{4,3,2,1,0:T(8,128)(2,1)S(1)} %add_convert_fusion.1), channel_id=1, source_target_pairs={{0,1},{1,0},{2,3},{3,2},{4,5},{5,4},{6,7},{7,6},{8,11},{9,10},{10,... | collective-permute-start | bytes 1179656 | tf_op jit(solution)/shard_map/ppermute | solution.py:49
  119.7 0.9 collective-permute-start.8
  120.6 1.7 %collective-permute-done.10 = bf16[4,2,2,48,256]{4,3,2,1,0:T(8,128)(2,1)S(1)} collective-permute-done((bf16[4,2,2,48,256]{4,3,2,1,0:T(8,128)(2,1)}, bf16[4,2,2,48,256]{4,3,2,1,0:T(8,128)(2,1)S(1)}, u32[]{:S(2)}, u32[]{:S(2)}) %collective-permute-start.10) | collective-permute-done | bytes 393248 | tf_op jit(solution)/shard_map/ppermute | solution.py:49
  122.3 2.6 %collective-permute-done.12 = bf16[4,2,2,48,256]{4,3,2,1,0:T(8,128)(2,1)S(1)} collective-permute-done((bf16[4,2,2,48,256]{4,3,2,1,0:T(8,128)(2,1)S(1)}, bf16[4,2,2,48,256]{4,3,2,1,0:T(8,128)(2,1)S(1)}, u32[]{:S(2)}, u32[]{:S(2)}) %collective-permute-start.12) | collective-permute-done | bytes 393248 | tf_op jit(solution)/shard_map/ppermute | solution.py:49
  126.0 3.2 %collective-permute-done.16 = bf16[2,4,2,48,256]{4,3,2,1,0:T(8,128)(2,1)S(1)} collective-permute-done((bf16[2,4,2,48,256]{4,3,2,1,0:T(8,128)(2,1)S(1)}, bf16[2,4,2,48,256]{4,3,2,1,0:T(8,128)(2,1)S(1)}, u32[]{:S(2)}, u32[]{:S(2)}) %collective-permute-start.16) | collective-permute-done | bytes 393248 | tf_op jit(solution)/shard_map/ppermute | solution.py:49
  131.8 3.3 %collective-permute-done.17 = bf16[2,2,2,48,256]{4,3,2,1,0:T(8,128)(2,1)S(1)} collective-permute-done((bf16[2,2,2,48,256]{4,3,2,1,0:T(8,128)(2,1)S(1)}, bf16[2,2,2,48,256]{4,3,2,1,0:T(8,128)(2,1)S(1)}, u32[]{:S(2)}, u32[]{:S(2)}) %collective-permute-start.17) | collective-permute-done | bytes 196640 | tf_op jit(solution)/shard_map/ppermute | solution.py:49
  135.2 2.1 %collective-permute-done.9 = bf16[2,2,2,48,256]{4,3,2,1,0:T(8,128)(2,1)S(1)} collective-permute-done((bf16[2,2,2,48,256]{4,3,2,1,0:T(8,128)(2,1)S(1)}, bf16[2,2,2,48,256]{4,3,2,1,0:T(8,128)(2,1)S(1)}, u32[]{:S(2)}, u32[]{:S(2)}) %collective-permute-start.9) | collective-permute-done | bytes 196640 | tf_op jit(solution)/shard_map/ppermute | solution.py:49
  138.1 6.2 %all-to-all-start.1 = ((bf16[8,48,768]{2,1,0:T(8,128)(2,1)}), bf16[8,48,768]{2,1,0:T(8,128)(2,1)S(1)}, u32[]{:S(2)}, u32[]{:S(2)}) async-start(bf16[8,48,768]{2,1,0:T(8,128)(2,1)} %pad_maximum_fusion.4), calls=%async_computation.1 | async-start | bytes 1179648 | tf_op jit(solution)/shard_map/all_to_all | solution.py:453
  144.5 1.1 collective-permute-done.18
  146.2 10.5 %all-to-all-done.1 = bf16[8,48,768]{2,1,0:T(8,128)(2,1)S(1)} async-done(((bf16[8,48,768]{2,1,0:T(8,128)(2,1)}), bf16[8,48,768]{2,1,0:T(8,128)(2,1)S(1)}, u32[]{:S(2)}, u32[]{:S(2)}) %all-to-all-start.1) | async-done | bytes 589856 | tf_op jit(solution)/shard_map/all_to_all | solution.py:453
  (81 shorter events, 14.1 us)
Async XLA Ops:
  0.6 29.1 %collective-permute-start.3 = (bf16[394,6144]{1,0:T(8,128)(2,1)}, bf16[394,6144]{1,0:T(8,128)(2,1)}, u32[]{:S(2)}, u32[]{:S(2)}) collective-permute-start(bf16[394,6144]{1,0:T(8,128)(2,1)} %refs_0_.3), channel_id=1, source_target_pairs={{0,8},{1,9},{2,10},{3,11},{4,12},{5,13},{6,14},{7,15},{8,0},{9,1},... | collective-permute-start | bytes 14524424 | tf_op jit(solution)/shard_map/ppermute | solution.py:49
  0.7 44.6 %collective-permute-start.6 = (bf16[394,6144]{1,0:T(8,128)(2,1)}, bf16[394,6144]{1,0:T(8,128)(2,1)}, u32[]{:S(2)}, u32[]{:S(2)}) collective-permute-start(bf16[394,6144]{1,0:T(8,128)(2,1)} %refs_2_.3), channel_id=1, source_target_pairs={{0,8},{1,9},{2,10},{3,11},{4,12},{5,13},{6,14},{7,15},{8,0},{9,1},... | collective-permute-start | bytes 14524424 | tf_op jit(solution)/shard_map/ppermute | solution.py:49
  1.2 11.4 %collective-permute-start = (bf16[1,1,48,6144]{3,2,1,0:T(8,128)(2,1)}, bf16[1,1,48,6144]{3,2,1,0:T(8,128)(2,1)}, u32[]{:S(2)}, u32[]{:S(2)}) collective-permute-start(bf16[1,1,48,6144]{3,2,1,0:T(8,128)(2,1)} %bitcast.50), channel_id=1, source_target_pairs={{0,48},{1,49},{2,50},{3,51},{4,52},{5,53},{6,54},{7,55},{8,24},{9,... | collective-permute-start | bytes 1769480 | tf_op jit(solution)/shard_map/ppermute | solution.py:49
  4.3 7.4 %copy-start.14 = (bf16[48,6144]{1,0:T(8,128)(2,1)S(1)}, bf16[48,6144]{1,0:T(8,128)(2,1)}, u32[]{:S(2)}) copy-start(bf16[48,6144]{1,0:T(8,128)(2,1)} %param.5) | copy-start | bytes 1769476
  11.8 4.1 %copy-start.3 = (bf16[1,1,48,3072]{3,2,1,0:T(8,128)(2,1)}, bf16[1,1,48,3072]{3,2,1,0:T(8,128)(2,1)S(1)}, u32[]{:S(2)}) copy-start(bf16[1,1,48,3072]{3,2,1,0:T(8,128)(2,1)S(1)} %get-tuple-element.43) | copy-start | bytes 884740
  13.8 2.6 %copy-start.7 = (bf16[1,2,48,3072]{3,2,1,0:T(8,128)(2,1)}, bf16[1,2,48,3072]{3,2,1,0:T(8,128)(2,1)S(1)}, u32[]{:S(2)}) copy-start(bf16[1,2,48,3072]{3,2,1,0:T(8,128)(2,1)S(1)} %pad_maximum_fusion.3.refs_10_) | copy-start | bytes 1769476
  13.8 10.3 %collective-permute-start.4 = (bf16[1,2,48,3072]{3,2,1,0:T(8,128)(2,1)S(1)}, bf16[1,2,48,3072]{3,2,1,0:T(8,128)(2,1)S(1)}, u32[]{:S(2)}, u32[]{:S(2)}) collective-permute-start(bf16[1,2,48,3072]{3,2,1,0:T(8,128)(2,1)S(1)} %pad_maximum_fusion.3.refs_10_), channel_id=1, source_target_pairs={{0,64},{1,65},{2,66},{3,67},{4,68},{5,69},{6,70},{7,71},{8,76},{9,... | collective-permute-start | bytes 1769480 | tf_op jit(solution)/shard_map/ppermute | solution.py:49
  16.0 11.6 %collective-permute-start.1 = (bf16[1,2,48,3072]{3,2,1,0:T(8,128)(2,1)S(1)}, bf16[1,2,48,3072]{3,2,1,0:T(8,128)(2,1)}, u32[]{:S(2)}, u32[]{:S(2)}) collective-permute-start(bf16[1,2,48,3072]{3,2,1,0:T(8,128)(2,1)S(1)} %pad_maximum_fusion.2.refs_9_), channel_id=1, source_target_pairs={{0,16},{1,17},{2,18},{3,19},{4,20},{5,21},{6,22},{7,23},{8,56},{9,... | collective-permute-start | bytes 1769480 | tf_op jit(solution)/shard_map/ppermute | solution.py:49
  26.1 2.8 %copy-start = (bf16[2,2,48,3072]{3,2,1,0:T(8,128)(2,1)}, bf16[2,2,48,3072]{3,2,1,0:T(8,128)(2,1)S(1)}, u32[]{:S(2)}) copy-start(bf16[2,2,48,3072]{3,2,1,0:T(8,128)(2,1)S(1)} %pad_maximum_fusion.1.refs_10_) | copy-start | bytes 3538948
  26.1 16.3 %collective-permute-start.5 = (bf16[2,2,48,3072]{3,2,1,0:T(8,128)(2,1)S(1)}, bf16[2,2,48,3072]{3,2,1,0:T(8,128)(2,1)S(1)}, u32[]{:S(2)}, u32[]{:S(2)}) collective-permute-start(bf16[2,2,48,3072]{3,2,1,0:T(8,128)(2,1)S(1)} %pad_maximum_fusion.1.refs_10_), channel_id=1, source_target_pairs={{0,16},{1,17},{2,18},{3,19},{4,20},{5,21},{6,22},{7,23},{8,56},{9,... | collective-permute-start | bytes 3538952 | tf_op jit(solution)/shard_map/ppermute | solution.py:49
  28.9 16.4 %collective-permute-start.2 = (bf16[1,4,48,3072]{3,2,1,0:T(8,128)(2,1)S(1)}, bf16[1,4,48,3072]{3,2,1,0:T(8,128)(2,1)}, u32[]{:S(2)}, u32[]{:S(2)}) collective-permute-start(bf16[1,4,48,3072]{3,2,1,0:T(8,128)(2,1)S(1)} %pad_maximum_fusion.refs_9_), channel_id=1, source_target_pairs={{0,64},{1,65},{2,66},{3,67},{4,68},{5,69},{6,70},{7,71},{8,76},{9,... | collective-permute-start | bytes 3538952 | tf_op jit(solution)/shard_map/ppermute | solution.py:49
  45.3 28.5 %copy-start.15 = (s32[768]{0:T(1024)S(1)}, s32[768]{0:T(1024)}, u32[]{:S(2)}) copy-start(s32[768]{0:T(1024)} %param.6) | copy-start | bytes 9220
  62.6 22.1 %all-to-all-start = ((f32[64,3,384]{2,1,0:T(4,128)}), f32[64,3,384]{2,1,0:T(4,128)S(1)}, u32[]{:S(2)}, u32[]{:S(2)}) async-start(f32[64,3,384]{2,1,0:T(4,128)} %get-tuple-element.26), calls=%async_computation | async-start | bytes 786432 | tf_op jit(solution)/shard_map/all_to_all | solution.py:422
  101.5 15.5 %collective-permute-start.11 = (bf16[4,2,2,48,256]{4,3,2,1,0:T(8,128)(2,1)}, bf16[4,2,2,48,256]{4,3,2,1,0:T(8,128)(2,1)S(1)}, u32[]{:S(2)}, u32[]{:S(2)}) collective-permute-start(bf16[4,2,2,48,256]{4,3,2,1,0:T(8,128)(2,1)} %get-tuple-element.36), channel_id=1, source_target_pairs={{0,16},{1,17},{2,18},{3,19},{4,20},{5,21},{6,22},{7,23},{8,56},{9,... | collective-permute-start | bytes 1179656 | tf_op jit(solution)/shard_map/ppermute | solution.py:49
  102.2 17.2 %collective-permute-start.7 = (bf16[4,4,2,48,256]{4,3,2,1,0:T(8,128)(2,1)}, bf16[4,4,2,48,256]{4,3,2,1,0:T(8,128)(2,1)S(1)}, u32[]{:S(2)}, u32[]{:S(2)}) collective-permute-start(bf16[4,4,2,48,256]{4,3,2,1,0:T(8,128)(2,1)} %get-tuple-element.31.refs_4_), channel_id=1, source_target_pairs={{0,1},{1,0},{2,3},{3,2},{4,5},{5,4},{6,7},{7,6},{8,11},{9,10},{10,... | collective-permute-start | bytes 2359304 | tf_op jit(solution)/shard_map/ppermute | solution.py:49
  102.7 14.3 %copy-start.11 = (f32[4,2,2,48,256]{4,3,2,1,0:T(8,128)S(1)}, f32[4,2,2,48,256]{4,3,2,1,0:T(8,128)}, u32[]{:S(2)}) copy-start(f32[4,2,2,48,256]{4,3,2,1,0:T(8,128)} %get-tuple-element.35) | copy-start | bytes 2359300
  102.7 16.0 %collective-permute-start.15 = (bf16[2,4,2,48,256]{4,3,2,1,0:T(8,128)(2,1)}, bf16[2,4,2,48,256]{4,3,2,1,0:T(8,128)(2,1)S(1)}, u32[]{:S(2)}, u32[]{:S(2)}) collective-permute-start(bf16[2,4,2,48,256]{4,3,2,1,0:T(8,128)(2,1)} %get-tuple-element.40), channel_id=1, source_target_pairs={{0,64},{1,65},{2,66},{3,67},{4,68},{5,69},{6,70},{7,71},{8,76},{9,... | collective-permute-start | bytes 1179656 | tf_op jit(solution)/shard_map/ppermute | solution.py:49
  114.2 4.5 %copy-start.10 = (f32[2,4,2,48,256]{4,3,2,1,0:T(8,128)S(1)}, f32[2,4,2,48,256]{4,3,2,1,0:T(8,128)}, u32[]{:S(2)}) copy-start(f32[2,4,2,48,256]{4,3,2,1,0:T(8,128)} %get-tuple-element.39) | copy-start | bytes 2359300
  114.2 8.1 %collective-permute-start.10 = (bf16[4,2,2,48,256]{4,3,2,1,0:T(8,128)(2,1)}, bf16[4,2,2,48,256]{4,3,2,1,0:T(8,128)(2,1)S(1)}, u32[]{:S(2)}, u32[]{:S(2)}) collective-permute-start(bf16[4,2,2,48,256]{4,3,2,1,0:T(8,128)(2,1)} %get-tuple-element.34), channel_id=1, source_target_pairs={{0,16},{1,17},{2,18},{3,19},{4,20},{5,21},{6,22},{7,23},{8,56},{9,... | collective-permute-start | bytes 1179656 | tf_op jit(solution)/shard_map/ppermute | solution.py:49
  115.7 10.3 %collective-permute-start.14 = (bf16[2,4,2,48,256]{4,3,2,1,0:T(8,128)(2,1)}, bf16[2,4,2,48,256]{4,3,2,1,0:T(8,128)(2,1)S(1)}, u32[]{:S(2)}, u32[]{:S(2)}) collective-permute-start(bf16[2,4,2,48,256]{4,3,2,1,0:T(8,128)(2,1)} %get-tuple-element.38), channel_id=1, source_target_pairs={{0,64},{1,65},{2,66},{3,67},{4,68},{5,69},{6,70},{7,71},{8,76},{9,... | collective-permute-start | bytes 1179656 | tf_op jit(solution)/shard_map/ppermute | solution.py:49
  117.1 2.3 %copy-start.9 = (f32[4,4,2,48,256]{4,3,2,1,0:T(8,128)S(1)}, f32[4,4,2,48,256]{4,3,2,1,0:T(8,128)}, u32[]{:S(2)}) copy-start(f32[4,4,2,48,256]{4,3,2,1,0:T(8,128)} %get-tuple-element.32) | copy-start | bytes 4718596
  117.1 7.9 %collective-permute-start.12 = (bf16[4,2,2,48,256]{4,3,2,1,0:T(8,128)(2,1)S(1)}, bf16[4,2,2,48,256]{4,3,2,1,0:T(8,128)(2,1)S(1)}, u32[]{:S(2)}, u32[]{:S(2)}) collective-permute-start(bf16[4,2,2,48,256]{4,3,2,1,0:T(8,128)(2,1)S(1)} %add_convert_fusion.1), channel_id=1, source_target_pairs={{0,1},{1,0},{2,3},{3,2},{4,5},{5,4},{6,7},{7,6},{8,11},{9,10},{10,... | collective-permute-start | bytes 1179656 | tf_op jit(solution)/shard_map/ppermute | solution.py:49
  118.8 10.4 %collective-permute-start.16 = (bf16[2,4,2,48,256]{4,3,2,1,0:T(8,128)(2,1)S(1)}, bf16[2,4,2,48,256]{4,3,2,1,0:T(8,128)(2,1)S(1)}, u32[]{:S(2)}, u32[]{:S(2)}) collective-permute-start(bf16[2,4,2,48,256]{4,3,2,1,0:T(8,128)(2,1)S(1)} %add_convert_fusion), channel_id=1, source_target_pairs={{0,1},{1,0},{2,3},{3,2},{4,5},{5,4},{6,7},{7,6},{8,11},{9,10},{10,... | collective-permute-start | bytes 1179656 | tf_op jit(solution)/shard_map/ppermute | solution.py:49
  119.6 5.3 %copy-start.13 = (f32[4,2,2,48,256]{4,3,2,1,0:T(8,128)S(1)}, f32[4,2,2,48,256]{4,3,2,1,0:T(8,128)}, u32[]{:S(2)}) copy-start(f32[4,2,2,48,256]{4,3,2,1,0:T(8,128)} %get-tuple-element.33) | copy-start | bytes 2359300
  119.7 11.2 %collective-permute-start.8 = (bf16[2,4,2,48,256]{4,3,2,1,0:T(8,128)(2,1)S(1)}, bf16[2,4,2,48,256]{4,3,2,1,0:T(8,128)(2,1)S(1)}, u32[]{:S(2)}, u32[]{:S(2)}) collective-permute-start(bf16[2,4,2,48,256]{4,3,2,1,0:T(8,128)(2,1)S(1)} %slice.86), channel_id=1, source_target_pairs={{0,64},{1,65},{2,66},{3,67},{4,68},{5,69},{6,70},{7,71},{8,76},{9,... | collective-permute-start | bytes 1179656 | tf_op jit(solution)/shard_map/ppermute | solution.py:49
  124.9 4.2 %copy-start.12 = (f32[2,4,2,48,256]{4,3,2,1,0:T(8,128)S(1)}, f32[2,4,2,48,256]{4,3,2,1,0:T(8,128)}, u32[]{:S(2)}) copy-start(f32[2,4,2,48,256]{4,3,2,1,0:T(8,128)} %get-tuple-element.37) | copy-start | bytes 2359300
  125.1 5.8 %collective-permute-start.13 = (bf16[2,2,2,48,256]{4,3,2,1,0:T(8,128)(2,1)S(1)}, bf16[2,2,2,48,256]{4,3,2,1,0:T(8,128)(2,1)S(1)}, u32[]{:S(2)}, u32[]{:S(2)}) collective-permute-start(bf16[2,2,2,48,256]{4,3,2,1,0:T(8,128)(2,1)S(1)} %slice.88), channel_id=1, source_target_pairs={{0,64},{1,65},{2,66},{3,67},{4,68},{5,69},{6,70},{7,71},{8,76},{9,... | collective-permute-start | bytes 589832 | tf_op jit(solution)/shard_map/ppermute | solution.py:49
  129.3 5.7 %collective-permute-start.17 = (bf16[2,2,2,48,256]{4,3,2,1,0:T(8,128)(2,1)S(1)}, bf16[2,2,2,48,256]{4,3,2,1,0:T(8,128)(2,1)S(1)}, u32[]{:S(2)}, u32[]{:S(2)}) collective-permute-start(bf16[2,2,2,48,256]{4,3,2,1,0:T(8,128)(2,1)S(1)} %slice.87), channel_id=1, source_target_pairs={{0,16},{1,17},{2,18},{3,19},{4,20},{5,21},{6,22},{7,23},{8,56},{9,... | collective-permute-start | bytes 589832 | tf_op jit(solution)/shard_map/ppermute | solution.py:49
  131.1 6.1 %collective-permute-start.9 = (bf16[2,2,2,48,256]{4,3,2,1,0:T(8,128)(2,1)S(1)}, bf16[2,2,2,48,256]{4,3,2,1,0:T(8,128)(2,1)S(1)}, u32[]{:S(2)}, u32[]{:S(2)}) collective-permute-start(bf16[2,2,2,48,256]{4,3,2,1,0:T(8,128)(2,1)S(1)} %slice.89), channel_id=1, source_target_pairs={{0,16},{1,17},{2,18},{3,19},{4,20},{5,21},{6,22},{7,23},{8,56},{9,... | collective-permute-start | bytes 589832 | tf_op jit(solution)/shard_map/ppermute | solution.py:49
  137.3 7.1 %copy-start.16 = (f32[2,394]{1,0:T(2,128)S(1)}, f32[2,394]{1,0:T(2,128)}, u32[]{:S(2)}) copy-start(f32[2,394]{1,0:T(2,128)} %get-tuple-element.41) | copy-start | bytes 9460
  138.1 18.6 %all-to-all-start.1 = ((bf16[8,48,768]{2,1,0:T(8,128)(2,1)}), bf16[8,48,768]{2,1,0:T(8,128)(2,1)S(1)}, u32[]{:S(2)}, u32[]{:S(2)}) async-start(bf16[8,48,768]{2,1,0:T(8,128)(2,1)} %pad_maximum_fusion.4), calls=%async_computation.1 | async-start | bytes 1179648 | tf_op jit(solution)/shard_map/all_to_all | solution.py:453
  144.4 1.2 collective-permute-start.18
  (6 other events, 6.7 us)

commit v3 on v2

--- a/solution.py
+++ b/solution.py
@@ -15,6 +15,8 @@
 PROBE_BLOCK = 2048
 ROWS = 48
 MIB = 1 << 20
+LIMIT = 60 * MIB
+BACK_LIMIT = 40 * MIB
 NT = (((1,), (1,)), ((), ()))
 
 
@@ -130,7 +132,7 @@
             out_specs=pl.BlockSpec((m, n), lambda s, me: (0, 0)),
         ),
         out_shape=jax.ShapeDtypeStruct((m, n), F32),
-        compiler_params=pltpu.CompilerParams(vmem_limit_bytes=60 * MIB),
+        compiler_params=pltpu.CompilerParams(vmem_limit_bytes=LIMIT),
         cost_estimate=pl.CostEstimate(flops=MIB, bytes_accessed=MIB, transcendentals=0),
     )(me, *([rows] * 8), table, *after)
 
@@ -243,70 +245,76 @@
             ],
         ),
         out_shape=[jax.ShapeDtypeStruct((m, n), F32)] * 4 + [jax.ShapeDtypeStruct((64, 3, m), F32)],
-        compiler_params=pltpu.CompilerParams(vmem_limit_bytes=60 * MIB),
+        compiler_params=pltpu.CompilerParams(vmem_limit_bytes=LIMIT),
         cost_estimate=pl.CostEstimate(flops=MIB, bytes_accessed=MIB, transcendentals=0),
     )(me, *pieces, *tables, *tangents)
 
 
-def coefficients(me, logits, sides, tangents, probes, stats, targets, scale):
-    m, n = logits[0].shape
-
-    def kernel(me_ref, *refs):
-        l_refs, h_refs, t_refs, p_refs = refs[0:2], refs[2:4], refs[4:6], refs[6:8]
-        stats_ref, targets_ref = refs[8:10]
-        c_refs, g_refs, curve_ref, column_ref = refs[10:12], refs[12:14], refs[14], refs[15]
-        here = me_ref[0]
-        tops = stats_ref[:, 0, :]
-        top = jnp.max(tops, axis=0, keepdims=True)
-        factor = jnp.exp(tops - top)
-        total = jnp.sum(stats_ref[:, 1, :] * factor, axis=0, keepdims=True)
-        mean = jnp.sum(stats_ref[:, 2, :] * factor, axis=0, keepdims=True) / total
-        inverse = 1.0 / total
-        line = lax.broadcasted_iota(jnp.int32, (128, m), 0)
-        column_ref[...] = jnp.where(line == 0, top, jnp.where(line == 1, inverse, mean)).T
-        for i in range(2):
-            vocab_start = (here ^ (8 * i)) * n
-            curve_sum = jnp.zeros((1, n), F32)
-            for j in range(8):
-                at = slice(j * ROWS, (j + 1) * ROWS)
-                place = row_place(here, j)
-                values = column_ref[pl.ds(pl.multiple_of(place * ROWS, ROWS), ROWS), :]
-                mine = pl.multiple_of(owner(here, j) * ROWS, ROWS)
-                wanted = targets_ref[pl.ds(mine, ROWS), :]
-                side = h_refs[i][at, :] * scale
-                tangent = t_refs[i][at, :] + side
-                probability = jnp.exp(l_refs[i][at, :] - values[:, 0:1]) * values[:, 1:2]
-                curve = probability * (tangent - values[:, 2:3])
-                column = lax.broadcasted_iota(jnp.int32, (ROWS, n), 1) + vocab_start
-                gradient = probability - jnp.where(wanted == column, 1.0, 0.0)
-                c_refs[i][at, :] = curve.astype(BF16)
-                g_refs[i][at, :] = gradient.astype(BF16)
-                curve_sum += jnp.sum(
-                    curve * side + gradient * (p_refs[i][at, :] * scale), axis=0, keepdims=True
-                )
-            curve_ref[i : i + 1, :] = curve_sum
-
-    vmem = pl.BlockSpec(memory_space=pltpu.VMEM)
-    return pl.pallas_call(
-        kernel,
-        in_specs=[pl.BlockSpec(memory_space=pltpu.SMEM)] + [vmem] * 10,
-        out_specs=[vmem] * 5,
-        out_shape=[jax.ShapeDtypeStruct((m, n), BF16)] * 4 + [jax.ShapeDtypeStruct((2, n), F32)],
-        scratch_shapes=[pltpu.VMEM((m, 128), F32)],
-        compiler_params=pltpu.CompilerParams(vmem_limit_bytes=60 * MIB),
-    )(me, *logits, *sides, *tangents, *probes, stats, targets)
-
-
-def back(me, curves, gradients, tables, probes, root, turn, after=()):
-    m, n = curves[0].shape
+def coefficients(here, loads, arrays, stats_ref, targets_ref, c_refs, g_refs, curve_ref, column_ref, scale):
+    m, n = c_refs[0].shape
+    tops = stats_ref[:, 0, :]
+    top = jnp.max(tops, axis=0, keepdims=True)
+    factor = jnp.exp(tops - top)
+    total = jnp.sum(stats_ref[:, 1, :] * factor, axis=0, keepdims=True)
+    mean = jnp.sum(stats_ref[:, 2, :] * factor, axis=0, keepdims=True) / total
+    inverse = 1.0 / total
+    line = lax.broadcasted_iota(jnp.int32, (128, m), 0)
+    column_ref[...] = jnp.where(line == 0, top, jnp.where(line == 1, inverse, mean)).T
+    for i in range(2):
+        for load in loads[i::2]:
+            load.wait()
+        vocab_start = (here ^ (8 * i)) * n
+        curve_sum = jnp.zeros((1, n), F32)
+        for j in range(8):
+            at = slice(j * ROWS, (j + 1) * ROWS)
+            place = row_place(here, j)
+            values = column_ref[pl.ds(pl.multiple_of(place * ROWS, ROWS), ROWS), :]
+            mine = pl.multiple_of(owner(here, j) * ROWS, ROWS)
+            wanted = targets_ref[pl.ds(mine, ROWS), :]
+            side = arrays[2 + i, at, :] * scale
+            tangent = arrays[4 + i, at, :] + side
+            probability = jnp.exp(arrays[i, at, :] - values[:, 0:1]) * values[:, 1:2]
+            curve = probability * (tangent - values[:, 2:3])
+            column = lax.broadcasted_iota(jnp.int32, (ROWS, n), 1) + vocab_start
+            gradient = probability - jnp.where(wanted == column, 1.0, 0.0)
+            c_refs[i][at, :] = curve.astype(BF16)
+            g_refs[i][at, :] = gradient.astype(BF16)
+            curve_sum += jnp.sum(
+                curve * side + gradient * (arrays[6 + i, at, :] * scale), axis=0, keepdims=True
+            )
+        curve_ref[i : i + 1, :] = curve_sum
+
+
+def back(me, tables, root, turn, factors=(), arrays=(), stats=None, targets=None, scale=1.0, after=()):
+    m, n = 8 * ROWS, tables[0].shape[0]
     width = 768
     part = width // 3
     steps = 4
-
-    def kernel(me_ref, c0, c1, g0, g1, *refs):
-        table_refs, outs, (held, sems) = refs[0:4], refs[4 + len(after) : 9 + len(after)], refs[-2:]
+    made = turn == 0
+
+    def kernel(me_ref, *refs):
+        refs = list(refs)
+
+        def take(length):
+            taken = refs[:length]
+            del refs[:length]
+            return taken
+
+        factor_refs = take(len(factors))
+        table_refs = take(4)
+        array_refs = take(len(arrays))
+        if made:
+            stats_ref, targets_ref = take(2)
+        take(len(after))
+        outs = take(5)
+        if made:
+            factor_refs = take(4)
+            (curve_ref,) = take(1)
+        held, sems = take(2)
         step = pl.program_id(0)
-        zl, y, c, zh, x = decode(me_ref[0])
+        here = me_ref[0]
+        zl, y, c, zh, x = decode(here)
+        c0, c1, g0, g1 = factor_refs
 
         def copies(at):
             slot = 2 * (1 - turn) + (at >> 1)
@@ -321,16 +329,40 @@
 
         @pl.when(step == 0)
         def _():
+            if made:
+                array_ref, array_sems, column_ref = refs
+                loads = [
+                    pltpu.make_async_copy(array_refs[i], array_ref.at[i], array_sems.at[i]) for i in range(8)
+                ]
+                for i in (0, 2, 4, 6, 1, 3, 5, 7):
+                    loads[i].start()
             for copy in copies(0):
                 copy.start()
+            if made:
+                for copy in copies(1):
+                    copy.start()
+                coefficients(
+                    here,
+                    loads,
+                    array_ref,
+                    stats_ref,
+                    targets_ref,
+                    factor_refs[:2],
+                    factor_refs[2:],
+                    curve_ref,
+                    column_ref,
+                    scale,
+                )
 
         for copy in copies(step):
             copy.wait()
 
-        @pl.when(step == 0)
-        def _():
-            for copy in copies(1):
-                copy.start()
+        if not made:
+
+            @pl.when(step == 0)
+            def _():
+                for copy in copies(1):
+                    copy.start()
 
         @pl.when(step < steps - 2)
         def _():
@@ -372,23 +404,39 @@
                     outs[4][zs, ys, 0] = total[at, 2 * part :]
 
     shapes, specs = [], []
-    for z, y, dtype in ((4, 4, F32 if turn else BF16), (4, 2, BF16), (4, 2, F32), (2, 4, BF16), (2, 4, F32)):
+    for z, y, dtype in ((4, 4, BF16 if made else F32), (4, 2, BF16), (4, 2, F32), (2, 4, BF16), (2, 4, F32)):
         shapes.append(jax.ShapeDtypeStruct((z, y, 2, ROWS, part), dtype))
         specs.append(pl.BlockSpec((z, y, 1, ROWS, part), lambda s, me: (0, 0, s >> 1, 0, 0)))
+    whole = pl.BlockSpec((m, n), lambda s, me: (0, 0))
+    anywhere = pl.BlockSpec(memory_space=pl.ANY)
+    inputs = [me, *factors, *tables, *arrays]
+    in_specs = (
+        [whole] * len(factors)
+        + [pl.BlockSpec(memory_space=pltpu.HBM)] * (4 + len(arrays))
+    )
+    scratch = [pltpu.VMEM((steps, 4, n, width), BF16), pltpu.SemaphoreType.DMA((steps, 4))]
+    if made:
+        inputs += [stats, targets]
+        in_specs += [
+            pl.BlockSpec(stats.shape, lambda s, me: (0, 0, 0)),
+            pl.BlockSpec(targets.shape, lambda s, me: (0, 0)),
+        ]
+        shapes += [jax.ShapeDtypeStruct((m, n), BF16)] * 4 + [jax.ShapeDtypeStruct((2, n), F32)]
+        specs += [whole] * 4 + [pl.BlockSpec((2, n), lambda s, me: (0, 0))]
+        scratch += [pltpu.VMEM((8, m, n), F32), pltpu.SemaphoreType.DMA((8,)), pltpu.VMEM((m, 128), F32)]
     return pl.pallas_call(
         kernel,
         grid_spec=pltpu.PrefetchScalarGridSpec(
             num_scalar_prefetch=1,
             grid=(steps,),
-            in_specs=[pl.BlockSpec((m, n), lambda s, me: (0, 0))] * 4
-            + [pl.BlockSpec(memory_space=pl.ANY)] * (4 + len(after)),
+            in_specs=in_specs + [anywhere] * len(after),
             out_specs=specs,
-            scratch_shapes=[pltpu.VMEM((steps, 4, n, width), BF16), pltpu.SemaphoreType.DMA((steps, 4))],
+            scratch_shapes=scratch,
         ),
         out_shape=shapes,
-        compiler_params=pltpu.CompilerParams(vmem_limit_bytes=60 * MIB),
+        compiler_params=pltpu.CompilerParams(vmem_limit_bytes=BACK_LIMIT),
         cost_estimate=pl.CostEstimate(flops=MIB, bytes_accessed=MIB, transcendentals=0),
-    )(me, *curves, *gradients, *tables, *probes, *after)
+    )(*inputs, *after)
 
 
 def body(hidden, targets, hidden_probe, table, table_probe):
@@ -427,14 +475,20 @@
         axis_index_groups=groups_of_core(),
         tiled=True,
     )
-    c0, c1, g0, g1, curve = coefficients(
-        me, (l0, l1), (h0, h1), (t0, t1), (p0, p1), stats, targets.reshape(token_count, 1), scale
+    tables = (table, table_other, table_probe, probe_other)
+    x_send, *early = back(
+        me,
+        tables,
+        root,
+        0,
+        arrays=(l0, l1, h0, h1, t0, t1, p0, p1),
+        stats=stats,
+        targets=targets.reshape(token_count, 1),
+        scale=scale,
     )
+    *early, curve = early
+    x_keep, *late = back(me, tables, root, 1, factors=early[4:], after=(x_send,))
     curvature = (curve[0] + swap(curve[1], "c")) * (vocab_total / token_count)
-
-    operands = (me, (c0, c1), (g0, g1), (table, table_other), (table_probe, probe_other), root)
-    x_send, *early = back(*operands, 0)
-    x_keep, *late = back(*operands, 1, after=(x_send,))
 
     def wide(a):
         return a.astype(F32)
@@ -444,9 +498,10 @@
         send = lax.slice_in_dim(keep, 2, 4, axis=k).astype(BF16)
         return lax.slice_in_dim(keep, 0, 2, axis=k) + wide(swap(send, axis))
 
-    summed = [halve(halve(x_keep + wide(swap(x_send, "x")), "z"), "y")]
-    for i, (axis, last) in enumerate((("y", "z"), ("z", "y"))):
-        send = early[2 * i + 1] + wide(swap(early[2 * i], axis))
+    x_got, y_got, z_got = swap(x_send, "x"), swap(early[0], "y"), swap(early[2], "z")
+    summed = [halve(halve(x_keep + wide(x_got), "z"), "y")]
+    for i, (axis, last, got) in enumerate((("y", "z", y_got), ("z", "y", z_got))):
+        send = early[2 * i + 1] + wide(got)
         keep = late[2 * i + 1] + wide(swap(late[2 * i], axis))
         summed.append(halve(keep + wide(swap(send.astype(BF16), "x")), last))
     total = jnp.concatenate(summed, axis=-1).astype(BF16).reshape(8, ROWS, width // 8)

time: 158 us -> 153 us (0.968)
  Pallas kernels: 73.4 us -> 63.8 us
  local copies, waits for them, and re-layouts: 5.47 us -> 10 us
    pallas_call x1 -> x0, Pallas kernels: 5.39 us -> none  [coefficients(): pl.pallas_call(kernel, in_specs=[pl.BlockSpec(memory_space=pltpu.SMEM)] +...]
    unnamed x34 -> x40, local copies, waits for them, and re-layouts: 3.3 us -> 8.62 us
    pallas_call x2, Pallas kernels: 21.4 us -> 17 us  [back(): pl.pallas_call(kernel, grid_spec=pltpu.PrefetchScalarGridSpec(num_scalar_...]
where the time goes in v3:
time: 153 us; the launch traced here: 152 us
  Pallas kernels  63.8 us (42%)
  waiting for transfers between devices  36.4 us (24%)
  starting transfers between devices  35.4 us (23%)
  local copies, waits for them, and re-layouts  10 us (7%)
  other arithmetic  5.75 us (4%)
    pallas_call x4, Pallas kernels, probe_products(): pl.pallas_call(kernel, grid_spec=pltpu.PrefetchScalarGridSpec(num_scalar_...  29.6 us
    ppermute x19, waiting for transfers between devices, swap(): return lax.ppermute(a, AXES, pairs(axis, kind))  22.7 us
    ppermute x19, starting transfers between devices, swap(): return lax.ppermute(a, AXES, pairs(axis, kind))  18.5 us
    pallas_call x1, Pallas kernels, hidden_products(): pl.pallas_call(kernel, grid_spec=pltpu.PrefetchScalarGridSpec(num_scalar_...  17.2 us
    pallas_call x2, Pallas kernels, back(): pl.pallas_call(kernel, grid_spec=pltpu.PrefetchScalarGridSpec(num_scalar_...  17 us
    all_to_all x1, starting transfers between devices, body(): lax.all_to_all(stats, AXES, 0, 0, axis_index_groups=groups_of_core(), til...  11.3 us
    all_to_all x1, waiting for transfers between devices, body(): lax.all_to_all(total, AXES, 0, 0, axis_index_groups=groups_of_eight(), ti...  10.5 us
    unnamed x40, local copies, waits for them, and re-layouts  8.62 us
  transfers between devices with their start and end apart: 21, of which 12 were waited for; matrix products, arithmetic and copies ran while one was open for 4% of the time, Pallas kernels for 25%

profile of v3, /device:TPU:0, one launch (start us, length us, event | category | flops | bytes accessed | tf_op | source)
XLA Modules:
  0.0 152.3 jit_solution(8347214782447899265)
XLA Ops:
  1.2 3.1 %collective-permute-start.2 = (bf16[1,1,48,6144]{3,2,1,0:T(8,128)(2,1)}, bf16[1,1,48,6144]{3,2,1,0:T(8,128)(2,1)}, u32[]{:S(2)}, u32[]{:S(2)}) collective-permute-start(bf16[1,1,48,6144]{3,2,1,0:T(8,128)(2,1)} %bitcast.52), channel_id=1, source_target_pairs={{0,48},{1,49},{2,50},{3,51},{4,52},{5,53},{6,54},{7,55},{8,24},{9,... | collective-permute-start | bytes 1769480 | tf_op jit(solution)/shard_map/ppermute | solution.py:51
  4.3 7.5 %shard_map.68.refs_1_.refs_8_ = f32[384,394]{1,0:T(8,128)} custom-call(s32[1]{0:T(128)} %bitcast.me_ref, bf16[16,48,6144]{2,1,0:T(8,128)(2,1)} %bitcast.14, bf16[16,48,6144]{2,1,0:T(8,128)(2,1)} %bitcast.15, bf16[16,48,6144]{2,1,0:T(8,128)(2,1)} %bitcast.16, bf16[16,48,6144]{2,1,0:T(8,128)(2,1)} %bitcast.17, bf16[16,48,6144]{2,1,0:T(8,128)(2,1)} %bitcast.18, ...), custom_call_target="tpu_custom_call" | custom-call | flops 1048576 | bytes 1048576 | tf_op jit(solution)/shard_map/pallas_call | solution.py:122
  13.8 2.1 %collective-permute-start.5 = (bf16[1,2,48,3072]{3,2,1,0:T(8,128)(2,1)S(1)}, bf16[1,2,48,3072]{3,2,1,0:T(8,128)(2,1)S(1)}, u32[]{:S(2)}, u32[]{:S(2)}) collective-permute-start(bf16[1,2,48,3072]{3,2,1,0:T(8,128)(2,1)S(1)} %pad_maximum_fusion.3.refs_10_), channel_id=1, source_target_pairs={{0,64},{1,65},{2,66},{3,67},{4,68},{5,69},{6,70},{7,71},{8,76},{9,... | collective-permute-start | bytes 1769480 | tf_op jit(solution)/shard_map/ppermute | solution.py:51
  16.8 7.3 %shard_map.70.refs_1_.refs_10_ = f32[384,394]{1,0:T(8,128)} custom-call(s32[1]{0:T(128)} %bitcast.me_ref, bf16[16,48,6144]{2,1,0:T(8,128)(2,1)} %bitcast.29, bf16[16,48,6144]{2,1,0:T(8,128)(2,1)} %bitcast.23, bf16[16,48,6144]{2,1,0:T(8,128)(2,1)} %bitcast.24, bf16[16,48,6144]{2,1,0:T(8,128)(2,1)} %bitcast.25, bf16[16,48,6144]{2,1,0:T(8,128)(2,1)} %bitcast.26, ...), custom_call_target="tpu_custom_call" | custom-call | flops 1048576 | bytes 1048576 | tf_op jit(solution)/shard_map/pallas_call | solution.py:122
  25.0 1.2 pad_maximum_fusion.1.refs_10_
  26.2 1.4 collective-permute-start.6
  27.6 1.3 pad_maximum_fusion.refs_9_
  30.0 7.3 %shard_map.73.refs_1_.refs_9_ = f32[384,394]{1,0:T(8,128)} custom-call(s32[1]{0:T(128)} %bitcast.me_ref, bf16[16,48,6144]{2,1,0:T(8,128)(2,1)} %bitcast.30, bf16[16,48,6144]{2,1,0:T(8,128)(2,1)} %bitcast.31, bf16[16,48,6144]{2,1,0:T(8,128)(2,1)} %bitcast.32, bf16[16,48,6144]{2,1,0:T(8,128)(2,1)} %bitcast.33, bf16[16,48,6144]{2,1,0:T(8,128)(2,1)} %bitcast.34, ...), custom_call_target="tpu_custom_call" | custom-call | flops 1048576 | bytes 1048576 | tf_op jit(solution)/shard_map/pallas_call | solution.py:122
  37.3 5.1 %collective-permute-done.6.refs_0_ = bf16[2,2,48,3072]{3,2,1,0:T(8,128)(2,1)S(1)} collective-permute-done((bf16[2,2,48,3072]{3,2,1,0:T(8,128)(2,1)S(1)}, bf16[2,2,48,3072]{3,2,1,0:T(8,128)(2,1)S(1)}, u32[]{:S(2)}, u32[]{:S(2)}) %collective-permute-start.6) | collective-permute-done | bytes 1179680 | tf_op jit(solution)/shard_map/ppermute | solution.py:51
  43.5 1.9 %collective-permute-done.4.refs_0_ = bf16[1,4,48,3072]{3,2,1,0:T(8,128)(2,1)} collective-permute-done((bf16[1,4,48,3072]{3,2,1,0:T(8,128)(2,1)S(1)}, bf16[1,4,48,3072]{3,2,1,0:T(8,128)(2,1)}, u32[]{:S(2)}, u32[]{:S(2)}) %collective-permute-start.4) | collective-permute-done | bytes 1179680 | tf_op jit(solution)/shard_map/ppermute | solution.py:51
  45.4 17.2 %shard_map.76 = (f32[384,394]{1,0:T(8,128)}, f32[384,394]{1,0:T(8,128)}, f32[384,394]{1,0:T(8,128)}, f32[384,394]{1,0:T(8,128)}, f32[64,3,384]{2,1,0:T(4,128)}) custom-call(s32[1]{0:T(128)} %bitcast.me_ref, bf16[192,3072]{1,0:T(8,128)(2,1)} %bitcast.47, bf16[192,3072]{1,0:T(8,128)(2,1)} %bitcast.4.refs_1_, bf16[192,3072]{1,0:T(8,128)(2,1)} %bitcast.46, ...), custom_call_target="tpu_custom_call" | custom-call | flops 1048576 | bytes 1048576 | tf_op jit(solution)/shard_map/pallas_call | solution.py:229
  62.6 11.3 %all-to-all-start = ((f32[64,3,384]{2,1,0:T(4,128)}), f32[64,3,384]{2,1,0:T(4,128)S(1)}, u32[]{:S(2)}, u32[]{:S(2)}) async-start(f32[64,3,384]{2,1,0:T(4,128)} %get-tuple-element.26), calls=%async_computation | async-start | bytes 786432 | tf_op jit(solution)/shard_map/all_to_all | solution.py:470
  74.0 7.5 %shard_map.77.refs_11_ = f32[384,394]{1,0:T(8,128)} custom-call(s32[1]{0:T(128)} %bitcast.me_ref, bf16[16,48,6144]{2,1,0:T(8,128)(2,1)} %bitcast.38, bf16[16,48,6144]{2,1,0:T(8,128)(2,1)} %bitcast.39, bf16[16,48,6144]{2,1,0:T(8,128)(2,1)} %bitcast.40, bf16[16,48,6144]{2,1,0:T(8,128)(2,1)} %bitcast.41, bf16[16,48,6144]{2,1,0:T(8,128)(2,1)} %bitcast.42, ...), custom_call_target="tpu_custom_call" | custom-call | flops 1048576 | bytes 1048576 | tf_op jit(solution)/shard_map/pallas_call | solution.py:122
  81.6 3.1 %all-to-all-done.refs_12_ = f32[64,3,384]{2,1,0:T(4,128)S(1)} async-done(((f32[64,3,384]{2,1,0:T(4,128)}), f32[64,3,384]{2,1,0:T(4,128)S(1)}, u32[]{:S(2)}, u32[]{:S(2)}) %all-to-all-start) | async-done | bytes 294944 | tf_op jit(solution)/shard_map/all_to_all | solution.py:470
  84.7 1.3 copy-done.3
  86.0 1.3 copy-done.4
  87.3 1.1 copy-done.5
  88.4 1.1 copy-done.6
  89.6 1.1 copy-done.7
  90.7 8.7 %shard_map.78 = (bf16[4,4,2,48,256]{4,3,2,1,0:T(8,128)(2,1)S(1)}, bf16[4,2,2,48,256]{4,3,2,1,0:T(8,128)(2,1)S(1)}, f32[4,2,2,48,256]{4,3,2,1,0:T(8,128)S(1)}, bf...) custom-call(s32[1]{0:T(128)} %bitcast.me_ref, ...), custom_call_target="tpu_custom_call" | custom-call | flops 1048576 | bytes 1048576 | tf_op jit(solution)/shard_map/pallas_call | solution.py:427
  101.4 8.3 %shard_map.79 = (f32[4,4,2,48,256]{4,3,2,1,0:T(8,128)S(1)}, bf16[4,2,2,48,256]{4,3,2,1,0:T(8,128)(2,1)S(1)}, f32[4,2,2,48,256]{4,3,2,1,0:T(8,128)S(1)}, bf16[2,4...) custom-call(s32[1]{0:T(128)} %bitcast.me_ref, bf16[384,394]{1,0:T(8,128)(2,1)S(1)} %get-tuple-element.27.refs_0_, ...), custom_call_target="tpu_custom_call" | custom-call | flops 1048576 | bytes 1048576 | tf_op jit(solution)/shard_map/pallas_call | solution.py:427
  109.7 1.5 collective-permute-start.10
  111.2 1.2 collective-permute-start.14
  112.6 1.6 %collective-permute-start.12 = (bf16[4,2,2,48,256]{4,3,2,1,0:T(8,128)(2,1)S(1)}, bf16[4,2,2,48,256]{4,3,2,1,0:T(8,128)(2,1)S(1)}, u32[]{:S(2)}, u32[]{:S(2)}) collective-permute-start(bf16[4,2,2,48,256]{4,3,2,1,0:T(8,128)(2,1)S(1)} %add_convert_fusion.1), channel_id=1, source_target_pairs={{0,1},{1,0},{2,3},{3,2},{4,5},{5,4},{6,7},{7,6},{8,11},{9,10},{10,... | collective-permute-start | bytes 1179656 | tf_op jit(solution)/shard_map/ppermute | solution.py:51
  116.1 1.5 collective-permute-done.10
  117.6 2.9 %collective-permute-done.12 = bf16[4,2,2,48,256]{4,3,2,1,0:T(8,128)(2,1)S(1)} collective-permute-done((bf16[4,2,2,48,256]{4,3,2,1,0:T(8,128)(2,1)S(1)}, bf16[4,2,2,48,256]{4,3,2,1,0:T(8,128)(2,1)S(1)}, u32[]{:S(2)}, u32[]{:S(2)}) %collective-permute-start.12) | collective-permute-done | bytes 393248 | tf_op jit(solution)/shard_map/ppermute | solution.py:51
  121.5 3.2 %collective-permute-done.16 = bf16[2,4,2,48,256]{4,3,2,1,0:T(8,128)(2,1)S(1)} collective-permute-done((bf16[2,4,2,48,256]{4,3,2,1,0:T(8,128)(2,1)S(1)}, bf16[2,4,2,48,256]{4,3,2,1,0:T(8,128)(2,1)S(1)}, u32[]{:S(2)}, u32[]{:S(2)}) %collective-permute-start.16) | collective-permute-done | bytes 393248 | tf_op jit(solution)/shard_map/ppermute | solution.py:51
  127.2 3.3 %collective-permute-done.17 = bf16[2,2,2,48,256]{4,3,2,1,0:T(8,128)(2,1)S(1)} collective-permute-done((bf16[2,2,2,48,256]{4,3,2,1,0:T(8,128)(2,1)S(1)}, bf16[2,2,2,48,256]{4,3,2,1,0:T(8,128)(2,1)S(1)}, u32[]{:S(2)}, u32[]{:S(2)}) %collective-permute-start.17) | collective-permute-done | bytes 196640 | tf_op jit(solution)/shard_map/ppermute | solution.py:51
  130.6 2.1 %collective-permute-done.9 = bf16[2,2,2,48,256]{4,3,2,1,0:T(8,128)(2,1)S(1)} collective-permute-done((bf16[2,2,2,48,256]{4,3,2,1,0:T(8,128)(2,1)S(1)}, bf16[2,2,2,48,256]{4,3,2,1,0:T(8,128)(2,1)S(1)}, u32[]{:S(2)}, u32[]{:S(2)}) %collective-permute-start.9) | collective-permute-done | bytes 196640 | tf_op jit(solution)/shard_map/ppermute | solution.py:51
  133.6 5.7 %all-to-all-start.1 = ((bf16[8,48,768]{2,1,0:T(8,128)(2,1)}), bf16[8,48,768]{2,1,0:T(8,128)(2,1)S(1)}, u32[]{:S(2)}, u32[]{:S(2)}) async-start(bf16[8,48,768]{2,1,0:T(8,128)(2,1)} %pad_maximum_fusion.4), calls=%async_computation.1 | async-start | bytes 1179648 | tf_op jit(solution)/shard_map/all_to_all | solution.py:508
  139.3 1.1 collective-permute-done.18
  141.1 10.5 %all-to-all-done.1 = bf16[8,48,768]{2,1,0:T(8,128)(2,1)S(1)} async-done(((bf16[8,48,768]{2,1,0:T(8,128)(2,1)}), bf16[8,48,768]{2,1,0:T(8,128)(2,1)S(1)}, u32[]{:S(2)}, u32[]{:S(2)}) %all-to-all-start.1) | async-done | bytes 589856 | tf_op jit(solution)/shard_map/all_to_all | solution.py:508
  (87 shorter events, 16.5 us)
Async XLA Ops:
  0.6 29.1 %collective-permute-start = (bf16[394,6144]{1,0:T(8,128)(2,1)}, bf16[394,6144]{1,0:T(8,128)(2,1)}, u32[]{:S(2)}, u32[]{:S(2)}) collective-permute-start(bf16[394,6144]{1,0:T(8,128)(2,1)} %refs_4_.3), channel_id=1, source_target_pairs={{0,8},{1,9},{2,10},{3,11},{4,12},{5,13},{6,14},{7,15},{8,0},{9,1},... | collective-permute-start | bytes 14524424 | tf_op jit(solution)/shard_map/ppermute | solution.py:51
  0.7 44.6 %collective-permute-start.1 = (bf16[394,6144]{1,0:T(8,128)(2,1)}, bf16[394,6144]{1,0:T(8,128)(2,1)}, u32[]{:S(2)}, u32[]{:S(2)}) collective-permute-start(bf16[394,6144]{1,0:T(8,128)(2,1)} %refs_6_.3), channel_id=1, source_target_pairs={{0,8},{1,9},{2,10},{3,11},{4,12},{5,13},{6,14},{7,15},{8,0},{9,1},... | collective-permute-start | bytes 14524424 | tf_op jit(solution)/shard_map/ppermute | solution.py:51
  1.2 11.4 %collective-permute-start.2 = (bf16[1,1,48,6144]{3,2,1,0:T(8,128)(2,1)}, bf16[1,1,48,6144]{3,2,1,0:T(8,128)(2,1)}, u32[]{:S(2)}, u32[]{:S(2)}) collective-permute-start(bf16[1,1,48,6144]{3,2,1,0:T(8,128)(2,1)} %bitcast.52), channel_id=1, source_target_pairs={{0,48},{1,49},{2,50},{3,51},{4,52},{5,53},{6,54},{7,55},{8,24},{9,... | collective-permute-start | bytes 1769480 | tf_op jit(solution)/shard_map/ppermute | solution.py:51
  4.3 7.5 %copy-start.16 = (bf16[48,6144]{1,0:T(8,128)(2,1)S(1)}, bf16[48,6144]{1,0:T(8,128)(2,1)}, u32[]{:S(2)}) copy-start(bf16[48,6144]{1,0:T(8,128)(2,1)} %param.5) | copy-start | bytes 1769476
  11.8 4.1 %copy-start.11 = (bf16[1,1,48,3072]{3,2,1,0:T(8,128)(2,1)}, bf16[1,1,48,3072]{3,2,1,0:T(8,128)(2,1)S(1)}, u32[]{:S(2)}) copy-start(bf16[1,1,48,3072]{3,2,1,0:T(8,128)(2,1)S(1)} %get-tuple-element.43) | copy-start | bytes 884740
  13.7 2.2 %copy-start.12 = (bf16[1,1,48,3072]{3,2,1,0:T(8,128)(2,1)}, bf16[1,1,48,3072]{3,2,1,0:T(8,128)(2,1)S(1)}, u32[]{:S(2)}) copy-start(bf16[1,1,48,3072]{3,2,1,0:T(8,128)(2,1)S(1)} %get-tuple-element.45) | copy-start | bytes 884740
  13.8 2.6 %copy-start.15 = (bf16[1,2,48,3072]{3,2,1,0:T(8,128)(2,1)}, bf16[1,2,48,3072]{3,2,1,0:T(8,128)(2,1)S(1)}, u32[]{:S(2)}) copy-start(bf16[1,2,48,3072]{3,2,1,0:T(8,128)(2,1)S(1)} %pad_maximum_fusion.3.refs_10_) | copy-start | bytes 1769476
  13.8 10.3 %collective-permute-start.5 = (bf16[1,2,48,3072]{3,2,1,0:T(8,128)(2,1)S(1)}, bf16[1,2,48,3072]{3,2,1,0:T(8,128)(2,1)S(1)}, u32[]{:S(2)}, u32[]{:S(2)}) collective-permute-start(bf16[1,2,48,3072]{3,2,1,0:T(8,128)(2,1)S(1)} %pad_maximum_fusion.3.refs_10_), channel_id=1, source_target_pairs={{0,64},{1,65},{2,66},{3,67},{4,68},{5,69},{6,70},{7,71},{8,76},{9,... | collective-permute-start | bytes 1769480 | tf_op jit(solution)/shard_map/ppermute | solution.py:51
  16.0 11.6 %collective-permute-start.3 = (bf16[1,2,48,3072]{3,2,1,0:T(8,128)(2,1)S(1)}, bf16[1,2,48,3072]{3,2,1,0:T(8,128)(2,1)}, u32[]{:S(2)}, u32[]{:S(2)}) collective-permute-start(bf16[1,2,48,3072]{3,2,1,0:T(8,128)(2,1)S(1)} %pad_maximum_fusion.2.refs_9_), channel_id=1, source_target_pairs={{0,16},{1,17},{2,18},{3,19},{4,20},{5,21},{6,22},{7,23},{8,56},{9,... | collective-permute-start | bytes 1769480 | tf_op jit(solution)/shard_map/ppermute | solution.py:51
  26.1 2.8 %copy-start.8 = (bf16[2,2,48,3072]{3,2,1,0:T(8,128)(2,1)}, bf16[2,2,48,3072]{3,2,1,0:T(8,128)(2,1)S(1)}, u32[]{:S(2)}) copy-start(bf16[2,2,48,3072]{3,2,1,0:T(8,128)(2,1)S(1)} %pad_maximum_fusion.1.refs_10_) | copy-start | bytes 3538948
  26.2 16.3 %collective-permute-start.6 = (bf16[2,2,48,3072]{3,2,1,0:T(8,128)(2,1)S(1)}, bf16[2,2,48,3072]{3,2,1,0:T(8,128)(2,1)S(1)}, u32[]{:S(2)}, u32[]{:S(2)}) collective-permute-start(bf16[2,2,48,3072]{3,2,1,0:T(8,128)(2,1)S(1)} %pad_maximum_fusion.1.refs_10_), channel_id=1, source_target_pairs={{0,16},{1,17},{2,18},{3,19},{4,20},{5,21},{6,22},{7,23},{8,56},{9,... | collective-permute-start | bytes 3538952 | tf_op jit(solution)/shard_map/ppermute | solution.py:51
  29.0 16.4 %collective-permute-start.4 = (bf16[1,4,48,3072]{3,2,1,0:T(8,128)(2,1)S(1)}, bf16[1,4,48,3072]{3,2,1,0:T(8,128)(2,1)}, u32[]{:S(2)}, u32[]{:S(2)}) collective-permute-start(bf16[1,4,48,3072]{3,2,1,0:T(8,128)(2,1)S(1)} %pad_maximum_fusion.refs_9_), channel_id=1, source_target_pairs={{0,64},{1,65},{2,66},{3,67},{4,68},{5,69},{6,70},{7,71},{8,76},{9,... | collective-permute-start | bytes 3538952 | tf_op jit(solution)/shard_map/ppermute | solution.py:51
  45.4 28.5 %copy-start.17 = (s32[768]{0:T(1024)S(1)}, s32[768]{0:T(1024)}, u32[]{:S(2)}) copy-start(s32[768]{0:T(1024)} %param.6) | copy-start | bytes 9220
  62.6 22.1 %all-to-all-start = ((f32[64,3,384]{2,1,0:T(4,128)}), f32[64,3,384]{2,1,0:T(4,128)S(1)}, u32[]{:S(2)}, u32[]{:S(2)}) async-start(f32[64,3,384]{2,1,0:T(4,128)} %get-tuple-element.26), calls=%async_computation | async-start | bytes 786432 | tf_op jit(solution)/shard_map/all_to_all | solution.py:470
  74.0 10.7 %copy-start = (f32[384,394]{1,0:T(8,128)S(1)}, f32[384,394]{1,0:T(8,128)}, u32[]{:S(2)}) copy-start(f32[384,394]{1,0:T(8,128)} %shard_map.73.refs_1_.refs_9_) | copy-start | bytes 1815556
  74.0 10.7 %copy-start.1 = (f32[384,394]{1,0:T(8,128)S(1)}, f32[384,394]{1,0:T(8,128)}, u32[]{:S(2)}) copy-start(f32[384,394]{1,0:T(8,128)} %shard_map.68.refs_1_.refs_8_) | copy-start | bytes 1815556
  74.0 10.6 %copy-start.2 = (f32[384,394]{1,0:T(8,128)S(1)}, f32[384,394]{1,0:T(8,128)}, u32[]{:S(2)}) copy-start(f32[384,394]{1,0:T(8,128)} %shard_map.70.refs_1_.refs_10_) | copy-start | bytes 1815556
  84.7 16.8 %slice-start = ((s8[4915200]{0:T(1024)(128)(4,1)}), s8[4194304]{0:T(1024)(128)(4,1)S(1)}, s32[]{:S(2)}) async-start(s8[4915200]{0:T(1024)(128)(4,1)} %bitcast.12), calls=%async_computation.2 | async-start | bytes 8388608
  90.7 10.7 %slice-start.1 = ((s8[4915200]{0:T(1024)(128)(4,1)}), s8[720896]{0:T(1024)(128)(4,1)S(1)}, s32[]{:S(2)}) async-start(s8[4915200]{0:T(1024)(128)(4,1)} %bitcast.12), calls=%async_computation.3 | async-start | bytes 1441792
  99.4 13.0 %collective-permute-start.11 = (bf16[4,2,2,48,256]{4,3,2,1,0:T(8,128)(2,1)S(1)}, bf16[4,2,2,48,256]{4,3,2,1,0:T(8,128)(2,1)S(1)}, u32[]{:S(2)}, u32[]{:S(2)}) collective-permute-start(bf16[4,2,2,48,256]{4,3,2,1,0:T(8,128)(2,1)S(1)} %get-tuple-element.36), channel_id=1, source_target_pairs={{0,16},{1,17},{2,18},{3,19},{4,20},{5,21},{6,22},{7,23},{8,56},{9,... | collective-permute-start | bytes 1179656 | tf_op jit(solution)/shard_map/ppermute | solution.py:51
  100.1 14.7 %collective-permute-start.7 = (bf16[4,4,2,48,256]{4,3,2,1,0:T(8,128)(2,1)S(1)}, bf16[4,4,2,48,256]{4,3,2,1,0:T(8,128)(2,1)S(1)}, u32[]{:S(2)}, u32[]{:S(2)}) collective-permute-start(bf16[4,4,2,48,256]{4,3,2,1,0:T(8,128)(2,1)S(1)} %get-tuple-element.31.refs_8_), channel_id=1, source_target_pairs={{0,1},{1,0},{2,3},{3,2},{4,5},{5,4},{6,7},{7,6},{8,11},{9,10},{10,... | collective-permute-start | bytes 2359304 | tf_op jit(solution)/shard_map/ppermute | solution.py:51
  100.6 13.5 %collective-permute-start.15 = (bf16[2,4,2,48,256]{4,3,2,1,0:T(8,128)(2,1)S(1)}, bf16[2,4,2,48,256]{4,3,2,1,0:T(8,128)(2,1)S(1)}, u32[]{:S(2)}, u32[]{:S(2)}) collective-permute-start(bf16[2,4,2,48,256]{4,3,2,1,0:T(8,128)(2,1)S(1)} %get-tuple-element.40), channel_id=1, source_target_pairs={{0,64},{1,65},{2,66},{3,67},{4,68},{5,69},{6,70},{7,71},{8,76},{9,... | collective-permute-start | bytes 1179656 | tf_op jit(solution)/shard_map/ppermute | solution.py:51
  109.7 7.9 %collective-permute-start.10 = (bf16[4,2,2,48,256]{4,3,2,1,0:T(8,128)(2,1)S(1)}, bf16[4,2,2,48,256]{4,3,2,1,0:T(8,128)(2,1)S(1)}, u32[]{:S(2)}, u32[]{:S(2)}) collective-permute-start(bf16[4,2,2,48,256]{4,3,2,1,0:T(8,128)(2,1)S(1)} %get-tuple-element.34), channel_id=1, source_target_pairs={{0,16},{1,17},{2,18},{3,19},{4,20},{5,21},{6,22},{7,23},{8,56},{9,... | collective-permute-start | bytes 1179656 | tf_op jit(solution)/shard_map/ppermute | solution.py:51
  111.2 10.3 %collective-permute-start.14 = (bf16[2,4,2,48,256]{4,3,2,1,0:T(8,128)(2,1)S(1)}, bf16[2,4,2,48,256]{4,3,2,1,0:T(8,128)(2,1)S(1)}, u32[]{:S(2)}, u32[]{:S(2)}) collective-permute-start(bf16[2,4,2,48,256]{4,3,2,1,0:T(8,128)(2,1)S(1)} %get-tuple-element.38), channel_id=1, source_target_pairs={{0,64},{1,65},{2,66},{3,67},{4,68},{5,69},{6,70},{7,71},{8,76},{9,... | collective-permute-start | bytes 1179656 | tf_op jit(solution)/shard_map/ppermute | solution.py:51
  112.6 7.9 %collective-permute-start.12 = (bf16[4,2,2,48,256]{4,3,2,1,0:T(8,128)(2,1)S(1)}, bf16[4,2,2,48,256]{4,3,2,1,0:T(8,128)(2,1)S(1)}, u32[]{:S(2)}, u32[]{:S(2)}) collective-permute-start(bf16[4,2,2,48,256]{4,3,2,1,0:T(8,128)(2,1)S(1)} %add_convert_fusion.1), channel_id=1, source_target_pairs={{0,1},{1,0},{2,3},{3,2},{4,5},{5,4},{6,7},{7,6},{8,11},{9,10},{10,... | collective-permute-start | bytes 1179656 | tf_op jit(solution)/shard_map/ppermute | solution.py:51
  114.3 10.3 %collective-permute-start.16 = (bf16[2,4,2,48,256]{4,3,2,1,0:T(8,128)(2,1)S(1)}, bf16[2,4,2,48,256]{4,3,2,1,0:T(8,128)(2,1)S(1)}, u32[]{:S(2)}, u32[]{:S(2)}) collective-permute-start(bf16[2,4,2,48,256]{4,3,2,1,0:T(8,128)(2,1)S(1)} %add_convert_fusion), channel_id=1, source_target_pairs={{0,1},{1,0},{2,3},{3,2},{4,5},{5,4},{6,7},{7,6},{8,11},{9,10},{10,... | collective-permute-start | bytes 1179656 | tf_op jit(solution)/shard_map/ppermute | solution.py:51
  115.2 11.2 %collective-permute-start.8 = (bf16[2,4,2,48,256]{4,3,2,1,0:T(8,128)(2,1)S(1)}, bf16[2,4,2,48,256]{4,3,2,1,0:T(8,128)(2,1)S(1)}, u32[]{:S(2)}, u32[]{:S(2)}) collective-permute-start(bf16[2,4,2,48,256]{4,3,2,1,0:T(8,128)(2,1)S(1)} %slice.86), channel_id=1, source_target_pairs={{0,64},{1,65},{2,66},{3,67},{4,68},{5,69},{6,70},{7,71},{8,76},{9,... | collective-permute-start | bytes 1179656 | tf_op jit(solution)/shard_map/ppermute | solution.py:51
  120.6 5.8 %collective-permute-start.13 = (bf16[2,2,2,48,256]{4,3,2,1,0:T(8,128)(2,1)S(1)}, bf16[2,2,2,48,256]{4,3,2,1,0:T(8,128)(2,1)S(1)}, u32[]{:S(2)}, u32[]{:S(2)}) collective-permute-start(bf16[2,2,2,48,256]{4,3,2,1,0:T(8,128)(2,1)S(1)} %slice.88), channel_id=1, source_target_pairs={{0,64},{1,65},{2,66},{3,67},{4,68},{5,69},{6,70},{7,71},{8,76},{9,... | collective-permute-start | bytes 589832 | tf_op jit(solution)/shard_map/ppermute | solution.py:51
  124.8 5.7 %collective-permute-start.17 = (bf16[2,2,2,48,256]{4,3,2,1,0:T(8,128)(2,1)S(1)}, bf16[2,2,2,48,256]{4,3,2,1,0:T(8,128)(2,1)S(1)}, u32[]{:S(2)}, u32[]{:S(2)}) collective-permute-start(bf16[2,2,2,48,256]{4,3,2,1,0:T(8,128)(2,1)S(1)} %slice.87), channel_id=1, source_target_pairs={{0,16},{1,17},{2,18},{3,19},{4,20},{5,21},{6,22},{7,23},{8,56},{9,... | collective-permute-start | bytes 589832 | tf_op jit(solution)/shard_map/ppermute | solution.py:51
  126.5 6.1 %collective-permute-start.9 = (bf16[2,2,2,48,256]{4,3,2,1,0:T(8,128)(2,1)S(1)}, bf16[2,2,2,48,256]{4,3,2,1,0:T(8,128)(2,1)S(1)}, u32[]{:S(2)}, u32[]{:S(2)}) collective-permute-start(bf16[2,2,2,48,256]{4,3,2,1,0:T(8,128)(2,1)S(1)} %slice.89), channel_id=1, source_target_pairs={{0,16},{1,17},{2,18},{3,19},{4,20},{5,21},{6,22},{7,23},{8,56},{9,... | collective-permute-start | bytes 589832 | tf_op jit(solution)/shard_map/ppermute | solution.py:51
  133.6 18.0 %all-to-all-start.1 = ((bf16[8,48,768]{2,1,0:T(8,128)(2,1)}), bf16[8,48,768]{2,1,0:T(8,128)(2,1)S(1)}, u32[]{:S(2)}, u32[]{:S(2)}) async-start(bf16[8,48,768]{2,1,0:T(8,128)(2,1)} %pad_maximum_fusion.4), calls=%async_computation.1 | async-start | bytes 1179648 | tf_op jit(solution)/shard_map/all_to_all | solution.py:508
  139.2 1.2 collective-permute-start.18
  (9 other events, 9.8 us)

commit v4 on v3

--- a/solution.py
+++ b/solution.py
@@ -16,7 +16,7 @@
 ROWS = 48
 MIB = 1 << 20
 LIMIT = 60 * MIB
-BACK_LIMIT = 40 * MIB
+BACK_LIMITS = (46 * MIB, 40 * MIB)
 NT = (((1,), (1,)), ((), ()))
 
 
@@ -434,7 +434,7 @@
             scratch_shapes=scratch,
         ),
         out_shape=shapes,
-        compiler_params=pltpu.CompilerParams(vmem_limit_bytes=BACK_LIMIT),
+        compiler_params=pltpu.CompilerParams(vmem_limit_bytes=BACK_LIMITS[turn]),
         cost_estimate=pl.CostEstimate(flops=MIB, bytes_accessed=MIB, transcendentals=0),
     )(*inputs, *after)
 

time: 153 us -> 149 us (0.974)
  local copies, waits for them, and re-layouts: 10 us -> 3.99 us
  Pallas kernels: 63.8 us -> 66 us
    unnamed x40 -> x30, local copies, waits for them, and re-layouts: 8.62 us -> 2.59 us
    pallas_call x2, Pallas kernels: 17 us -> 19.2 us  [back(): pl.pallas_call(kernel, grid_spec=pltpu.PrefetchScalarGridSpec(num_scalar_...]
  transfers between devices with their start and end apart: 21 -> 21, of which waited for: 12 -> 12; matrix products, arithmetic and copies ran while one was open for 4% -> 4% of each run, Pallas kernels for 25% -> 26%
where the time goes in v4:
time: 149 us
  Pallas kernels  66 us (44%)
  waiting for transfers between devices  36.4 us (24%)
  starting transfers between devices  35.4 us (24%)
  other arithmetic  5.7 us (4%)
  local copies, waits for them, and re-layouts  3.99 us (3%)
    pallas_call x4, Pallas kernels, probe_products(): pl.pallas_call(kernel, grid_spec=pltpu.PrefetchScalarGridSpec(num_scalar_...  29.6 us
    ppermute x19, waiting for transfers between devices, swap(): return lax.ppermute(a, AXES, pairs(axis, kind))  22.8 us
    pallas_call x2, Pallas kernels, back(): pl.pallas_call(kernel, grid_spec=pltpu.PrefetchScalarGridSpec(num_scalar_...  19.2 us
    ppermute x19, starting transfers between devices, swap(): return lax.ppermute(a, AXES, pairs(axis, kind))  18.5 us
    pallas_call x1, Pallas kernels, hidden_products(): pl.pallas_call(kernel, grid_spec=pltpu.PrefetchScalarGridSpec(num_scalar_...  17.3 us
    all_to_all x1, starting transfers between devices, body(): lax.all_to_all(stats, AXES, 0, 0, axis_index_groups=groups_of_core(), til...  11.3 us
    all_to_all x1, waiting for transfers between devices, body(): lax.all_to_all(total, AXES, 0, 0, axis_index_groups=groups_of_eight(), ti...  10.5 us
    all_to_all x1, starting transfers between devices, body(): lax.all_to_all(total, AXES, 0, 0, axis_index_groups=groups_of_eight(), ti...  5.69 us
  transfers between devices with their start and end apart: 21, of which 12 were waited for; matrix products, arithmetic and copies ran while one was open for 4% of the time, Pallas kernels for 26%

profile of v4, /device:TPU:0, one launch (start us, length us, event | category | flops | bytes accessed | tf_op | source)
XLA Modules:
  0.0 148.5 jit_solution(17895274839288775277)
XLA Ops:
  1.2 3.1 %collective-permute-start.2 = (bf16[1,1,48,6144]{3,2,1,0:T(8,128)(2,1)}, bf16[1,1,48,6144]{3,2,1,0:T(8,128)(2,1)}, u32[]{:S(2)}, u32[]{:S(2)}) collective-permute-start(bf16[1,1,48,6144]{3,2,1,0:T(8,128)(2,1)} %bitcast.52), channel_id=1, source_target_pairs={{0,48},{1,49},{2,50},{3,51},{4,52},{5,53},{6,54},{7,55},{8,24},{9,... | collective-permute-start | bytes 1769480 | tf_op jit(solution)/shard_map/ppermute | solution.py:51
  4.3 7.4 %shard_map.68.refs_1_.refs_8_ = f32[384,394]{1,0:T(8,128)} custom-call(s32[1]{0:T(128)} %bitcast.me_ref, bf16[16,48,6144]{2,1,0:T(8,128)(2,1)} %bitcast.14, bf16[16,48,6144]{2,1,0:T(8,128)(2,1)} %bitcast.15, bf16[16,48,6144]{2,1,0:T(8,128)(2,1)} %bitcast.16, bf16[16,48,6144]{2,1,0:T(8,128)(2,1)} %bitcast.17, bf16[16,48,6144]{2,1,0:T(8,128)(2,1)} %bitcast.18, ...), custom_call_target="tpu_custom_call" | custom-call | flops 1048576 | bytes 1048576 | tf_op jit(solution)/shard_map/pallas_call | solution.py:122
  12.6 1.1 fusion.4
  13.8 2.1 %collective-permute-start.5 = (bf16[1,2,48,3072]{3,2,1,0:T(8,128)(2,1)S(1)}, bf16[1,2,48,3072]{3,2,1,0:T(8,128)(2,1)S(1)}, u32[]{:S(2)}, u32[]{:S(2)}) collective-permute-start(bf16[1,2,48,3072]{3,2,1,0:T(8,128)(2,1)S(1)} %pad_maximum_fusion.3.refs_10_), channel_id=1, source_target_pairs={{0,64},{1,65},{2,66},{3,67},{4,68},{5,69},{6,70},{7,71},{8,76},{9,... | collective-permute-start | bytes 1769480 | tf_op jit(solution)/shard_map/ppermute | solution.py:51
  16.8 7.3 %shard_map.70.refs_1_.refs_10_ = f32[384,394]{1,0:T(8,128)} custom-call(s32[1]{0:T(128)} %bitcast.me_ref, bf16[16,48,6144]{2,1,0:T(8,128)(2,1)} %bitcast.29, bf16[16,48,6144]{2,1,0:T(8,128)(2,1)} %bitcast.23, bf16[16,48,6144]{2,1,0:T(8,128)(2,1)} %bitcast.24, bf16[16,48,6144]{2,1,0:T(8,128)(2,1)} %bitcast.25, bf16[16,48,6144]{2,1,0:T(8,128)(2,1)} %bitcast.26, ...), custom_call_target="tpu_custom_call" | custom-call | flops 1048576 | bytes 1048576 | tf_op jit(solution)/shard_map/pallas_call | solution.py:122
  25.0 1.2 pad_maximum_fusion.1.refs_10_
  26.2 1.4 collective-permute-start.6
  27.6 1.3 pad_maximum_fusion.refs_9_
  30.0 7.3 %shard_map.73.refs_1_.refs_9_ = f32[384,394]{1,0:T(8,128)} custom-call(s32[1]{0:T(128)} %bitcast.me_ref, bf16[16,48,6144]{2,1,0:T(8,128)(2,1)} %bitcast.30, bf16[16,48,6144]{2,1,0:T(8,128)(2,1)} %bitcast.31, bf16[16,48,6144]{2,1,0:T(8,128)(2,1)} %bitcast.32, bf16[16,48,6144]{2,1,0:T(8,128)(2,1)} %bitcast.33, bf16[16,48,6144]{2,1,0:T(8,128)(2,1)} %bitcast.34, ...), custom_call_target="tpu_custom_call" | custom-call | flops 1048576 | bytes 1048576 | tf_op jit(solution)/shard_map/pallas_call | solution.py:122
  37.3 5.1 %collective-permute-done.6.refs_0_ = bf16[2,2,48,3072]{3,2,1,0:T(8,128)(2,1)S(1)} collective-permute-done((bf16[2,2,48,3072]{3,2,1,0:T(8,128)(2,1)S(1)}, bf16[2,2,48,3072]{3,2,1,0:T(8,128)(2,1)S(1)}, u32[]{:S(2)}, u32[]{:S(2)}) %collective-permute-start.6) | collective-permute-done | bytes 1179680 | tf_op jit(solution)/shard_map/ppermute | solution.py:51
  42.5 1.0 copy-done.5
  43.5 1.9 %collective-permute-done.4.refs_0_ = bf16[1,4,48,3072]{3,2,1,0:T(8,128)(2,1)} collective-permute-done((bf16[1,4,48,3072]{3,2,1,0:T(8,128)(2,1)S(1)}, bf16[1,4,48,3072]{3,2,1,0:T(8,128)(2,1)}, u32[]{:S(2)}, u32[]{:S(2)}) %collective-permute-start.4) | collective-permute-done | bytes 1179680 | tf_op jit(solution)/shard_map/ppermute | solution.py:51
  45.4 17.3 %shard_map.76 = (f32[384,394]{1,0:T(8,128)}, f32[384,394]{1,0:T(8,128)}, f32[384,394]{1,0:T(8,128)}, f32[384,394]{1,0:T(8,128)}, f32[64,3,384]{2,1,0:T(4,128)}) custom-call(s32[1]{0:T(128)} %bitcast.me_ref, bf16[192,3072]{1,0:T(8,128)(2,1)} %bitcast.47, bf16[192,3072]{1,0:T(8,128)(2,1)} %bitcast.4.refs_1_, bf16[192,3072]{1,0:T(8,128)(2,1)} %bitcast.46, ...), custom_call_target="tpu_custom_call" | custom-call | flops 1048576 | bytes 1048576 | tf_op jit(solution)/shard_map/pallas_call | solution.py:229
  62.6 11.3 %all-to-all-start = ((f32[64,3,384]{2,1,0:T(4,128)}), f32[64,3,384]{2,1,0:T(4,128)S(1)}, u32[]{:S(2)}, u32[]{:S(2)}) async-start(f32[64,3,384]{2,1,0:T(4,128)} %get-tuple-element.26), calls=%async_computation | async-start | bytes 786432 | tf_op jit(solution)/shard_map/all_to_all | solution.py:470
  74.1 7.5 %shard_map.77.refs_11_ = f32[384,394]{1,0:T(8,128)} custom-call(s32[1]{0:T(128)} %bitcast.me_ref, bf16[16,48,6144]{2,1,0:T(8,128)(2,1)} %bitcast.38, bf16[16,48,6144]{2,1,0:T(8,128)(2,1)} %bitcast.39, bf16[16,48,6144]{2,1,0:T(8,128)(2,1)} %bitcast.40, bf16[16,48,6144]{2,1,0:T(8,128)(2,1)} %bitcast.41, bf16[16,48,6144]{2,1,0:T(8,128)(2,1)} %bitcast.42, ...), custom_call_target="tpu_custom_call" | custom-call | flops 1048576 | bytes 1048576 | tf_op jit(solution)/shard_map/pallas_call | solution.py:122
  81.6 3.1 %all-to-all-done.refs_12_ = f32[64,3,384]{2,1,0:T(4,128)S(1)} async-done(((f32[64,3,384]{2,1,0:T(4,128)}), f32[64,3,384]{2,1,0:T(4,128)S(1)}, u32[]{:S(2)}, u32[]{:S(2)}) %all-to-all-start) | async-done | bytes 294944 | tf_op jit(solution)/shard_map/all_to_all | solution.py:470
  84.8 10.9 %shard_map.78 = (bf16[4,4,2,48,256]{4,3,2,1,0:T(8,128)(2,1)S(1)}, bf16[4,2,2,48,256]{4,3,2,1,0:T(8,128)(2,1)S(1)}, f32[4,2,2,48,256]{4,3,2,1,0:T(8,128)S(1)}, bf...) custom-call(s32[1]{0:T(128)} %bitcast.me_ref, ...), custom_call_target="tpu_custom_call" | custom-call | flops 1048576 | bytes 1048576 | tf_op jit(solution)/shard_map/pallas_call | solution.py:427
  97.7 8.3 %shard_map.79 = (f32[4,4,2,48,256]{4,3,2,1,0:T(8,128)S(1)}, bf16[4,2,2,48,256]{4,3,2,1,0:T(8,128)(2,1)S(1)}, f32[4,2,2,48,256]{4,3,2,1,0:T(8,128)S(1)}, bf16[2,4...) custom-call(s32[1]{0:T(128)} %bitcast.me_ref, bf16[384,394]{1,0:T(8,128)(2,1)S(1)} %get-tuple-element.27.refs_0_, ...), custom_call_target="tpu_custom_call" | custom-call | flops 1048576 | bytes 1048576 | tf_op jit(solution)/shard_map/pallas_call | solution.py:427
  105.9 1.5 collective-permute-start.10
  107.4 1.2 collective-permute-start.14
  108.8 1.6 %collective-permute-start.12 = (bf16[4,2,2,48,256]{4,3,2,1,0:T(8,128)(2,1)S(1)}, bf16[4,2,2,48,256]{4,3,2,1,0:T(8,128)(2,1)S(1)}, u32[]{:S(2)}, u32[]{:S(2)}) collective-permute-start(bf16[4,2,2,48,256]{4,3,2,1,0:T(8,128)(2,1)S(1)} %add_convert_fusion.1), channel_id=1, source_target_pairs={{0,1},{1,0},{2,3},{3,2},{4,5},{5,4},{6,7},{7,6},{8,11},{9,10},{10,... | collective-permute-start | bytes 1179656 | tf_op jit(solution)/shard_map/ppermute | solution.py:51
  111.3 0.9 collective-permute-start.8
  112.2 1.6 %collective-permute-done.10 = bf16[4,2,2,48,256]{4,3,2,1,0:T(8,128)(2,1)S(1)} collective-permute-done((bf16[4,2,2,48,256]{4,3,2,1,0:T(8,128)(2,1)S(1)}, bf16[4,2,2,48,256]{4,3,2,1,0:T(8,128)(2,1)S(1)}, u32[]{:S(2)}, u32[]{:S(2)}) %collective-permute-start.10) | collective-permute-done | bytes 393248 | tf_op jit(solution)/shard_map/ppermute | solution.py:51
  113.8 2.8 %collective-permute-done.12 = bf16[4,2,2,48,256]{4,3,2,1,0:T(8,128)(2,1)S(1)} collective-permute-done((bf16[4,2,2,48,256]{4,3,2,1,0:T(8,128)(2,1)S(1)}, bf16[4,2,2,48,256]{4,3,2,1,0:T(8,128)(2,1)S(1)}, u32[]{:S(2)}, u32[]{:S(2)}) %collective-permute-start.12) | collective-permute-done | bytes 393248 | tf_op jit(solution)/shard_map/ppermute | solution.py:51
  116.8 0.9 collective-permute-start.13
  117.6 3.2 %collective-permute-done.16 = bf16[2,4,2,48,256]{4,3,2,1,0:T(8,128)(2,1)S(1)} collective-permute-done((bf16[2,4,2,48,256]{4,3,2,1,0:T(8,128)(2,1)S(1)}, bf16[2,4,2,48,256]{4,3,2,1,0:T(8,128)(2,1)S(1)}, u32[]{:S(2)}, u32[]{:S(2)}) %collective-permute-start.16) | collective-permute-done | bytes 393248 | tf_op jit(solution)/shard_map/ppermute | solution.py:51
  123.4 3.3 %collective-permute-done.17 = bf16[2,2,2,48,256]{4,3,2,1,0:T(8,128)(2,1)S(1)} collective-permute-done((bf16[2,2,2,48,256]{4,3,2,1,0:T(8,128)(2,1)S(1)}, bf16[2,2,2,48,256]{4,3,2,1,0:T(8,128)(2,1)S(1)}, u32[]{:S(2)}, u32[]{:S(2)}) %collective-permute-start.17) | collective-permute-done | bytes 196640 | tf_op jit(solution)/shard_map/ppermute | solution.py:51
  126.8 2.1 %collective-permute-done.9 = bf16[2,2,2,48,256]{4,3,2,1,0:T(8,128)(2,1)S(1)} collective-permute-done((bf16[2,2,2,48,256]{4,3,2,1,0:T(8,128)(2,1)S(1)}, bf16[2,2,2,48,256]{4,3,2,1,0:T(8,128)(2,1)S(1)}, u32[]{:S(2)}, u32[]{:S(2)}) %collective-permute-start.9) | collective-permute-done | bytes 196640 | tf_op jit(solution)/shard_map/ppermute | solution.py:51
  128.9 0.9 pad_maximum_fusion.4
  129.8 5.7 %all-to-all-start.1 = ((bf16[8,48,768]{2,1,0:T(8,128)(2,1)}), bf16[8,48,768]{2,1,0:T(8,128)(2,1)S(1)}, u32[]{:S(2)}, u32[]{:S(2)}) async-start(bf16[8,48,768]{2,1,0:T(8,128)(2,1)} %pad_maximum_fusion.4), calls=%async_computation.1 | async-start | bytes 1179648 | tf_op jit(solution)/shard_map/all_to_all | solution.py:508
  135.5 1.1 collective-permute-done.18
  137.3 10.5 %all-to-all-done.1 = bf16[8,48,768]{2,1,0:T(8,128)(2,1)S(1)} async-done(((bf16[8,48,768]{2,1,0:T(8,128)(2,1)}), bf16[8,48,768]{2,1,0:T(8,128)(2,1)S(1)}, u32[]{:S(2)}, u32[]{:S(2)}) %all-to-all-start.1) | async-done | bytes 589856 | tf_op jit(solution)/shard_map/all_to_all | solution.py:508
  (77 shorter events, 11.7 us)
Async XLA Ops:
  0.6 29.1 %collective-permute-start = (bf16[394,6144]{1,0:T(8,128)(2,1)}, bf16[394,6144]{1,0:T(8,128)(2,1)}, u32[]{:S(2)}, u32[]{:S(2)}) collective-permute-start(bf16[394,6144]{1,0:T(8,128)(2,1)} %refs_4_.3), channel_id=1, source_target_pairs={{0,8},{1,9},{2,10},{3,11},{4,12},{5,13},{6,14},{7,15},{8,0},{9,1},... | collective-permute-start | bytes 14524424 | tf_op jit(solution)/shard_map/ppermute | solution.py:51
  0.7 44.6 %collective-permute-start.1 = (bf16[394,6144]{1,0:T(8,128)(2,1)}, bf16[394,6144]{1,0:T(8,128)(2,1)}, u32[]{:S(2)}, u32[]{:S(2)}) collective-permute-start(bf16[394,6144]{1,0:T(8,128)(2,1)} %refs_6_.3), channel_id=1, source_target_pairs={{0,8},{1,9},{2,10},{3,11},{4,12},{5,13},{6,14},{7,15},{8,0},{9,1},... | collective-permute-start | bytes 14524424 | tf_op jit(solution)/shard_map/ppermute | solution.py:51
  1.2 11.4 %collective-permute-start.2 = (bf16[1,1,48,6144]{3,2,1,0:T(8,128)(2,1)}, bf16[1,1,48,6144]{3,2,1,0:T(8,128)(2,1)}, u32[]{:S(2)}, u32[]{:S(2)}) collective-permute-start(bf16[1,1,48,6144]{3,2,1,0:T(8,128)(2,1)} %bitcast.52), channel_id=1, source_target_pairs={{0,48},{1,49},{2,50},{3,51},{4,52},{5,53},{6,54},{7,55},{8,24},{9,... | collective-permute-start | bytes 1769480 | tf_op jit(solution)/shard_map/ppermute | solution.py:51
  4.3 7.4 %copy-start.11 = (bf16[48,6144]{1,0:T(8,128)(2,1)S(1)}, bf16[48,6144]{1,0:T(8,128)(2,1)}, u32[]{:S(2)}) copy-start(bf16[48,6144]{1,0:T(8,128)(2,1)} %param.5) | copy-start | bytes 1769476
  11.8 4.1 %copy-start.6 = (bf16[1,1,48,3072]{3,2,1,0:T(8,128)(2,1)}, bf16[1,1,48,3072]{3,2,1,0:T(8,128)(2,1)S(1)}, u32[]{:S(2)}) copy-start(bf16[1,1,48,3072]{3,2,1,0:T(8,128)(2,1)S(1)} %get-tuple-element.43) | copy-start | bytes 884740
  13.7 2.2 %copy-start.7 = (bf16[1,1,48,3072]{3,2,1,0:T(8,128)(2,1)}, bf16[1,1,48,3072]{3,2,1,0:T(8,128)(2,1)S(1)}, u32[]{:S(2)}) copy-start(bf16[1,1,48,3072]{3,2,1,0:T(8,128)(2,1)S(1)} %get-tuple-element.45) | copy-start | bytes 884740
  13.8 2.6 %copy-start.10 = (bf16[1,2,48,3072]{3,2,1,0:T(8,128)(2,1)}, bf16[1,2,48,3072]{3,2,1,0:T(8,128)(2,1)S(1)}, u32[]{:S(2)}) copy-start(bf16[1,2,48,3072]{3,2,1,0:T(8,128)(2,1)S(1)} %pad_maximum_fusion.3.refs_10_) | copy-start | bytes 1769476
  13.8 10.3 %collective-permute-start.5 = (bf16[1,2,48,3072]{3,2,1,0:T(8,128)(2,1)S(1)}, bf16[1,2,48,3072]{3,2,1,0:T(8,128)(2,1)S(1)}, u32[]{:S(2)}, u32[]{:S(2)}) collective-permute-start(bf16[1,2,48,3072]{3,2,1,0:T(8,128)(2,1)S(1)} %pad_maximum_fusion.3.refs_10_), channel_id=1, source_target_pairs={{0,64},{1,65},{2,66},{3,67},{4,68},{5,69},{6,70},{7,71},{8,76},{9,... | collective-permute-start | bytes 1769480 | tf_op jit(solution)/shard_map/ppermute | solution.py:51
  16.0 11.6 %collective-permute-start.3 = (bf16[1,2,48,3072]{3,2,1,0:T(8,128)(2,1)S(1)}, bf16[1,2,48,3072]{3,2,1,0:T(8,128)(2,1)}, u32[]{:S(2)}, u32[]{:S(2)}) collective-permute-start(bf16[1,2,48,3072]{3,2,1,0:T(8,128)(2,1)S(1)} %pad_maximum_fusion.2.refs_9_), channel_id=1, source_target_pairs={{0,16},{1,17},{2,18},{3,19},{4,20},{5,21},{6,22},{7,23},{8,56},{9,... | collective-permute-start | bytes 1769480 | tf_op jit(solution)/shard_map/ppermute | solution.py:51
  26.2 2.8 %copy-start.3 = (bf16[2,2,48,3072]{3,2,1,0:T(8,128)(2,1)}, bf16[2,2,48,3072]{3,2,1,0:T(8,128)(2,1)S(1)}, u32[]{:S(2)}) copy-start(bf16[2,2,48,3072]{3,2,1,0:T(8,128)(2,1)S(1)} %pad_maximum_fusion.1.refs_10_) | copy-start | bytes 3538948
  26.2 16.3 %collective-permute-start.6 = (bf16[2,2,48,3072]{3,2,1,0:T(8,128)(2,1)S(1)}, bf16[2,2,48,3072]{3,2,1,0:T(8,128)(2,1)S(1)}, u32[]{:S(2)}, u32[]{:S(2)}) collective-permute-start(bf16[2,2,48,3072]{3,2,1,0:T(8,128)(2,1)S(1)} %pad_maximum_fusion.1.refs_10_), channel_id=1, source_target_pairs={{0,16},{1,17},{2,18},{3,19},{4,20},{5,21},{6,22},{7,23},{8,56},{9,... | collective-permute-start | bytes 3538952 | tf_op jit(solution)/shard_map/ppermute | solution.py:51
  29.0 16.4 %collective-permute-start.4 = (bf16[1,4,48,3072]{3,2,1,0:T(8,128)(2,1)S(1)}, bf16[1,4,48,3072]{3,2,1,0:T(8,128)(2,1)}, u32[]{:S(2)}, u32[]{:S(2)}) collective-permute-start(bf16[1,4,48,3072]{3,2,1,0:T(8,128)(2,1)S(1)} %pad_maximum_fusion.refs_9_), channel_id=1, source_target_pairs={{0,64},{1,65},{2,66},{3,67},{4,68},{5,69},{6,70},{7,71},{8,76},{9,... | collective-permute-start | bytes 3538952 | tf_op jit(solution)/shard_map/ppermute | solution.py:51
  45.4 28.5 %copy-start.12 = (s32[768]{0:T(1024)S(1)}, s32[768]{0:T(1024)}, u32[]{:S(2)}) copy-start(s32[768]{0:T(1024)} %param.6) | copy-start | bytes 9220
  62.6 22.1 %all-to-all-start = ((f32[64,3,384]{2,1,0:T(4,128)}), f32[64,3,384]{2,1,0:T(4,128)S(1)}, u32[]{:S(2)}, u32[]{:S(2)}) async-start(f32[64,3,384]{2,1,0:T(4,128)} %get-tuple-element.26), calls=%async_computation | async-start | bytes 786432 | tf_op jit(solution)/shard_map/all_to_all | solution.py:470
  74.1 10.7 %copy-start = (f32[384,394]{1,0:T(8,128)S(1)}, f32[384,394]{1,0:T(8,128)}, u32[]{:S(2)}) copy-start(f32[384,394]{1,0:T(8,128)} %get-tuple-element.22.refs_4_) | copy-start | bytes 1815556
  74.1 10.7 %copy-start.1 = (f32[384,394]{1,0:T(8,128)S(1)}, f32[384,394]{1,0:T(8,128)}, u32[]{:S(2)}) copy-start(f32[384,394]{1,0:T(8,128)} %get-tuple-element.23.refs_5_) | copy-start | bytes 1815556
  74.1 10.6 %copy-start.2 = (f32[384,394]{1,0:T(8,128)S(1)}, f32[384,394]{1,0:T(8,128)}, u32[]{:S(2)}) copy-start(f32[384,394]{1,0:T(8,128)} %get-tuple-element.24.refs_6_) | copy-start | bytes 1815556
  84.7 12.9 %slice-start = ((s8[4915200]{0:T(1024)(128)(4,1)}), s8[4194304]{0:T(1024)(128)(4,1)S(1)}, s32[]{:S(2)}) async-start(s8[4915200]{0:T(1024)(128)(4,1)} %bitcast.12), calls=%async_computation.2 | async-start | bytes 8388608
  84.7 12.9 %slice-start.1 = ((s8[4915200]{0:T(1024)(128)(4,1)}), s8[720896]{0:T(1024)(128)(4,1)S(1)}, s32[]{:S(2)}) async-start(s8[4915200]{0:T(1024)(128)(4,1)} %bitcast.12), calls=%async_computation.3 | async-start | bytes 1441792
  95.7 13.0 %collective-permute-start.11 = (bf16[4,2,2,48,256]{4,3,2,1,0:T(8,128)(2,1)S(1)}, bf16[4,2,2,48,256]{4,3,2,1,0:T(8,128)(2,1)S(1)}, u32[]{:S(2)}, u32[]{:S(2)}) collective-permute-start(bf16[4,2,2,48,256]{4,3,2,1,0:T(8,128)(2,1)S(1)} %get-tuple-element.36), channel_id=1, source_target_pairs={{0,16},{1,17},{2,18},{3,19},{4,20},{5,21},{6,22},{7,23},{8,56},{9,... | collective-permute-start | bytes 1179656 | tf_op jit(solution)/shard_map/ppermute | solution.py:51
  96.4 14.7 %collective-permute-start.7 = (bf16[4,4,2,48,256]{4,3,2,1,0:T(8,128)(2,1)S(1)}, bf16[4,4,2,48,256]{4,3,2,1,0:T(8,128)(2,1)S(1)}, u32[]{:S(2)}, u32[]{:S(2)}) collective-permute-start(bf16[4,4,2,48,256]{4,3,2,1,0:T(8,128)(2,1)S(1)} %get-tuple-element.31.refs_8_), channel_id=1, source_target_pairs={{0,1},{1,0},{2,3},{3,2},{4,5},{5,4},{6,7},{7,6},{8,11},{9,10},{10,... | collective-permute-start | bytes 2359304 | tf_op jit(solution)/shard_map/ppermute | solution.py:51
  96.9 13.5 %collective-permute-start.15 = (bf16[2,4,2,48,256]{4,3,2,1,0:T(8,128)(2,1)S(1)}, bf16[2,4,2,48,256]{4,3,2,1,0:T(8,128)(2,1)S(1)}, u32[]{:S(2)}, u32[]{:S(2)}) collective-permute-start(bf16[2,4,2,48,256]{4,3,2,1,0:T(8,128)(2,1)S(1)} %get-tuple-element.40), channel_id=1, source_target_pairs={{0,64},{1,65},{2,66},{3,67},{4,68},{5,69},{6,70},{7,71},{8,76},{9,... | collective-permute-start | bytes 1179656 | tf_op jit(solution)/shard_map/ppermute | solution.py:51
  105.9 7.9 %collective-permute-start.10 = (bf16[4,2,2,48,256]{4,3,2,1,0:T(8,128)(2,1)S(1)}, bf16[4,2,2,48,256]{4,3,2,1,0:T(8,128)(2,1)S(1)}, u32[]{:S(2)}, u32[]{:S(2)}) collective-permute-start(bf16[4,2,2,48,256]{4,3,2,1,0:T(8,128)(2,1)S(1)} %get-tuple-element.34), channel_id=1, source_target_pairs={{0,16},{1,17},{2,18},{3,19},{4,20},{5,21},{6,22},{7,23},{8,56},{9,... | collective-permute-start | bytes 1179656 | tf_op jit(solution)/shard_map/ppermute | solution.py:51
  107.4 10.2 %collective-permute-start.14 = (bf16[2,4,2,48,256]{4,3,2,1,0:T(8,128)(2,1)S(1)}, bf16[2,4,2,48,256]{4,3,2,1,0:T(8,128)(2,1)S(1)}, u32[]{:S(2)}, u32[]{:S(2)}) collective-permute-start(bf16[2,4,2,48,256]{4,3,2,1,0:T(8,128)(2,1)S(1)} %get-tuple-element.38), channel_id=1, source_target_pairs={{0,64},{1,65},{2,66},{3,67},{4,68},{5,69},{6,70},{7,71},{8,76},{9,... | collective-permute-start | bytes 1179656 | tf_op jit(solution)/shard_map/ppermute | solution.py:51
  108.8 7.9 %collective-permute-start.12 = (bf16[4,2,2,48,256]{4,3,2,1,0:T(8,128)(2,1)S(1)}, bf16[4,2,2,48,256]{4,3,2,1,0:T(8,128)(2,1)S(1)}, u32[]{:S(2)}, u32[]{:S(2)}) collective-permute-start(bf16[4,2,2,48,256]{4,3,2,1,0:T(8,128)(2,1)S(1)} %add_convert_fusion.1), channel_id=1, source_target_pairs={{0,1},{1,0},{2,3},{3,2},{4,5},{5,4},{6,7},{7,6},{8,11},{9,10},{10,... | collective-permute-start | bytes 1179656 | tf_op jit(solution)/shard_map/ppermute | solution.py:51
  110.5 10.4 %collective-permute-start.16 = (bf16[2,4,2,48,256]{4,3,2,1,0:T(8,128)(2,1)S(1)}, bf16[2,4,2,48,256]{4,3,2,1,0:T(8,128)(2,1)S(1)}, u32[]{:S(2)}, u32[]{:S(2)}) collective-permute-start(bf16[2,4,2,48,256]{4,3,2,1,0:T(8,128)(2,1)S(1)} %add_convert_fusion), channel_id=1, source_target_pairs={{0,1},{1,0},{2,3},{3,2},{4,5},{5,4},{6,7},{7,6},{8,11},{9,10},{10,... | collective-permute-start | bytes 1179656 | tf_op jit(solution)/shard_map/ppermute | solution.py:51
  111.3 11.2 %collective-permute-start.8 = (bf16[2,4,2,48,256]{4,3,2,1,0:T(8,128)(2,1)S(1)}, bf16[2,4,2,48,256]{4,3,2,1,0:T(8,128)(2,1)S(1)}, u32[]{:S(2)}, u32[]{:S(2)}) collective-permute-start(bf16[2,4,2,48,256]{4,3,2,1,0:T(8,128)(2,1)S(1)} %slice.86), channel_id=1, source_target_pairs={{0,64},{1,65},{2,66},{3,67},{4,68},{5,69},{6,70},{7,71},{8,76},{9,... | collective-permute-start | bytes 1179656 | tf_op jit(solution)/shard_map/ppermute | solution.py:51
  116.8 5.8 %collective-permute-start.13 = (bf16[2,2,2,48,256]{4,3,2,1,0:T(8,128)(2,1)S(1)}, bf16[2,2,2,48,256]{4,3,2,1,0:T(8,128)(2,1)S(1)}, u32[]{:S(2)}, u32[]{:S(2)}) collective-permute-start(bf16[2,2,2,48,256]{4,3,2,1,0:T(8,128)(2,1)S(1)} %slice.88), channel_id=1, source_target_pairs={{0,64},{1,65},{2,66},{3,67},{4,68},{5,69},{6,70},{7,71},{8,76},{9,... | collective-permute-start | bytes 589832 | tf_op jit(solution)/shard_map/ppermute | solution.py:51
  121.0 5.7 %collective-permute-start.17 = (bf16[2,2,2,48,256]{4,3,2,1,0:T(8,128)(2,1)S(1)}, bf16[2,2,2,48,256]{4,3,2,1,0:T(8,128)(2,1)S(1)}, u32[]{:S(2)}, u32[]{:S(2)}) collective-permute-start(bf16[2,2,2,48,256]{4,3,2,1,0:T(8,128)(2,1)S(1)} %slice.87), channel_id=1, source_target_pairs={{0,16},{1,17},{2,18},{3,19},{4,20},{5,21},{6,22},{7,23},{8,56},{9,... | collective-permute-start | bytes 589832 | tf_op jit(solution)/shard_map/ppermute | solution.py:51
  122.7 6.1 %collective-permute-start.9 = (bf16[2,2,2,48,256]{4,3,2,1,0:T(8,128)(2,1)S(1)}, bf16[2,2,2,48,256]{4,3,2,1,0:T(8,128)(2,1)S(1)}, u32[]{:S(2)}, u32[]{:S(2)}) collective-permute-start(bf16[2,2,2,48,256]{4,3,2,1,0:T(8,128)(2,1)S(1)} %slice.89), channel_id=1, source_target_pairs={{0,16},{1,17},{2,18},{3,19},{4,20},{5,21},{6,22},{7,23},{8,56},{9,... | collective-permute-start | bytes 589832 | tf_op jit(solution)/shard_map/ppermute | solution.py:51
  129.8 18.0 %all-to-all-start.1 = ((bf16[8,48,768]{2,1,0:T(8,128)(2,1)}), bf16[8,48,768]{2,1,0:T(8,128)(2,1)S(1)}, u32[]{:S(2)}, u32[]{:S(2)}) async-start(bf16[8,48,768]{2,1,0:T(8,128)(2,1)} %pad_maximum_fusion.4), calls=%async_computation.1 | async-start | bytes 1179648 | tf_op jit(solution)/shard_map/all_to_all | solution.py:508
  135.5 1.2 collective-permute-start.18
  (4 other events, 3.8 us)

commit v5 on v4

--- a/solution.py
+++ b/solution.py
@@ -16,7 +16,7 @@
 ROWS = 48
 MIB = 1 << 20
 LIMIT = 60 * MIB
-BACK_LIMITS = (46 * MIB, 40 * MIB)
+BACK_LIMITS = (44 * MIB, 40 * MIB)
 NT = (((1,), (1,)), ((), ()))
 
 

time: 149 us -> 152 us (1.020)
  local copies, waits for them, and re-layouts: 3.99 us -> 7.71 us
    unnamed x30 -> x36, local copies, waits for them, and re-layouts: 2.59 us -> 6.31 us
  transfers between devices with their start and end apart: 21 -> 21, of which waited for: 12 -> 12; matrix products, arithmetic and copies ran while one was open for 4% -> 4% of each run, Pallas kernels for 26% -> 25%
where the time goes in v5:
time: 152 us; the launch traced here: 151 us
  Pallas kernels  65.3 us (43%)
  waiting for transfers between devices  36.4 us (24%)
  starting transfers between devices  35.4 us (23%)
  local copies, waits for them, and re-layouts  7.71 us (5%)
  other arithmetic  5.7 us (4%)
    pallas_call x4, Pallas kernels, probe_products(): pl.pallas_call(kernel, grid_spec=pltpu.PrefetchScalarGridSpec(num_scalar_...  29.6 us
    ppermute x19, waiting for transfers between devices, swap(): return lax.ppermute(a, AXES, pairs(axis, kind))  22.8 us
    ppermute x19, starting transfers between devices, swap(): return lax.ppermute(a, AXES, pairs(axis, kind))  18.5 us
    pallas_call x2, Pallas kernels, back(): pl.pallas_call(kernel, grid_spec=pltpu.PrefetchScalarGridSpec(num_scalar_...  18.4 us
    pallas_call x1, Pallas kernels, hidden_products(): pl.pallas_call(kernel, grid_spec=pltpu.PrefetchScalarGridSpec(num_scalar_...  17.2 us
    all_to_all x1, starting transfers between devices, body(): lax.all_to_all(stats, AXES, 0, 0, axis_index_groups=groups_of_core(), til...  11.3 us
    all_to_all x1, waiting for transfers between devices, body(): lax.all_to_all(total, AXES, 0, 0, axis_index_groups=groups_of_eight(), ti...  10.5 us
    unnamed x36, local copies, waits for them, and re-layouts  6.31 us
  transfers between devices with their start and end apart: 21, of which 12 were waited for; matrix products, arithmetic and copies ran while one was open for 4% of the time, Pallas kernels for 25%

profile of v5, /device:TPU:0, one launch (start us, length us, event | category | flops | bytes accessed | tf_op | source)
XLA Modules:
  0.0 151.5 jit_solution(2985551471100869666)
XLA Ops:
  1.2 3.1 %collective-permute-start.2 = (bf16[1,1,48,6144]{3,2,1,0:T(8,128)(2,1)}, bf16[1,1,48,6144]{3,2,1,0:T(8,128)(2,1)}, u32[]{:S(2)}, u32[]{:S(2)}) collective-permute-start(bf16[1,1,48,6144]{3,2,1,0:T(8,128)(2,1)} %bitcast.52), channel_id=1, source_target_pairs={{0,48},{1,49},{2,50},{3,51},{4,52},{5,53},{6,54},{7,55},{8,24},{9,... | collective-permute-start | bytes 1769480 | tf_op jit(solution)/shard_map/ppermute | solution.py:51
  4.3 7.4 %shard_map.68.refs_1_.refs_8_ = f32[384,394]{1,0:T(8,128)} custom-call(s32[1]{0:T(128)} %bitcast.me_ref, bf16[16,48,6144]{2,1,0:T(8,128)(2,1)} %bitcast.14, bf16[16,48,6144]{2,1,0:T(8,128)(2,1)} %bitcast.15, bf16[16,48,6144]{2,1,0:T(8,128)(2,1)} %bitcast.16, bf16[16,48,6144]{2,1,0:T(8,128)(2,1)} %bitcast.17, bf16[16,48,6144]{2,1,0:T(8,128)(2,1)} %bitcast.18, ...), custom_call_target="tpu_custom_call" | custom-call | flops 1048576 | bytes 1048576 | tf_op jit(solution)/shard_map/pallas_call | solution.py:122
  12.6 1.1 fusion.4
  13.8 2.1 %collective-permute-start.5 = (bf16[1,2,48,3072]{3,2,1,0:T(8,128)(2,1)S(1)}, bf16[1,2,48,3072]{3,2,1,0:T(8,128)(2,1)S(1)}, u32[]{:S(2)}, u32[]{:S(2)}) collective-permute-start(bf16[1,2,48,3072]{3,2,1,0:T(8,128)(2,1)S(1)} %pad_maximum_fusion.3.refs_10_), channel_id=1, source_target_pairs={{0,64},{1,65},{2,66},{3,67},{4,68},{5,69},{6,70},{7,71},{8,76},{9,... | collective-permute-start | bytes 1769480 | tf_op jit(solution)/shard_map/ppermute | solution.py:51
  16.8 7.3 %shard_map.70.refs_1_.refs_10_ = f32[384,394]{1,0:T(8,128)} custom-call(s32[1]{0:T(128)} %bitcast.me_ref, bf16[16,48,6144]{2,1,0:T(8,128)(2,1)} %bitcast.29, bf16[16,48,6144]{2,1,0:T(8,128)(2,1)} %bitcast.23, bf16[16,48,6144]{2,1,0:T(8,128)(2,1)} %bitcast.24, bf16[16,48,6144]{2,1,0:T(8,128)(2,1)} %bitcast.25, bf16[16,48,6144]{2,1,0:T(8,128)(2,1)} %bitcast.26, ...), custom_call_target="tpu_custom_call" | custom-call | flops 1048576 | bytes 1048576 | tf_op jit(solution)/shard_map/pallas_call | solution.py:122
  24.9 1.2 pad_maximum_fusion.1.refs_10_
  26.1 1.4 collective-permute-start.6
  27.6 1.3 pad_maximum_fusion.refs_9_
  30.0 7.3 %shard_map.73.refs_1_.refs_9_ = f32[384,394]{1,0:T(8,128)} custom-call(s32[1]{0:T(128)} %bitcast.me_ref, bf16[16,48,6144]{2,1,0:T(8,128)(2,1)} %bitcast.30, bf16[16,48,6144]{2,1,0:T(8,128)(2,1)} %bitcast.31, bf16[16,48,6144]{2,1,0:T(8,128)(2,1)} %bitcast.32, bf16[16,48,6144]{2,1,0:T(8,128)(2,1)} %bitcast.33, bf16[16,48,6144]{2,1,0:T(8,128)(2,1)} %bitcast.34, ...), custom_call_target="tpu_custom_call" | custom-call | flops 1048576 | bytes 1048576 | tf_op jit(solution)/shard_map/pallas_call | solution.py:122
  37.3 5.1 %collective-permute-done.6.refs_0_ = bf16[2,2,48,3072]{3,2,1,0:T(8,128)(2,1)S(1)} collective-permute-done((bf16[2,2,48,3072]{3,2,1,0:T(8,128)(2,1)S(1)}, bf16[2,2,48,3072]{3,2,1,0:T(8,128)(2,1)S(1)}, u32[]{:S(2)}, u32[]{:S(2)}) %collective-permute-start.6) | collective-permute-done | bytes 1179680 | tf_op jit(solution)/shard_map/ppermute | solution.py:51
  42.4 1.0 copy-done.8
  43.5 1.9 %collective-permute-done.4.refs_0_ = bf16[1,4,48,3072]{3,2,1,0:T(8,128)(2,1)} collective-permute-done((bf16[1,4,48,3072]{3,2,1,0:T(8,128)(2,1)S(1)}, bf16[1,4,48,3072]{3,2,1,0:T(8,128)(2,1)}, u32[]{:S(2)}, u32[]{:S(2)}) %collective-permute-start.4) | collective-permute-done | bytes 1179680 | tf_op jit(solution)/shard_map/ppermute | solution.py:51
  45.4 17.2 %shard_map.76 = (f32[384,394]{1,0:T(8,128)}, f32[384,394]{1,0:T(8,128)}, f32[384,394]{1,0:T(8,128)}, f32[384,394]{1,0:T(8,128)}, f32[64,3,384]{2,1,0:T(4,128)}) custom-call(s32[1]{0:T(128)} %bitcast.me_ref, bf16[192,3072]{1,0:T(8,128)(2,1)} %bitcast.47, bf16[192,3072]{1,0:T(8,128)(2,1)} %bitcast.4.refs_1_, bf16[192,3072]{1,0:T(8,128)(2,1)} %bitcast.46, ...), custom_call_target="tpu_custom_call" | custom-call | flops 1048576 | bytes 1048576 | tf_op jit(solution)/shard_map/pallas_call | solution.py:229
  62.6 11.3 %all-to-all-start = ((f32[64,3,384]{2,1,0:T(4,128)}), f32[64,3,384]{2,1,0:T(4,128)S(1)}, u32[]{:S(2)}, u32[]{:S(2)}) async-start(f32[64,3,384]{2,1,0:T(4,128)} %get-tuple-element.26), calls=%async_computation | async-start | bytes 786432 | tf_op jit(solution)/shard_map/all_to_all | solution.py:470
  74.1 7.5 %shard_map.77.refs_11_ = f32[384,394]{1,0:T(8,128)} custom-call(s32[1]{0:T(128)} %bitcast.me_ref, bf16[16,48,6144]{2,1,0:T(8,128)(2,1)} %bitcast.38, bf16[16,48,6144]{2,1,0:T(8,128)(2,1)} %bitcast.39, bf16[16,48,6144]{2,1,0:T(8,128)(2,1)} %bitcast.40, bf16[16,48,6144]{2,1,0:T(8,128)(2,1)} %bitcast.41, bf16[16,48,6144]{2,1,0:T(8,128)(2,1)} %bitcast.42, ...), custom_call_target="tpu_custom_call" | custom-call | flops 1048576 | bytes 1048576 | tf_op jit(solution)/shard_map/pallas_call | solution.py:122
  81.6 3.1 %all-to-all-done.refs_12_ = f32[64,3,384]{2,1,0:T(4,128)S(1)} async-done(((f32[64,3,384]{2,1,0:T(4,128)}), f32[64,3,384]{2,1,0:T(4,128)S(1)}, u32[]{:S(2)}, u32[]{:S(2)}) %all-to-all-start) | async-done | bytes 294944 | tf_op jit(solution)/shard_map/all_to_all | solution.py:470
  84.7 1.3 copy-done.3
  86.0 1.3 copy-done.4
  87.3 1.1 copy-done.5
  88.5 10.2 %shard_map.78 = (bf16[4,4,2,48,256]{4,3,2,1,0:T(8,128)(2,1)S(1)}, bf16[4,2,2,48,256]{4,3,2,1,0:T(8,128)(2,1)S(1)}, f32[4,2,2,48,256]{4,3,2,1,0:T(8,128)S(1)}, bf...) custom-call(s32[1]{0:T(128)} %bitcast.me_ref, ...), custom_call_target="tpu_custom_call" | custom-call | flops 1048576 | bytes 1048576 | tf_op jit(solution)/shard_map/pallas_call | solution.py:427
  100.6 8.3 %shard_map.79 = (f32[4,4,2,48,256]{4,3,2,1,0:T(8,128)S(1)}, bf16[4,2,2,48,256]{4,3,2,1,0:T(8,128)(2,1)S(1)}, f32[4,2,2,48,256]{4,3,2,1,0:T(8,128)S(1)}, bf16[2,4...) custom-call(s32[1]{0:T(128)} %bitcast.me_ref, bf16[384,394]{1,0:T(8,128)(2,1)S(1)} %get-tuple-element.27.refs_0_, ...), custom_call_target="tpu_custom_call" | custom-call | flops 1048576 | bytes 1048576 | tf_op jit(solution)/shard_map/pallas_call | solution.py:427
  108.9 1.5 collective-permute-start.10
  110.4 1.2 collective-permute-start.14
  111.7 1.6 %collective-permute-start.12 = (bf16[4,2,2,48,256]{4,3,2,1,0:T(8,128)(2,1)S(1)}, bf16[4,2,2,48,256]{4,3,2,1,0:T(8,128)(2,1)S(1)}, u32[]{:S(2)}, u32[]{:S(2)}) collective-permute-start(bf16[4,2,2,48,256]{4,3,2,1,0:T(8,128)(2,1)S(1)} %add_convert_fusion.1), channel_id=1, source_target_pairs={{0,1},{1,0},{2,3},{3,2},{4,5},{5,4},{6,7},{7,6},{8,11},{9,10},{10,... | collective-permute-start | bytes 1179656 | tf_op jit(solution)/shard_map/ppermute | solution.py:51
  115.2 1.6 %collective-permute-done.10 = bf16[4,2,2,48,256]{4,3,2,1,0:T(8,128)(2,1)S(1)} collective-permute-done((bf16[4,2,2,48,256]{4,3,2,1,0:T(8,128)(2,1)S(1)}, bf16[4,2,2,48,256]{4,3,2,1,0:T(8,128)(2,1)S(1)}, u32[]{:S(2)}, u32[]{:S(2)}) %collective-permute-start.10) | collective-permute-done | bytes 393248 | tf_op jit(solution)/shard_map/ppermute | solution.py:51
  116.8 2.8 %collective-permute-done.12 = bf16[4,2,2,48,256]{4,3,2,1,0:T(8,128)(2,1)S(1)} collective-permute-done((bf16[4,2,2,48,256]{4,3,2,1,0:T(8,128)(2,1)S(1)}, bf16[4,2,2,48,256]{4,3,2,1,0:T(8,128)(2,1)S(1)}, u32[]{:S(2)}, u32[]{:S(2)}) %collective-permute-start.12) | collective-permute-done | bytes 393248 | tf_op jit(solution)/shard_map/ppermute | solution.py:51
  120.6 3.2 %collective-permute-done.16 = bf16[2,4,2,48,256]{4,3,2,1,0:T(8,128)(2,1)S(1)} collective-permute-done((bf16[2,4,2,48,256]{4,3,2,1,0:T(8,128)(2,1)S(1)}, bf16[2,4,2,48,256]{4,3,2,1,0:T(8,128)(2,1)S(1)}, u32[]{:S(2)}, u32[]{:S(2)}) %collective-permute-start.16) | collective-permute-done | bytes 393248 | tf_op jit(solution)/shard_map/ppermute | solution.py:51
  126.4 3.3 %collective-permute-done.17 = bf16[2,2,2,48,256]{4,3,2,1,0:T(8,128)(2,1)S(1)} collective-permute-done((bf16[2,2,2,48,256]{4,3,2,1,0:T(8,128)(2,1)S(1)}, bf16[2,2,2,48,256]{4,3,2,1,0:T(8,128)(2,1)S(1)}, u32[]{:S(2)}, u32[]{:S(2)}) %collective-permute-start.17) | collective-permute-done | bytes 196640 | tf_op jit(solution)/shard_map/ppermute | solution.py:51
  129.8 2.1 %collective-permute-done.9 = bf16[2,2,2,48,256]{4,3,2,1,0:T(8,128)(2,1)S(1)} collective-permute-done((bf16[2,2,2,48,256]{4,3,2,1,0:T(8,128)(2,1)S(1)}, bf16[2,2,2,48,256]{4,3,2,1,0:T(8,128)(2,1)S(1)}, u32[]{:S(2)}, u32[]{:S(2)}) %collective-permute-start.9) | collective-permute-done | bytes 196640 | tf_op jit(solution)/shard_map/ppermute | solution.py:51
  132.7 5.7 %all-to-all-start.1 = ((bf16[8,48,768]{2,1,0:T(8,128)(2,1)}), bf16[8,48,768]{2,1,0:T(8,128)(2,1)S(1)}, u32[]{:S(2)}, u32[]{:S(2)}) async-start(bf16[8,48,768]{2,1,0:T(8,128)(2,1)} %pad_maximum_fusion.4), calls=%async_computation.1 | async-start | bytes 1179648 | tf_op jit(solution)/shard_map/all_to_all | solution.py:508
  138.5 1.1 collective-permute-done.18
  140.2 10.5 %all-to-all-done.1 = bf16[8,48,768]{2,1,0:T(8,128)(2,1)S(1)} async-done(((bf16[8,48,768]{2,1,0:T(8,128)(2,1)}), bf16[8,48,768]{2,1,0:T(8,128)(2,1)S(1)}, u32[]{:S(2)}, u32[]{:S(2)}) %all-to-all-start.1) | async-done | bytes 589856 | tf_op jit(solution)/shard_map/all_to_all | solution.py:508
  (83 shorter events, 14.2 us)
Async XLA Ops:
  0.6 29.1 %collective-permute-start = (bf16[394,6144]{1,0:T(8,128)(2,1)}, bf16[394,6144]{1,0:T(8,128)(2,1)}, u32[]{:S(2)}, u32[]{:S(2)}) collective-permute-start(bf16[394,6144]{1,0:T(8,128)(2,1)} %refs_4_.3), channel_id=1, source_target_pairs={{0,8},{1,9},{2,10},{3,11},{4,12},{5,13},{6,14},{7,15},{8,0},{9,1},... | collective-permute-start | bytes 14524424 | tf_op jit(solution)/shard_map/ppermute | solution.py:51
  0.7 44.6 %collective-permute-start.1 = (bf16[394,6144]{1,0:T(8,128)(2,1)}, bf16[394,6144]{1,0:T(8,128)(2,1)}, u32[]{:S(2)}, u32[]{:S(2)}) collective-permute-start(bf16[394,6144]{1,0:T(8,128)(2,1)} %refs_6_.3), channel_id=1, source_target_pairs={{0,8},{1,9},{2,10},{3,11},{4,12},{5,13},{6,14},{7,15},{8,0},{9,1},... | collective-permute-start | bytes 14524424 | tf_op jit(solution)/shard_map/ppermute | solution.py:51
  1.2 11.4 %collective-permute-start.2 = (bf16[1,1,48,6144]{3,2,1,0:T(8,128)(2,1)}, bf16[1,1,48,6144]{3,2,1,0:T(8,128)(2,1)}, u32[]{:S(2)}, u32[]{:S(2)}) collective-permute-start(bf16[1,1,48,6144]{3,2,1,0:T(8,128)(2,1)} %bitcast.52), channel_id=1, source_target_pairs={{0,48},{1,49},{2,50},{3,51},{4,52},{5,53},{6,54},{7,55},{8,24},{9,... | collective-permute-start | bytes 1769480 | tf_op jit(solution)/shard_map/ppermute | solution.py:51
  4.3 7.5 %copy-start.14 = (bf16[48,6144]{1,0:T(8,128)(2,1)S(1)}, bf16[48,6144]{1,0:T(8,128)(2,1)}, u32[]{:S(2)}) copy-start(bf16[48,6144]{1,0:T(8,128)(2,1)} %param.5) | copy-start | bytes 1769476
  11.8 4.1 %copy-start.9 = (bf16[1,1,48,3072]{3,2,1,0:T(8,128)(2,1)}, bf16[1,1,48,3072]{3,2,1,0:T(8,128)(2,1)S(1)}, u32[]{:S(2)}) copy-start(bf16[1,1,48,3072]{3,2,1,0:T(8,128)(2,1)S(1)} %get-tuple-element.43) | copy-start | bytes 884740
  13.7 2.2 %copy-start.10 = (bf16[1,1,48,3072]{3,2,1,0:T(8,128)(2,1)}, bf16[1,1,48,3072]{3,2,1,0:T(8,128)(2,1)S(1)}, u32[]{:S(2)}) copy-start(bf16[1,1,48,3072]{3,2,1,0:T(8,128)(2,1)S(1)} %get-tuple-element.45) | copy-start | bytes 884740
  13.8 2.6 %copy-start.13 = (bf16[1,2,48,3072]{3,2,1,0:T(8,128)(2,1)}, bf16[1,2,48,3072]{3,2,1,0:T(8,128)(2,1)S(1)}, u32[]{:S(2)}) copy-start(bf16[1,2,48,3072]{3,2,1,0:T(8,128)(2,1)S(1)} %pad_maximum_fusion.3.refs_10_) | copy-start | bytes 1769476
  13.8 10.3 %collective-permute-start.5 = (bf16[1,2,48,3072]{3,2,1,0:T(8,128)(2,1)S(1)}, bf16[1,2,48,3072]{3,2,1,0:T(8,128)(2,1)S(1)}, u32[]{:S(2)}, u32[]{:S(2)}) collective-permute-start(bf16[1,2,48,3072]{3,2,1,0:T(8,128)(2,1)S(1)} %pad_maximum_fusion.3.refs_10_), channel_id=1, source_target_pairs={{0,64},{1,65},{2,66},{3,67},{4,68},{5,69},{6,70},{7,71},{8,76},{9,... | collective-permute-start | bytes 1769480 | tf_op jit(solution)/shard_map/ppermute | solution.py:51
  16.0 11.6 %collective-permute-start.3 = (bf16[1,2,48,3072]{3,2,1,0:T(8,128)(2,1)S(1)}, bf16[1,2,48,3072]{3,2,1,0:T(8,128)(2,1)}, u32[]{:S(2)}, u32[]{:S(2)}) collective-permute-start(bf16[1,2,48,3072]{3,2,1,0:T(8,128)(2,1)S(1)} %pad_maximum_fusion.2.refs_9_), channel_id=1, source_target_pairs={{0,16},{1,17},{2,18},{3,19},{4,20},{5,21},{6,22},{7,23},{8,56},{9,... | collective-permute-start | bytes 1769480 | tf_op jit(solution)/shard_map/ppermute | solution.py:51
  26.1 2.8 %copy-start.6 = (bf16[2,2,48,3072]{3,2,1,0:T(8,128)(2,1)}, bf16[2,2,48,3072]{3,2,1,0:T(8,128)(2,1)S(1)}, u32[]{:S(2)}) copy-start(bf16[2,2,48,3072]{3,2,1,0:T(8,128)(2,1)S(1)} %pad_maximum_fusion.1.refs_10_) | copy-start | bytes 3538948
  26.1 16.3 %collective-permute-start.6 = (bf16[2,2,48,3072]{3,2,1,0:T(8,128)(2,1)S(1)}, bf16[2,2,48,3072]{3,2,1,0:T(8,128)(2,1)S(1)}, u32[]{:S(2)}, u32[]{:S(2)}) collective-permute-start(bf16[2,2,48,3072]{3,2,1,0:T(8,128)(2,1)S(1)} %pad_maximum_fusion.1.refs_10_), channel_id=1, source_target_pairs={{0,16},{1,17},{2,18},{3,19},{4,20},{5,21},{6,22},{7,23},{8,56},{9,... | collective-permute-start | bytes 3538952 | tf_op jit(solution)/shard_map/ppermute | solution.py:51
  29.0 16.4 %collective-permute-start.4 = (bf16[1,4,48,3072]{3,2,1,0:T(8,128)(2,1)S(1)}, bf16[1,4,48,3072]{3,2,1,0:T(8,128)(2,1)}, u32[]{:S(2)}, u32[]{:S(2)}) collective-permute-start(bf16[1,4,48,3072]{3,2,1,0:T(8,128)(2,1)S(1)} %pad_maximum_fusion.refs_9_), channel_id=1, source_target_pairs={{0,64},{1,65},{2,66},{3,67},{4,68},{5,69},{6,70},{7,71},{8,76},{9,... | collective-permute-start | bytes 3538952 | tf_op jit(solution)/shard_map/ppermute | solution.py:51
  45.4 28.5 %copy-start.15 = (s32[768]{0:T(1024)S(1)}, s32[768]{0:T(1024)}, u32[]{:S(2)}) copy-start(s32[768]{0:T(1024)} %param.6) | copy-start | bytes 9220
  62.6 22.1 %all-to-all-start = ((f32[64,3,384]{2,1,0:T(4,128)}), f32[64,3,384]{2,1,0:T(4,128)S(1)}, u32[]{:S(2)}, u32[]{:S(2)}) async-start(f32[64,3,384]{2,1,0:T(4,128)} %get-tuple-element.26), calls=%async_computation | async-start | bytes 786432 | tf_op jit(solution)/shard_map/all_to_all | solution.py:470
  74.0 10.7 %copy-start = (f32[384,394]{1,0:T(8,128)S(1)}, f32[384,394]{1,0:T(8,128)}, u32[]{:S(2)}) copy-start(f32[384,394]{1,0:T(8,128)} %shard_map.73.refs_1_.refs_9_) | copy-start | bytes 1815556
  74.0 10.7 %copy-start.1 = (f32[384,394]{1,0:T(8,128)S(1)}, f32[384,394]{1,0:T(8,128)}, u32[]{:S(2)}) copy-start(f32[384,394]{1,0:T(8,128)} %shard_map.68.refs_1_.refs_8_) | copy-start | bytes 1815556
  74.1 10.6 %copy-start.2 = (f32[384,394]{1,0:T(8,128)S(1)}, f32[384,394]{1,0:T(8,128)}, u32[]{:S(2)}) copy-start(f32[384,394]{1,0:T(8,128)} %get-tuple-element.22.refs_4_) | copy-start | bytes 1815556
  84.7 15.9 %slice-start = ((s8[4915200]{0:T(1024)(128)(4,1)}), s8[4194304]{0:T(1024)(128)(4,1)S(1)}, s32[]{:S(2)}) async-start(s8[4915200]{0:T(1024)(128)(4,1)} %bitcast.12), calls=%async_computation.2 | async-start | bytes 8388608
  88.5 12.2 %slice-start.1 = ((s8[4915200]{0:T(1024)(128)(4,1)}), s8[720896]{0:T(1024)(128)(4,1)S(1)}, s32[]{:S(2)}) async-start(s8[4915200]{0:T(1024)(128)(4,1)} %bitcast.12), calls=%async_computation.3 | async-start | bytes 1441792
  98.6 13.0 %collective-permute-start.11 = (bf16[4,2,2,48,256]{4,3,2,1,0:T(8,128)(2,1)S(1)}, bf16[4,2,2,48,256]{4,3,2,1,0:T(8,128)(2,1)S(1)}, u32[]{:S(2)}, u32[]{:S(2)}) collective-permute-start(bf16[4,2,2,48,256]{4,3,2,1,0:T(8,128)(2,1)S(1)} %get-tuple-element.36), channel_id=1, source_target_pairs={{0,16},{1,17},{2,18},{3,19},{4,20},{5,21},{6,22},{7,23},{8,56},{9,... | collective-permute-start | bytes 1179656 | tf_op jit(solution)/shard_map/ppermute | solution.py:51
  99.3 14.7 %collective-permute-start.7 = (bf16[4,4,2,48,256]{4,3,2,1,0:T(8,128)(2,1)S(1)}, bf16[4,4,2,48,256]{4,3,2,1,0:T(8,128)(2,1)S(1)}, u32[]{:S(2)}, u32[]{:S(2)}) collective-permute-start(bf16[4,4,2,48,256]{4,3,2,1,0:T(8,128)(2,1)S(1)} %get-tuple-element.31.refs_8_), channel_id=1, source_target_pairs={{0,1},{1,0},{2,3},{3,2},{4,5},{5,4},{6,7},{7,6},{8,11},{9,10},{10,... | collective-permute-start | bytes 2359304 | tf_op jit(solution)/shard_map/ppermute | solution.py:51
  99.8 13.5 %collective-permute-start.15 = (bf16[2,4,2,48,256]{4,3,2,1,0:T(8,128)(2,1)S(1)}, bf16[2,4,2,48,256]{4,3,2,1,0:T(8,128)(2,1)S(1)}, u32[]{:S(2)}, u32[]{:S(2)}) collective-permute-start(bf16[2,4,2,48,256]{4,3,2,1,0:T(8,128)(2,1)S(1)} %get-tuple-element.40), channel_id=1, source_target_pairs={{0,64},{1,65},{2,66},{3,67},{4,68},{5,69},{6,70},{7,71},{8,76},{9,... | collective-permute-start | bytes 1179656 | tf_op jit(solution)/shard_map/ppermute | solution.py:51
  108.9 7.9 %collective-permute-start.10 = (bf16[4,2,2,48,256]{4,3,2,1,0:T(8,128)(2,1)S(1)}, bf16[4,2,2,48,256]{4,3,2,1,0:T(8,128)(2,1)S(1)}, u32[]{:S(2)}, u32[]{:S(2)}) collective-permute-start(bf16[4,2,2,48,256]{4,3,2,1,0:T(8,128)(2,1)S(1)} %get-tuple-element.34), channel_id=1, source_target_pairs={{0,16},{1,17},{2,18},{3,19},{4,20},{5,21},{6,22},{7,23},{8,56},{9,... | collective-permute-start | bytes 1179656 | tf_op jit(solution)/shard_map/ppermute | solution.py:51
  110.4 10.2 %collective-permute-start.14 = (bf16[2,4,2,48,256]{4,3,2,1,0:T(8,128)(2,1)S(1)}, bf16[2,4,2,48,256]{4,3,2,1,0:T(8,128)(2,1)S(1)}, u32[]{:S(2)}, u32[]{:S(2)}) collective-permute-start(bf16[2,4,2,48,256]{4,3,2,1,0:T(8,128)(2,1)S(1)} %get-tuple-element.38), channel_id=1, source_target_pairs={{0,64},{1,65},{2,66},{3,67},{4,68},{5,69},{6,70},{7,71},{8,76},{9,... | collective-permute-start | bytes 1179656 | tf_op jit(solution)/shard_map/ppermute | solution.py:51
  111.7 7.9 %collective-permute-start.12 = (bf16[4,2,2,48,256]{4,3,2,1,0:T(8,128)(2,1)S(1)}, bf16[4,2,2,48,256]{4,3,2,1,0:T(8,128)(2,1)S(1)}, u32[]{:S(2)}, u32[]{:S(2)}) collective-permute-start(bf16[4,2,2,48,256]{4,3,2,1,0:T(8,128)(2,1)S(1)} %add_convert_fusion.1), channel_id=1, source_target_pairs={{0,1},{1,0},{2,3},{3,2},{4,5},{5,4},{6,7},{7,6},{8,11},{9,10},{10,... | collective-permute-start | bytes 1179656 | tf_op jit(solution)/shard_map/ppermute | solution.py:51
  113.4 10.4 %collective-permute-start.16 = (bf16[2,4,2,48,256]{4,3,2,1,0:T(8,128)(2,1)S(1)}, bf16[2,4,2,48,256]{4,3,2,1,0:T(8,128)(2,1)S(1)}, u32[]{:S(2)}, u32[]{:S(2)}) collective-permute-start(bf16[2,4,2,48,256]{4,3,2,1,0:T(8,128)(2,1)S(1)} %add_convert_fusion), channel_id=1, source_target_pairs={{0,1},{1,0},{2,3},{3,2},{4,5},{5,4},{6,7},{7,6},{8,11},{9,10},{10,... | collective-permute-start | bytes 1179656 | tf_op jit(solution)/shard_map/ppermute | solution.py:51
  114.3 11.2 %collective-permute-start.8 = (bf16[2,4,2,48,256]{4,3,2,1,0:T(8,128)(2,1)S(1)}, bf16[2,4,2,48,256]{4,3,2,1,0:T(8,128)(2,1)S(1)}, u32[]{:S(2)}, u32[]{:S(2)}) collective-permute-start(bf16[2,4,2,48,256]{4,3,2,1,0:T(8,128)(2,1)S(1)} %slice.86), channel_id=1, source_target_pairs={{0,64},{1,65},{2,66},{3,67},{4,68},{5,69},{6,70},{7,71},{8,76},{9,... | collective-permute-start | bytes 1179656 | tf_op jit(solution)/shard_map/ppermute | solution.py:51
  119.8 5.8 %collective-permute-start.13 = (bf16[2,2,2,48,256]{4,3,2,1,0:T(8,128)(2,1)S(1)}, bf16[2,2,2,48,256]{4,3,2,1,0:T(8,128)(2,1)S(1)}, u32[]{:S(2)}, u32[]{:S(2)}) collective-permute-start(bf16[2,2,2,48,256]{4,3,2,1,0:T(8,128)(2,1)S(1)} %slice.88), channel_id=1, source_target_pairs={{0,64},{1,65},{2,66},{3,67},{4,68},{5,69},{6,70},{7,71},{8,76},{9,... | collective-permute-start | bytes 589832 | tf_op jit(solution)/shard_map/ppermute | solution.py:51
  124.0 5.7 %collective-permute-start.17 = (bf16[2,2,2,48,256]{4,3,2,1,0:T(8,128)(2,1)S(1)}, bf16[2,2,2,48,256]{4,3,2,1,0:T(8,128)(2,1)S(1)}, u32[]{:S(2)}, u32[]{:S(2)}) collective-permute-start(bf16[2,2,2,48,256]{4,3,2,1,0:T(8,128)(2,1)S(1)} %slice.87), channel_id=1, source_target_pairs={{0,16},{1,17},{2,18},{3,19},{4,20},{5,21},{6,22},{7,23},{8,56},{9,... | collective-permute-start | bytes 589832 | tf_op jit(solution)/shard_map/ppermute | solution.py:51
  125.7 6.1 %collective-permute-start.9 = (bf16[2,2,2,48,256]{4,3,2,1,0:T(8,128)(2,1)S(1)}, bf16[2,2,2,48,256]{4,3,2,1,0:T(8,128)(2,1)S(1)}, u32[]{:S(2)}, u32[]{:S(2)}) collective-permute-start(bf16[2,2,2,48,256]{4,3,2,1,0:T(8,128)(2,1)S(1)} %slice.89), channel_id=1, source_target_pairs={{0,16},{1,17},{2,18},{3,19},{4,20},{5,21},{6,22},{7,23},{8,56},{9,... | collective-permute-start | bytes 589832 | tf_op jit(solution)/shard_map/ppermute | solution.py:51
  132.7 18.0 %all-to-all-start.1 = ((bf16[8,48,768]{2,1,0:T(8,128)(2,1)}), bf16[8,48,768]{2,1,0:T(8,128)(2,1)S(1)}, u32[]{:S(2)}, u32[]{:S(2)}) async-start(bf16[8,48,768]{2,1,0:T(8,128)(2,1)} %pad_maximum_fusion.4), calls=%async_computation.1 | async-start | bytes 1179648 | tf_op jit(solution)/shard_map/all_to_all | solution.py:508
  138.4 1.2 collective-permute-start.18
  (7 other events, 7.5 us)
